TPU v7x, 128 devices: a whole 4x4x4 slice. The times are simulated.
128 devices in a mesh: layer: 8 (over y_hi, z), latent: 16 (over y_lo, x, core).
Axes of the slice: x: 4, y: 4 (y_hi: 2, y_lo: 2; y = y_hi * 2 + y_lo), z: 4, core: 2. Of those that a mesh axis runs over, the one named last changes fastest.
Arguments:
- acts: bfloat16 [8, 384, 2304], P('layer'), may hold values from -6 to 6
- decoder: bfloat16 [8, 32768, 2304], P('layer', 'latent'), may hold values from -0.225 to 0.225
- enc_bias: float32 [32768], P('latent'), may hold values from -3 to 3
- dec_bias: float32 [8, 2304], P('layer'), may hold values from -6 to 6
Outputs:
- grad_decoder: bfloat16 [8, 32768, 2304], P('layer', 'latent')
- grad_enc_bias: float32 [32768], P('latent')
- grad_dec_bias: float32 [8, 2304], P('layer')
- total_norm: float32 [32768], P('latent')
All inputs are finite; a program needn't handle non-finite values.
Results may differ from a plain program's by a relative error of at most 0.03.
Values may be sent and summed in bfloat16 or wider, within the bound.
No kernel may reach another device: no remote copies, remote signals or barrier semaphores. Data moves between devices by JAX's collectives and lax.ppermute only.
A program may use at most 128 MiB of HBM per device.

v0:
```python
import jax
import jax.numpy as jnp
from jax import lax
from jax.sharding import PartitionSpec as P

penalty_weight = 3.0
norm_eps = 1e-06


def body(acts, decoder, enc_bias, dec_bias):
    inputs = acts[0]
    weights = decoder[0]
    rows = inputs.shape[0]
    contract_last = (((1,), (1,)), ((), ()))
    contract_first = (((0,), (0,)), ((), ()))
    part = lax.dot_general(inputs, weights, contract_last, preferred_element_type=jnp.float32)
    pre = lax.psum(part.astype(jnp.bfloat16), "layer").astype(jnp.float32) + enc_bias[None, :]
    squares = jnp.einsum("fd,fd->f", weights, weights, preferred_element_type=jnp.float32)
    norms = jnp.sqrt(squares + norm_eps)
    total_norm = lax.psum(norms, "layer")
    active = jnp.maximum(pre, 0.0)
    latents = active * active
    lat_bf = latents.astype(jnp.bfloat16)
    partial_recon = jnp.dot(lat_bf, weights, preferred_element_type=jnp.float32)
    recon = lax.psum(partial_recon.astype(jnp.bfloat16), "latent").astype(jnp.float32)
    errors = ((recon + dec_bias - inputs.astype(jnp.float32)) * (2.0 / rows)).astype(jnp.bfloat16)
    grad_dec_bias = jnp.sum(errors.astype(jnp.float32), axis=0)[None, :]
    back = lax.dot_general(errors, weights, contract_last, preferred_element_type=jnp.float32)
    scale = penalty_weight / rows
    dlat = (
        lax.psum(back.astype(jnp.bfloat16), "layer").astype(jnp.float32)
        + scale * total_norm[None, :]
    )
    dpre = dlat * (2.0 * active)
    grad_enc_bias = jnp.sum(dpre, axis=0)
    dpre_bf = dpre.astype(jnp.bfloat16)
    grad = lax.dot_general(lat_bf, errors, contract_first, preferred_element_type=jnp.float32)
    grad = grad + lax.dot_general(
        dpre_bf, inputs, contract_first, preferred_element_type=jnp.float32
    )
    usage = jnp.sum(latents, axis=0)
    grad = grad + (scale * usage / norms)[:, None] * weights.astype(jnp.float32)
    return (grad.astype(jnp.bfloat16)[None], grad_enc_bias, grad_dec_bias, total_norm)


def solution(mesh):
    placed = (P("layer", None, None), P("layer", "latent", None), P("latent"), P("layer", None))
    return jax.shard_map(
        body,
        mesh=mesh,
        in_specs=placed,
        out_specs=(P("layer", "latent", None), P("latent"), P("layer", None), P("latent")),
        check_vma=False,
    )
```

profile of v0, /device:TPU:0, one launch (start us, length us, event | category | flops | bytes accessed | tf_op | source)
XLA Modules:
  0.0 369.3 jit_solution(7994008566892158541)
XLA Ops:
  7.2 0.0 copy-start.2
  7.2 0.0 all-reduce.4.cloned.1.call-start
  7.2 9.2 %fusion.16 = bf16[384,2048]{1,0:T(8,128)(2,1)} fusion(bf16[1,2048,2304]{2,1,0:T(8,128)(2,1)} %param.5, bf16[1,384,2304]{2,1,0:T(8,128)(2,1)} %param.4), kind=kOutput, calls=%fused_computation.20 | convolution fusion | flops 3624665088 | bytes 12779520 | tf_op jit(solution)/shard_map/dot_general | solution.py:16
  16.4 0.0 all-reduce.4.cloned.1.call-update
  16.5 0.0 copy-start.4
  16.5 0.0 all-reduce.6.cloned.1.call-start
  16.5 93.0 %all-reduce.4.cloned.1.call-done = bf16[384,2048]{1,0:T(8,128)(2,1)} async-done(((bf16[384,2048]{1,0:T(8,128)(2,1)}), bf16[384,2048]{1,0:T(8,128)(2,1)}) %all-reduce.4.cloned.1.call-update) | async-done | bytes 1572880 | tf_op jit(solution)/shard_map/psum | solution.py:17
  109.5 0.0 copy-done.2
  109.5 9.2 %fusion.10 = bf16[384,2304]{1,0:T(8,128)(2,1)} fusion(bf16[1,2048,2304]{2,1,0:T(8,128)(2,1)} %param.5, bf16[384,2048]{1,0:T(8,128)(2,1)} %all-reduce.4.cloned.1.call-done, f32[2048]{0:T(1024)S(1)} %copy-done.2), kind=kOutput, calls=%fused_computation.12 | convolution fusion | flops 3628695552 | bytes 12787712 | tf_op jit(solution)/shard_map/dot_general | solution.py:24
  118.7 0.0 all-reduce.6.cloned.1.call-update
  118.8 0.0 all-reduce.8.cloned.1.call-start
  118.8 0.0 copy-done.4
  118.8 5.6 %fusion = f32[2048]{0:T(1024)S(1)} fusion(bf16[1,2048,2304]{2,1,0:T(8,128)(2,1)} %param.5), kind=kLoop, calls=%fused_computation.2 | loop fusion | flops 14153728 | bytes 9445376 | tf_op jit(solution)/shard_map/fd,fd->f/dot_general | solution.py:18
  124.4 21.7 %psum.31 = f32[2048]{0:T(1024)S(1)} all-reduce(f32[2048]{0:T(1024)S(1)} %add_sqrt_fusion), channel_id=1, replica_groups=mesh['layer'=8,'latent'=16] {'layer'}, use_global_device_ids=true, to_apply=%region_3.0 | all-reduce | flops 2048 | bytes 16384 | tf_op jit(solution)/shard_map/psum | solution.py:20
  146.1 0.0 copy-start.3
  146.1 92.2 %all-reduce.6.cloned.1.call-done = bf16[384,2304]{1,0:T(8,128)(2,1)} async-done(((bf16[384,2304]{1,0:T(8,128)(2,1)}), bf16[384,2304]{1,0:T(8,128)(2,1)}) %all-reduce.6.cloned.1.call-update) | async-done | bytes 1769488 | tf_op jit(solution)/shard_map/psum | solution.py:25
  238.3 2.8 convert_reduce_fusion
  241.1 0.0 copy-start
  241.1 11.1 %fusion.19 = bf16[384,2048]{1,0:T(8,128)(2,1)} fusion(bf16[384,2304]{1,0:T(8,128)(2,1)S(1)} %get-tuple-element.7, bf16[1,2048,2304]{2,1,0:T(8,128)(2,1)} %param.5), kind=kOutput, calls=%fused_computation.21 | convolution fusion | flops 3624665088 | bytes 12779520 | tf_op jit(solution)/shard_map/dot_general | solution.py:28
  252.2 0.0 all-reduce.8.cloned.1.call-update
  252.3 0.0 copy-done.3
  252.3 0.6 broadcast_in_dim.10
  252.9 0.0 copy-done
  252.9 9.1 %fusion.31 = f32[2048,2304]{1,0:T(8,128)} fusion(bf16[384,2304]{1,0:T(8,128)(2,1)S(1)} %get-tuple-element.7, bf16[384,2048]{1,0:T(8,128)(2,1)S(1)} %copy-done, f32[2048]{0:T(1024)S(1)} %copy-done.2), kind=kOutput, calls=%fused_computation.30 | convolution fusion | flops 3627810816 | bytes 22224896 | tf_op jit(solution)/shard_map/dot_general | solution.py:37
  262.0 0.0 copy-start.1
  262.0 82.5 %all-reduce.8.cloned.1.call-done = bf16[384,2048]{1,0:T(8,128)(2,1)} async-done(((bf16[384,2048]{1,0:T(8,128)(2,1)}), bf16[384,2048]{1,0:T(8,128)(2,1)}) %all-reduce.8.cloned.1.call-update) | async-done | bytes 1572880 | tf_op jit(solution)/shard_map/psum | solution.py:31
  344.5 3.0 fusion.22
  347.5 0.0 copy-done.1
  347.6 15.2 %fusion.3 = bf16[1,2048,2304]{2,1,0:T(8,128)(2,1)} fusion(f32[2048,2304]{1,0:T(8,128)} %fusion.31, bf16[1,2048,2304]{2,1,0:T(8,128)(2,1)} %param.5, f32[2048]{0:T(1024)S(1)} %multiply_divide_fusion, bf16[1,384,2304]{2,1,0:T(8,128)(2,1)S(1)} %copy-done.1, bf16[384,2048]{1,0:T(8,128)(2,1)S(1)} %copy-done, bf16[384,2048]{1,0:T(8,128)(2,1)} %all-reduce.8.cloned.1.call-done, ...), kind=kOutput, calls=%fused_computation.5 | convolution fusion | flops 3653763072 | bytes 42688512 | tf_op jit(solution)/shard_map/dot_general | solution.py:38
  (4 shorter events, 0.1 us)
Async XLA Ops:
  7.2 102.3 %copy-start.2 = (f32[2048]{0:T(1024)S(1)}, f32[2048]{0:T(1024)}, u32[]{:S(2)}) copy-start(f32[2048]{0:T(1024)} %param.6) | copy-start | bytes 24580
  7.2 102.3 %all-reduce.4.cloned.1.call-start = ((), (), s32[]{:S(2)}) async-start(), calls=%async_computation | async-start | bytes 3145728 | tf_op jit(solution)/shard_map/psum | solution.py:17
  16.5 102.3 %copy-start.4 = (f32[1,2304]{1,0:T(1,128)S(1)}, f32[1,2304]{1,0:T(1,128)}, u32[]{:S(2)}) copy-start(f32[1,2304]{1,0:T(1,128)} %param.7) | copy-start | bytes 27652
  16.5 221.8 %all-reduce.6.cloned.1.call-start = ((), (), s32[]{:S(2)}) async-start(), calls=%async_computation.1 | async-start | bytes 3538944 | tf_op jit(solution)/shard_map/psum | solution.py:25
  118.8 225.7 %all-reduce.8.cloned.1.call-start = ((), (), s32[]{:S(2)}) async-start(), calls=%async_computation.2 | async-start | bytes 3145728 | tf_op jit(solution)/shard_map/psum | solution.py:31
  146.1 106.1 %copy-start.3 = (f32[2048]{0:T(1024)}, f32[2048]{0:T(1024)S(1)}, u32[]{:S(2)}) copy-start(f32[2048]{0:T(1024)S(1)} %psum.31) | copy-start | bytes 24580
  241.1 11.7 %copy-start = (bf16[384,2048]{1,0:T(8,128)(2,1)S(1)}, bf16[384,2048]{1,0:T(8,128)(2,1)}, u32[]{:S(2)}) copy-start(bf16[384,2048]{1,0:T(8,128)(2,1)} %all-reduce.4.cloned.1.call-done) | copy-start | bytes 4718596
  262.0 85.5 %copy-start.1 = (bf16[1,384,2304]{2,1,0:T(8,128)(2,1)S(1)}, bf16[1,384,2304]{2,1,0:T(8,128)(2,1)}, u32[]{:S(2)}) copy-start(bf16[1,384,2304]{2,1,0:T(8,128)(2,1)} %param.4) | copy-start | bytes 5308420
Sparse Core Ops, SparseCore 0:
  16.6 92.8 all-reduce.3
  118.9 119.3 all-reduce.5
  252.4 92.0 all-reduce.7
where the time goes:
time: 369 us
  waiting for transfers between devices  268 us (73%)
  matrix products  53.9 us (15%)
  blocking collectives  21.7 us (6%)
  between operations  13.8 us (4%)
  other arithmetic  11.5 us (3%)
    psum x1, waiting for transfers between devices, body(): lax.psum(part.astype(jnp.bfloat16), 'layer').astype(jnp.float32)  93 us
    psum x1, waiting for transfers between devices, body(): lax.psum(partial_recon.astype(jnp.bfloat16), 'latent').astype(jnp.float32)  92.2 us
    psum x1, waiting for transfers between devices, body(): lax.psum(back.astype(jnp.bfloat16), 'layer').astype(jnp.float32)  82.5 us
    psum x1, blocking collectives, body(): total_norm = lax.psum(norms, 'layer')  21.7 us
    dot_general x1, matrix products, body(): lax.dot_general(dpre_bf, inputs, contract_first, preferred_element_type=j...  15.2 us
    dot_general x1, matrix products, body(): lax.dot_general(errors, weights, contract_last, preferred_element_type=jn...  11.1 us
    dot_general x1, matrix products, body(): partial_recon = jnp.dot(lat_bf, weights, preferred_element_type=jnp.float32)  9.24 us
    dot_general x1, matrix products, body(): lax.dot_general(inputs, weights, contract_last, preferred_element_type=jn...  9.22 us
  transfers between devices with their start and end apart: 3, of which 3 were waited for; matrix products, arithmetic and copies ran while one was open for 4% of the time, Pallas kernels for 0%

commit v1 on v0

v1 whole, which is shorter than its diff:
```python
import jax
import jax.numpy as jnp
from jax import lax
from jax.experimental import pallas as pl
from jax.experimental.pallas import tpu as pltpu
from jax.sharding import PartitionSpec as P

penalty_weight = 3.0
norm_eps = 1e-06

D = 2304
ROWS = 384
F = 2048
LAYERS = 8
BLOCK = F // LAYERS
HALF = ROWS // 2
GROUP = 8
PIECE = HALF // GROUP
EXTRA = 16
SCALE = penalty_weight / ROWS

f32 = jnp.float32
bf16 = jnp.bfloat16
NT = (((1,), (1,)), ((), ()))
TN = (((0,), (0,)), ((), ()))
VMEM = pl.BlockSpec(memory_space=pltpu.VMEM)
HBM = pl.BlockSpec(memory_space=pltpu.HBM)
SMEM = pl.BlockSpec(memory_space=pltpu.SMEM)
shaped = jax.ShapeDtypeStruct


def call(kernel, operands, in_specs, out_specs, out_shape, scratch, mib, flops, nbytes, name):
    return pl.pallas_call(
        kernel,
        in_specs=in_specs,
        out_specs=out_specs,
        out_shape=out_shape,
        scratch_shapes=scratch,
        compiler_params=pltpu.CompilerParams(vmem_limit_bytes=mib << 20),
        cost_estimate=pl.CostEstimate(flops=flops, bytes_accessed=nbytes, transcendentals=0),
        name=name,
    )(*operands)


MATMUL = 2 * ROWS * F * D


def encode(core, acts, weights):
    parts = 4
    rows = F // parts

    def kernel(core_ref, a_hbm, w_hbm, out, norms, w, a, a_sem, w_sem):
        c = core_ref[0]
        a_copies = [
            pltpu.make_async_copy(
                a_hbm.at[pl.ds(pl.multiple_of(h * HALF, HALF), HALF)],
                a.at[pl.ds(i * HALF, HALF)],
                a_sem.at[i],
            )
            for i, h in enumerate((c, 1 - c))
        ]
        w_copies = [
            pltpu.make_async_copy(
                w_hbm.at[pl.ds(i * rows, rows)], w.at[pl.ds(i * rows, rows)], w_sem.at[i]
            )
            for i in range(parts)
        ]
        for copy in a_copies + w_copies:
            copy.start()
        for copy in a_copies:
            copy.wait()
        for i in range(parts):
            w_copies[i].wait()
            for j in range(i * rows // BLOCK, (i + 1) * rows // BLOCK):
                wb = w[pl.ds(j * BLOCK, BLOCK)]
                out[j, :ROWS] = lax.dot_general(
                    a[...], wb, NT, preferred_element_type=f32
                ).astype(bf16)
                squares = jnp.zeros((BLOCK, 128), f32)
                for k in range(D // 128):
                    x = wb[:, k * 128 : (k + 1) * 128].astype(f32)
                    squares = squares + x * x
                total = lax.dot_general(
                    jnp.ones((8, 128), f32),
                    squares,
                    NT,
                    precision=lax.Precision.HIGHEST,
                    preferred_element_type=f32,
                )
                norm = jnp.sqrt(total + norm_eps)
                norms[j] = norm
                high = norm.astype(bf16)
                low = (norm - high.astype(f32)).astype(bf16)
                out[j, ROWS:] = jnp.concatenate([high, low], axis=0)

    return call(
        kernel,
        (core, acts, weights),
        [SMEM, HBM, HBM],
        [VMEM] * 4,
        [
            shaped((LAYERS, ROWS + EXTRA, BLOCK), bf16),
            shaped((LAYERS, 8, BLOCK), f32),
            shaped((F, D), bf16),
            shaped((ROWS, D), bf16),
        ],
        [pltpu.SemaphoreType.DMA((2,)), pltpu.SemaphoreType.DMA((parts,))],
        46,
        MATMUL,
        F * D * 2,
        "encode",
    )


def activate(terms, bias):
    def kernel(t, b, out):
        pre = t[0, :ROWS].astype(f32)
        extra = t[0, ROWS:].astype(f32)
        for i in range(1, LAYERS):
            pre = pre + t[i, :ROWS].astype(f32)
            extra = extra + t[i, ROWS:].astype(f32)
        active = jnp.maximum(pre + b[...], 0.0).astype(bf16)
        total = extra[:8] + extra[8:]
        high = total.astype(bf16)
        low = (total - high.astype(f32)).astype(bf16)
        both = jnp.concatenate([high, low], axis=0)
        for i in range(LAYERS):
            out[i, :ROWS] = active
            out[i, ROWS:] = both

    return call(
        kernel,
        (terms, bias),
        [VMEM] * 2,
        VMEM,
        shaped((LAYERS, ROWS + EXTRA, BLOCK), bf16),
        [],
        8,
        2 * LAYERS * ROWS * BLOCK,
        2 * LAYERS * ROWS * BLOCK,
        "activate",
    )


def decode(active, weights):
    width = 256

    def kernel(g, w, lat, usage, total, recon, flat):
        for j in range(LAYERS):
            x = g[j, :ROWS].astype(f32)
            x = x * x
            usage[j] = jnp.broadcast_to(jnp.sum(x, axis=0, keepdims=True), (8, BLOCK))
            x = x.astype(bf16)
            lat[j] = x
            flat[:, j * BLOCK : (j + 1) * BLOCK] = x
            extra = g[j, ROWS:].astype(f32)
            total[j] = extra[:8] + extra[8:]
        for k in range(D // width):
            cols = slice(k * width, (k + 1) * width)
            recon[:, cols] = jnp.dot(
                flat[...], w[:, cols], preferred_element_type=f32
            ).astype(bf16)

    return call(
        kernel,
        (active, weights),
        [VMEM] * 2,
        [VMEM] * 4,
        [
            shaped((LAYERS, ROWS, BLOCK), bf16),
            shaped((LAYERS, 8, BLOCK), f32),
            shaped((LAYERS, 8, BLOCK), f32),
            shaped((ROWS, D), bf16),
        ],
        [pltpu.VMEM((ROWS, F), bf16)],
        24,
        MATMUL,
        2 * ROWS * F,
        "decode",
    )


def backward(errors, weights):
    def kernel(e, w, out, bias):
        x = e[...].astype(f32)
        bias[...] = jnp.broadcast_to(jnp.sum(x, axis=0, keepdims=True), (8, D))
        for j in range(LAYERS):
            out[j] = lax.dot_general(
                e[...], w[pl.ds(j * BLOCK, BLOCK)], NT, preferred_element_type=f32
            ).astype(bf16)

    return call(
        kernel,
        (errors, weights),
        [VMEM] * 2,
        [VMEM] * 2,
        [shaped((LAYERS, ROWS, BLOCK), bf16), shaped((8, D), f32)],
        [],
        24,
        MATMUL,
        2 * ROWS * F,
        "backward",
    )


def latent_grad(terms, active, total):
    def kernel(t, a, n, out):
        back = t[0].astype(f32)
        for i in range(1, LAYERS):
            back = back + t[i].astype(f32)
        back = back + SCALE * n[:1]
        dpre = (back * (2.0 * a[:ROWS].astype(f32))).astype(bf16)
        for i in range(LAYERS):
            out[i] = dpre

    return call(
        kernel,
        (terms, active, total),
        [VMEM] * 3,
        VMEM,
        shaped((LAYERS, ROWS, BLOCK), bf16),
        [],
        8,
        2 * LAYERS * ROWS * BLOCK,
        2 * LAYERS * ROWS * BLOCK,
        "latent_grad",
    )


def grad_first(lat, errors, usage, norms, weights):
    width = 768

    def kernel(l, e, u, n, w, out):
        for j in range(LAYERS):
            column = (SCALE * u[j] / n[j]).T[:, :1]
            rows = pl.ds(j * BLOCK, BLOCK)
            for k in range(D // width):
                cols = slice(k * width, (k + 1) * width)
                g = lax.dot_general(l[j], e[:, cols], TN, preferred_element_type=f32)
                out[rows, cols] = (g + column * w[rows, cols].astype(f32)).astype(bf16)

    return call(
        kernel,
        (lat, errors, usage, norms, weights),
        [VMEM] * 5,
        VMEM,
        shaped((F, D), bf16),
        [],
        28,
        MATMUL,
        2 * ROWS * F,
        "grad_first",
    )


def grad_second(dpre, acts, first):
    width = 768

    def kernel(d, a, f, out, bias, buf, sem):
        copies = []
        for j in range(LAYERS):
            bias[j] = jnp.broadcast_to(
                jnp.sum(d[j].astype(f32), axis=0, keepdims=True), (8, BLOCK)
            )
            if j >= 2:
                copies[j - 2].wait()
            rows = pl.ds(j * BLOCK, BLOCK)
            for k in range(D // width):
                cols = slice(k * width, (k + 1) * width)
                g = lax.dot_general(d[j], a[:, cols], TN, preferred_element_type=f32)
                buf[j % 2, :, cols] = (g + f[rows, cols].astype(f32)).astype(bf16)
            copy = pltpu.make_async_copy(buf.at[j % 2], out.at[rows], sem.at[j % 2])
            copy.start()
            copies.append(copy)
        copies[-2].wait()
        copies[-1].wait()

    return call(
        kernel,
        (dpre, acts, first),
        [VMEM] * 3,
        [HBM, VMEM],
        [shaped((F, D), bf16), shaped((LAYERS, 8, BLOCK), f32)],
        [pltpu.VMEM((2, BLOCK, D), bf16), pltpu.SemaphoreType.DMA((2,))],
        24,
        MATMUL,
        F * D * 2,
        "grad_second",
    )


def spread(x):
    return jnp.broadcast_to(x[None], (GROUP,) + x.shape)


def body(acts, decoder, enc_bias, dec_bias):
    inputs = acts[0]
    layer = lax.axis_index("layer")
    latent = lax.axis_index("latent")
    core = lax.rem(latent, 2)
    place = lax.div(latent, 2)
    groups = [[2 * g + c for g in range(GROUP)] for c in range(2)]
    swap = [(i, i ^ 1) for i in range(2 * GROUP)]

    def over_layers(x):
        return lax.all_to_all(x, "layer", 0, 0, tiled=True)

    def over_chips(x):
        return lax.all_to_all(x, "latent", 0, 0, axis_index_groups=groups, tiled=True)

    parts, norms, weights, rows = encode(
        jnp.reshape(core, (1,)).astype(jnp.int32), inputs, decoder[0]
    )
    bias = lax.dynamic_slice(enc_bias, (layer * BLOCK,), (BLOCK,))[None, :]
    mine = activate(over_layers(parts), bias)
    lat, usage, total, recon = decode(over_layers(mine), weights)

    other = lax.ppermute(recon[HALF:], "latent", swap)
    summed = (recon[:HALF].astype(f32) + other.astype(f32)).astype(bf16)
    pieces = over_chips(summed.reshape(GROUP, PIECE, D))
    own = lax.dynamic_slice(rows, (place * PIECE, 0), (PIECE, D))
    full = jnp.sum(pieces.astype(f32), axis=0) + dec_bias
    piece = ((full - own.astype(f32)) * (2.0 / ROWS)).astype(bf16)
    near = over_chips(spread(piece)).reshape(HALF, D)
    far = lax.ppermute(near, "latent", swap)
    errors = jnp.concatenate([near, far], axis=0)

    back, dec_grad = backward(errors, weights)
    my_total = lax.dynamic_index_in_dim(total, layer, 0, keepdims=False)
    dpre = over_layers(latent_grad(over_layers(back), mine[0], my_total))
    first = grad_first(lat, errors, usage, norms, weights)
    grad, enc_grad = grad_second(dpre, rows, first)
    return (
        grad[None],
        enc_grad[:, 0].reshape(F),
        dec_grad[:1],
        total[:, 0].reshape(F),
    )


def solution(mesh):
    placed = (P("layer", None, None), P("layer", "latent", None), P("latent"), P("layer", None))
    return jax.shard_map(
        body,
        mesh=mesh,
        in_specs=placed,
        out_specs=(P("layer", "latent", None), P("latent"), P("layer", None), P("latent")),
        check_vma=False,
    )
```

time: 369 us -> 204 us (0.55)
  waiting for transfers between devices: 268 us -> 63.2 us
  matrix products: 53.9 us -> 0 us
  Pallas kernels: 0 us -> 37.3 us
  local copies, waits for them, and re-layouts: 0.63 us -> 32.6 us
  blocking collectives: 21.7 us -> 44.9 us
  starting transfers between devices: 0.12 us -> 21.7 us
  between operations: 13.8 us -> 0.81 us
  other arithmetic: 11.5 us -> 2.33 us
    psum x3 -> x0, waiting for transfers between devices: 268 us -> none  [the longest x1 93 us: body(): lax.psum(part.astype(jnp.bfloat16), 'layer').astype(jnp.float32)]
    all_to_all x0 -> x4, waiting for transfers between devices: none -> 58.4 us  [the longest x3 44.2 us: over_layers(): return lax.all_to_all(x, 'layer', 0, 0, tiled=True)]
    dot_general x5 -> x0, matrix products: 53.9 us -> none  [the longest x1 15.2 us: body(): lax.dot_general(dpre_bf, inputs, contract_first, preferred_element_type=j...]
    all_to_all x0 -> x2, blocking collectives: none -> 44.9 us  [the longest x1 28.4 us: over_layers(): return lax.all_to_all(x, 'layer', 0, 0, tiled=True)]
    pallas_call x0 -> x7, Pallas kernels: none -> 37.3 us  [call(): pl.pallas_call(kernel, in_specs=in_specs, out_specs=out_specs, out_shape=...]
    unnamed x10 -> x30, local copies, waits for them, and re-layouts: 0.03 us -> 26.8 us
    psum x1 -> x0, blocking collectives: 21.7 us -> none  [body(): total_norm = lax.psum(norms, 'layer')]
    all_to_all x0 -> x4, starting transfers between devices: none -> 21.7 us  [the longest x3 17.1 us: over_layers(): return lax.all_to_all(x, 'layer', 0, 0, tiled=True)]
  transfers between devices with their start and end apart: 3 -> 6, of which waited for: 3 -> 6; matrix products, arithmetic and copies ran while one was open for 4% -> 3% of each run, Pallas kernels for 0% -> 3%
where the time goes in v1:
time: 204 us; the launch traced here: 203 us
  waiting for transfers between devices  63.2 us (31%)
  blocking collectives  44.9 us (22%)
  Pallas kernels  37.3 us (18%)
  local copies, waits for them, and re-layouts  32.6 us (16%)
  starting transfers between devices  21.7 us (11%)
  other arithmetic  2.33 us (1%)
    all_to_all x3, waiting for transfers between devices, over_layers(): return lax.all_to_all(x, 'layer', 0, 0, tiled=True)  44.2 us
    pallas_call x7, Pallas kernels, call(): pl.pallas_call(kernel, in_specs=in_specs, out_specs=out_specs, out_shape=...  37.3 us
    all_to_all x1, blocking collectives, over_layers(): return lax.all_to_all(x, 'layer', 0, 0, tiled=True)  28.4 us
    unnamed x30, local copies, waits for them, and re-layouts  26.8 us
    all_to_all x3, starting transfers between devices, over_layers(): return lax.all_to_all(x, 'layer', 0, 0, tiled=True)  17.1 us
    all_to_all x1, blocking collectives, over_chips(): lax.all_to_all(x, 'latent', 0, 0, axis_index_groups=groups, tiled=True)  16.6 us
    all_to_all x1, waiting for transfers between devices, over_chips(): lax.all_to_all(x, 'latent', 0, 0, axis_index_groups=groups, tiled=True)  14.2 us
    all_to_all x1, starting transfers between devices, over_chips(): lax.all_to_all(x, 'latent', 0, 0, axis_index_groups=groups, tiled=True)  4.6 us
  transfers between devices with their start and end apart: 6, of which 6 were waited for; matrix products, arithmetic and copies ran while one was open for 3% of the time, Pallas kernels for 3%

profile of v1, /device:TPU:0, one launch (start us, length us, event | category | flops | bytes accessed | tf_op | source)
XLA Modules:
  0.0 202.9 jit_solution(7651767539443708679)
XLA Ops:
  0.6 1.5 copy-done.13
  2.1 12.2 %encode.1 = (bf16[8,400,256]{2,1,0:T(8,128)(2,1)}, f32[8,8,256]{2,1,0:T(8,128)S(1)}, bf16[2048,2304]{1,0:T(8,128)(2,1)}, bf16[384,2304]{1,0:T(8,128)(2,1)S(1)}) custom-call(s32[1]{0:T(128)} %bitcast.core_ref, bf16[384,2304]{1,0:T(8,128)(2,1)S(1)} %bitcast.14, bf16[2048,2304]{1,0:T(8,128)(2,1)} %bitcast.19), custom_call_target="tpu_custom_call" | custom-call | flops 3623878656 | bytes 9437184 | tf_op jit(solution)/shard_map/encode/pallas_call | solution.py:33
  14.3 1.2 copy-done.9
  15.6 8.0 %all-to-all-start = ((bf16[8,400,256]{2,1,0:T(8,128)(2,1)}), bf16[8,400,256]{2,1,0:T(8,128)(2,1)S(1)}, u32[]{:S(2)}, u32[]{:S(2)}) async-start(bf16[8,400,256]{2,1,0:T(8,128)(2,1)} %get-tuple-element.16), calls=%async_computation | async-start | bytes 3276800 | tf_op jit(solution)/shard_map/all_to_all | solution.py:306
  23.6 0.8 dynamic_slice.10
  24.4 20.7 %all-to-all-done.t = bf16[8,400,256]{2,1,0:T(8,128)(2,1)S(1)} async-done(((bf16[8,400,256]{2,1,0:T(8,128)(2,1)}), bf16[8,400,256]{2,1,0:T(8,128)(2,1)S(1)}, u32[]{:S(2)}, u32[]{:S(2)}) %all-to-all-start) | async-done | bytes 1638432 | tf_op jit(solution)/shard_map/all_to_all | solution.py:306
  45.1 0.2 activate.1
  45.3 28.4 %all_to_all.30.g = bf16[8,400,256]{2,1,0:T(8,128)(2,1)S(1)} all-to-all(bf16[8,400,256]{2,1,0:T(8,128)(2,1)S(1)} %activate.1), channel_id=1, replica_groups=mesh['layer'=8,'latent'=16] {'layer'}, dimensions={0} | all-to-all | bytes 3276800 | tf_op jit(solution)/shard_map/all_to_all | solution.py:306
  73.7 3.7 %copy-done = bf16[2048,2304]{1,0:T(8,128)(2,1)S(1)} copy-done((bf16[2048,2304]{1,0:T(8,128)(2,1)S(1)}, bf16[2048,2304]{1,0:T(8,128)(2,1)}, u32[]{:S(2)}) %copy-start) | copy-done | bytes 9437208
  77.4 3.8 %decode.1 = (bf16[8,384,256]{2,1,0:T(8,128)(2,1)S(1)}, f32[8,8,256]{2,1,0:T(8,128)S(1)}, f32[8,8,256]{2,1,0:T(8,128)S(1)}, bf16[384,2304]{1,0:T(8,128)(2,1)S(1)}) custom-call(bf16[8,400,256]{2,1,0:T(8,128)(2,1)S(1)} %all_to_all.30.g, bf16[2048,2304]{1,0:T(8,128)(2,1)S(1)} %copy-done), custom_call_target="tpu_custom_call" | custom-call | flops 3623878656 | bytes 1572864 | tf_op jit(solution)/shard_map/decode/pallas_call | solution.py:33
  81.2 0.1 slice.19
  81.3 0.0 copy-start.14
  81.3 0.1 collective-permute-start
  81.4 2.4 %collective-permute-done = bf16[192,2304]{1,0:T(8,128)(2,1)S(1)} collective-permute-done((bf16[192,2304]{1,0:T(8,128)(2,1)S(1)}, bf16[192,2304]{1,0:T(8,128)(2,1)S(1)}, u32[]{:S(2)}, u32[]{:S(2)}) %collective-permute-start) | collective-permute-done | bytes 884768 | tf_op jit(solution)/shard_map/ppermute | solution.py:318
  83.8 1.1 add_convert_fusion
  84.9 4.6 %all-to-all-start.2 = ((bf16[8,24,2304]{2,1,0:T(8,128)(2,1)}), bf16[8,24,2304]{2,1,0:T(8,128)(2,1)S(1)}, u32[]{:S(2)}, u32[]{:S(2)}) async-start(bf16[8,24,2304]{2,1,0:T(8,128)(2,1)} %bitcast.4), calls=%async_computation.2 | async-start | bytes 1769472 | tf_op jit(solution)/shard_map/all_to_all | solution.py:309
  89.6 14.2 %all-to-all-done.2 = bf16[8,24,2304]{2,1,0:T(8,128)(2,1)S(1)} async-done(((bf16[8,24,2304]{2,1,0:T(8,128)(2,1)}), bf16[8,24,2304]{2,1,0:T(8,128)(2,1)S(1)}, u32[]{:S(2)}, u32[]{:S(2)}) %all-to-all-start.2) | async-done | bytes 884768 | tf_op jit(solution)/shard_map/all_to_all | solution.py:309
  103.8 0.1 convert_reduce_fusion
  103.9 0.9 multiply_convert_fusion
  104.9 0.1 broadcast_in_dim.13
  104.9 16.6 %all_to_all.31 = bf16[8,24,2304]{2,1,0:T(8,128)(2,1)S(1)} all-to-all(bf16[8,24,2304]{2,1,0:T(8,128)(2,1)S(1)} %broadcast_in_dim.13), channel_id=1, replica_groups={{0,2,4,6,8,10,12,14},{1,3,5,7,9,11,13,15},{16,18,20,22,24,26,28,30},{17..., dimensions={0} | all-to-all | bytes 1769472 | tf_op jit(solution)/shard_map/all_to_all | solution.py:309
  121.5 0.0 collective-permute-start.1
  121.5 2.4 %collective-permute-done.1 = bf16[192,2304]{1,0:T(8,128)(2,1)S(1)} collective-permute-done((bf16[192,2304]{1,0:T(8,128)(2,1)S(1)}, bf16[192,2304]{1,0:T(8,128)(2,1)S(1)}, u32[]{:S(2)}, u32[]{:S(2)}) %collective-permute-start.1) | collective-permute-done | bytes 884768 | tf_op jit(solution)/shard_map/ppermute | solution.py:325
  123.9 0.1 pad_maximum_fusion.e
  124.0 0.0 copy-start.1
  124.1 3.7 %copy-done.1 = bf16[2048,2304]{1,0:T(8,128)(2,1)S(1)} copy-done((bf16[2048,2304]{1,0:T(8,128)(2,1)S(1)}, bf16[2048,2304]{1,0:T(8,128)(2,1)}, u32[]{:S(2)}) %copy-start.1) | copy-done | bytes 9437208
  127.7 4.0 %backward.1 = (bf16[8,384,256]{2,1,0:T(8,128)(2,1)S(1)}, f32[8,2304]{1,0:T(8,128)S(1)}) custom-call(bf16[384,2304]{1,0:T(8,128)(2,1)S(1)} %pad_maximum_fusion.e, bf16[2048,2304]{1,0:T(8,128)(2,1)S(1)} %copy-done.1), custom_call_target="tpu_custom_call" | custom-call | flops 3623878656 | bytes 1572864 | tf_op jit(solution)/shard_map/backward/pallas_call | solution.py:33
  131.7 1.2 copy-done.5
  132.9 0.6 copy-done.12
  133.5 4.3 %all-to-all-start.4 = ((bf16[8,384,256]{2,1,0:T(8,128)(2,1)}), bf16[8,384,256]{2,1,0:T(8,128)(2,1)}, u32[]{:S(2)}, u32[]{:S(2)}) async-start(bf16[8,384,256]{2,1,0:T(8,128)(2,1)} %copy-done.5), calls=%async_computation.4 | async-start | bytes 3145728 | tf_op jit(solution)/shard_map/all_to_all | solution.py:306
  137.8 0.7 slice_bitcast_fusion.a
  138.5 0.7 dynamic-slice_bitcast_fusion.n
  139.2 20.0 %all-to-all-done.4.t = bf16[8,384,256]{2,1,0:T(8,128)(2,1)} async-done(((bf16[8,384,256]{2,1,0:T(8,128)(2,1)}), bf16[8,384,256]{2,1,0:T(8,128)(2,1)}, u32[]{:S(2)}, u32[]{:S(2)}) %all-to-all-start.4) | async-done | bytes 1572896 | tf_op jit(solution)/shard_map/all_to_all | solution.py:306
  159.2 0.9 copy-done.8
  160.1 2.9 %latent_grad.1 = bf16[8,384,256]{2,1,0:T(8,128)(2,1)} custom-call(bf16[8,384,256]{2,1,0:T(8,128)(2,1)} %all-to-all-done.4.t, bf16[400,256]{1,0:T(8,128)(2,1)S(1)} %copy-done.8, f32[8,256]{1,0:T(8,128)S(1)} %dynamic-slice_bitcast_fusion.n), custom_call_target="tpu_custom_call" | custom-call | flops 1572864 | bytes 1572864 | tf_op jit(solution)/shard_map/latent_grad/pallas_call | solution.py:33
  163.0 4.7 %all-to-all-start.5 = ((bf16[8,384,256]{2,1,0:T(8,128)(2,1)}), bf16[8,384,256]{2,1,0:T(8,128)(2,1)S(1)}, u32[]{:S(2)}, u32[]{:S(2)}) async-start(bf16[8,384,256]{2,1,0:T(8,128)(2,1)} %latent_grad.1), calls=%async_computation.5 | async-start | bytes 3145728 | tf_op jit(solution)/shard_map/all_to_all | solution.py:306
  167.7 1.4 slice.23
  169.2 1.5 slice.22
  170.7 3.7 %copy-done.2 = bf16[2048,2304]{1,0:T(8,128)(2,1)S(1)} copy-done((bf16[2048,2304]{1,0:T(8,128)(2,1)S(1)}, bf16[2048,2304]{1,0:T(8,128)(2,1)}, u32[]{:S(2)}) %copy-start.2) | copy-done | bytes 9437208
  174.3 1.4 copy-done.7
  175.7 5.8 %grad_first.1.f = bf16[2048,2304]{1,0:T(8,128)(2,1)S(1)} custom-call(bf16[8,384,256]{2,1,0:T(8,128)(2,1)S(1)} %copy-done.7, bf16[384,2304]{1,0:T(8,128)(2,1)S(1)} %pad_maximum_fusion.e, f32[8,8,256]{2,1,0:T(8,128)S(1)} %get-tuple-element.23.u, f32[8,8,256]{2,1,0:T(8,128)S(1)} %get-tuple-element.24.n, bf16[2048,2304]{1,0:T(8,128)(2,1)S(1)} %copy-done.2), custom_call_target="tpu_custom_call" | custom-call | flops 3623878656 | bytes 1572864 | tf_op jit(solution)/shard_map/grad_first/pallas_call | solution.py:33
  181.5 0.0 copy-start.3
  181.5 3.7 %copy-done.3 = bf16[2048,2304]{1,0:T(8,128)(2,1)} copy-done((bf16[2048,2304]{1,0:T(8,128)(2,1)}, bf16[2048,2304]{1,0:T(8,128)(2,1)S(1)}, u32[]{:S(2)}) %copy-start.3) | copy-done | bytes 9437208
  185.3 3.4 %all-to-all-done.5.d = bf16[8,384,256]{2,1,0:T(8,128)(2,1)S(1)} async-done(((bf16[8,384,256]{2,1,0:T(8,128)(2,1)}), bf16[8,384,256]{2,1,0:T(8,128)(2,1)S(1)}, u32[]{:S(2)}, u32[]{:S(2)}) %all-to-all-start.5) | async-done | bytes 1572896 | tf_op jit(solution)/shard_map/all_to_all | solution.py:306
  188.7 3.7 %copy-done.4 = bf16[2048,2304]{1,0:T(8,128)(2,1)S(1)} copy-done((bf16[2048,2304]{1,0:T(8,128)(2,1)S(1)}, bf16[2048,2304]{1,0:T(8,128)(2,1)}, u32[]{:S(2)}) %copy-start.4) | copy-done | bytes 9437208
  192.4 1.5 copy-done.10
  193.9 8.4 %grad_second.1 = (bf16[2048,2304]{1,0:T(8,128)(2,1)}, f32[8,8,256]{2,1,0:T(8,128)S(1)}) custom-call(bf16[8,384,256]{2,1,0:T(8,128)(2,1)S(1)} %all-to-all-done.5.d, bf16[384,2304]{1,0:T(8,128)(2,1)S(1)} %copy-done.10, bf16[2048,2304]{1,0:T(8,128)(2,1)S(1)} %copy-done.4), custom_call_target="tpu_custom_call" | custom-call | flops 3623878656 | bytes 9437184 | tf_op jit(solution)/shard_map/grad_second/pallas_call | solution.py:33
  202.3 0.6 slice.21
  (16 shorter events, 0.1 us)
Async XLA Ops:
  0.6 1.5 copy-start.13
  14.3 1.2 copy-start.9
  15.6 29.5 %all-to-all-start = ((bf16[8,400,256]{2,1,0:T(8,128)(2,1)}), bf16[8,400,256]{2,1,0:T(8,128)(2,1)S(1)}, u32[]{:S(2)}, u32[]{:S(2)}) async-start(bf16[8,400,256]{2,1,0:T(8,128)(2,1)} %get-tuple-element.16), calls=%async_computation | async-start | bytes 3276800 | tf_op jit(solution)/shard_map/all_to_all | solution.py:306
  73.7 3.7 %copy-start = (bf16[2048,2304]{1,0:T(8,128)(2,1)S(1)}, bf16[2048,2304]{1,0:T(8,128)(2,1)}, u32[]{:S(2)}) copy-start(bf16[2048,2304]{1,0:T(8,128)(2,1)} %get-tuple-element.17.w) | copy-start | bytes 28311556
  81.2 3.7 %copy-start.6 = (bf16[8,384,256]{2,1,0:T(8,128)(2,1)}, bf16[8,384,256]{2,1,0:T(8,128)(2,1)S(1)}, u32[]{:S(2)}) copy-start(bf16[8,384,256]{2,1,0:T(8,128)(2,1)S(1)} %get-tuple-element.22.l) | copy-start | bytes 4718596
  81.2 3.7 %copy-start.11 = (f32[8,8,256]{2,1,0:T(8,128)}, f32[8,8,256]{2,1,0:T(8,128)S(1)}, u32[]{:S(2)}) copy-start(f32[8,8,256]{2,1,0:T(8,128)S(1)} %get-tuple-element.21) | copy-start | bytes 196612
  81.3 8.2 %copy-start.14 = (f32[1,2304]{1,0:T(1,128)S(1)}, f32[1,2304]{1,0:T(1,128)}, u32[]{:S(2)}) copy-start(f32[1,2304]{1,0:T(1,128)} %param.7) | copy-start | bytes 27652
  81.3 2.5 %collective-permute-start = (bf16[192,2304]{1,0:T(8,128)(2,1)S(1)}, bf16[192,2304]{1,0:T(8,128)(2,1)S(1)}, u32[]{:S(2)}, u32[]{:S(2)}) collective-permute-start(bf16[192,2304]{1,0:T(8,128)(2,1)S(1)} %slice.19), channel_id=1, source_target_pairs={{0,1},{1,0},{2,3},{3,2},{4,5},{5,4},{6,7},{7,6},{8,9},{9,8},{10,11... | collective-permute-start | bytes 2654216 | tf_op jit(solution)/shard_map/ppermute | solution.py:318
  84.9 18.8 %all-to-all-start.2 = ((bf16[8,24,2304]{2,1,0:T(8,128)(2,1)}), bf16[8,24,2304]{2,1,0:T(8,128)(2,1)S(1)}, u32[]{:S(2)}, u32[]{:S(2)}) async-start(bf16[8,24,2304]{2,1,0:T(8,128)(2,1)} %bitcast.4), calls=%async_computation.2 | async-start | bytes 1769472 | tf_op jit(solution)/shard_map/all_to_all | solution.py:309
  121.5 2.4 %collective-permute-start.1 = (bf16[192,2304]{1,0:T(8,128)(2,1)S(1)}, bf16[192,2304]{1,0:T(8,128)(2,1)S(1)}, u32[]{:S(2)}, u32[]{:S(2)}) collective-permute-start(bf16[192,2304]{1,0:T(8,128)(2,1)S(1)} %bitcast.15), channel_id=1, source_target_pairs={{0,1},{1,0},{2,3},{3,2},{4,5},{5,4},{6,7},{7,6},{8,9},{9,8},{10,11... | collective-permute-start | bytes 2654216 | tf_op jit(solution)/shard_map/ppermute | solution.py:325
  124.0 3.7 %copy-start.1 = (bf16[2048,2304]{1,0:T(8,128)(2,1)S(1)}, bf16[2048,2304]{1,0:T(8,128)(2,1)}, u32[]{:S(2)}) copy-start(bf16[2048,2304]{1,0:T(8,128)(2,1)} %get-tuple-element.17.w) | copy-start | bytes 28311556
  131.7 1.2 copy-start.5
  132.9 0.6 copy-start.12
  133.5 25.7 %all-to-all-start.4 = ((bf16[8,384,256]{2,1,0:T(8,128)(2,1)}), bf16[8,384,256]{2,1,0:T(8,128)(2,1)}, u32[]{:S(2)}, u32[]{:S(2)}) async-start(bf16[8,384,256]{2,1,0:T(8,128)(2,1)} %copy-done.5), calls=%async_computation.4 | async-start | bytes 3145728 | tf_op jit(solution)/shard_map/all_to_all | solution.py:306
  159.2 0.9 copy-start.8
  163.0 25.7 %all-to-all-start.5 = ((bf16[8,384,256]{2,1,0:T(8,128)(2,1)}), bf16[8,384,256]{2,1,0:T(8,128)(2,1)S(1)}, u32[]{:S(2)}, u32[]{:S(2)}) async-start(bf16[8,384,256]{2,1,0:T(8,128)(2,1)} %latent_grad.1), calls=%async_computation.5 | async-start | bytes 3145728 | tf_op jit(solution)/shard_map/all_to_all | solution.py:306
  170.7 3.7 %copy-start.2 = (bf16[2048,2304]{1,0:T(8,128)(2,1)S(1)}, bf16[2048,2304]{1,0:T(8,128)(2,1)}, u32[]{:S(2)}) copy-start(bf16[2048,2304]{1,0:T(8,128)(2,1)} %get-tuple-element.17.w) | copy-start | bytes 28311556
  174.3 1.4 copy-start.7
  181.5 3.7 %copy-start.3 = (bf16[2048,2304]{1,0:T(8,128)(2,1)}, bf16[2048,2304]{1,0:T(8,128)(2,1)S(1)}, u32[]{:S(2)}) copy-start(bf16[2048,2304]{1,0:T(8,128)(2,1)S(1)} %grad_first.1.f) | copy-start | bytes 28311556
  188.7 3.7 %copy-start.4 = (bf16[2048,2304]{1,0:T(8,128)(2,1)S(1)}, bf16[2048,2304]{1,0:T(8,128)(2,1)}, u32[]{:S(2)}) copy-start(bf16[2048,2304]{1,0:T(8,128)(2,1)} %copy-done.3) | copy-start | bytes 28311556
  192.4 1.5 copy-start.10

commit v2 on v0

v2 whole, which is shorter than its diff:
```python
import jax
import jax.numpy as jnp
from jax import lax
from jax.experimental import pallas as pl
from jax.experimental.pallas import tpu as pltpu
from jax.sharding import PartitionSpec as P

penalty_weight = 3.0
norm_eps = 1e-06

D = 2304
ROWS = 384
F = 2048
LAYERS = 8
BLOCK = F // LAYERS
EXTRA = 16
SCALE = penalty_weight / ROWS
MATMUL = 2 * ROWS * F * D

CHUNKS = ((0, 192, "z"), (192, 192, "z"))

f32 = jnp.float32
bf16 = jnp.bfloat16
NT = (((1,), (1,)), ((), ()))
TN = (((0,), (0,)), ((), ()))
VMEM = pl.BlockSpec(memory_space=pltpu.VMEM)
HBM = pl.BlockSpec(memory_space=pl.ANY)
SMEM = pl.BlockSpec(memory_space=pltpu.SMEM)


def half(*shape):
    return jax.ShapeDtypeStruct(shape, bf16)


def full(*shape):
    return jax.ShapeDtypeStruct(shape, f32)


def call(kernel, operands, out_shape, name, flops, scratch=(), mib=4, places=None, outs=None):
    many = isinstance(out_shape, (list, tuple))
    return pl.pallas_call(
        kernel,
        in_specs=places or [VMEM] * len(operands),
        out_specs=outs or ([VMEM] * len(out_shape) if many else VMEM),
        out_shape=out_shape,
        scratch_shapes=list(scratch),
        compiler_params=pltpu.CompilerParams(vmem_limit_bytes=mib << 20),
        cost_estimate=pl.CostEstimate(flops=flops, bytes_accessed=flops // 400, transcendentals=0),
        name=name,
    )(*operands)


def block(dy, dz):
    return dy * 4 + dz


def move_y(x):
    return lax.ppermute(x, "layer", [(i, i ^ 4) for i in range(8)])


def move_z(x, dz):
    return lax.ppermute(x, "layer", [(i, (i & 4) | ((i + dz) & 3)) for i in range(8)])


def move_core(x):
    return lax.ppermute(x, "latent", [(i, i ^ 1) for i in range(16)])


def move_x(x, dx):
    return lax.ppermute(x, "latent", [(i, (i & 9) | ((i + 2 * dx) & 6)) for i in range(16)])


def move_lo(x):
    return lax.ppermute(x, "latent", [(i, i ^ 8) for i in range(16)])


def split_sum(rows):
    return rows[:8].astype(f32) + rows[8:].astype(f32)


def split(value):
    high = value.astype(bf16)
    low = (value - high.astype(f32)).astype(bf16)
    return jnp.concatenate([high, low], axis=0)


def part_shapes(n, kind, extra):
    if kind == "z":
        return [half(2, n + extra, BLOCK)] * 4
    return [half(4, n, BLOCK)] * 2


def store_part(refs, kind, dy, dz, n, value):
    if kind == "z":
        refs[dz][dy, :n] = value
    else:
        refs[dy][dz, :n] = value


def encode(pos, acts, weights):
    shapes = []
    for i, (_, n, kind) in enumerate(CHUNKS):
        shapes += part_shapes(n, kind, EXTRA if i == 0 else 0)
    counts = [4 if kind == "z" else 2 for _, _, kind in CHUNKS]

    def kernel(pos_ref, acts_ref, w, *refs):
        groups, at = [], 0
        for count in counts:
            groups.append(refs[at : at + count])
            at += count
        norms, a = refs[at:]
        c = pos_ref[8]
        for start, n, _ in CHUNKS:
            h = n // 2
            for k, core in enumerate((c, 1 - c)):
                source = pl.multiple_of(start + core * h, 32)
                a[start + k * h : start + (k + 1) * h] = acts_ref[pl.ds(source, h)]
        for r in range(LAYERS):
            dy, dz = divmod(r, 4)
            wb = w[block_rows(pos_ref, r)]
            value = lax.dot_general(a[...], wb, NT, preferred_element_type=f32).astype(bf16)
            squares = jnp.zeros((BLOCK, 128), f32)
            for k in range(D // 128):
                x = wb[:, k * 128 : (k + 1) * 128].astype(f32)
                squares = squares + x * x
            total = lax.dot_general(
                jnp.ones((8, 128), f32),
                squares,
                NT,
                precision=lax.Precision.HIGHEST,
                preferred_element_type=f32,
            )
            norm = jnp.sqrt(total + norm_eps)
            norms[pos_ref[r]] = norm
            for i, (start, n, kind) in enumerate(CHUNKS):
                store_part(groups[i], kind, dy, dz, n, value[start : start + n])
                if i == 0:
                    groups[0][dz][dy, n:] = split(norm)

    out = call(
        kernel,
        (pos, acts, weights),
        shapes + [full(LAYERS, 8, BLOCK), half(ROWS, D)],
        "encode",
        MATMUL,
        (),
        24,
        [SMEM, VMEM, VMEM],
    )
    groups, at = [], 0
    for count in counts:
        groups.append(out[at : at + count])
        at += count
    return groups, out[at], out[at + 1]


def block_rows(pos_ref, r):
    return pl.ds(pl.multiple_of(pos_ref[r] * BLOCK, BLOCK), BLOCK)


def add_z(parts, extra):
    n = parts[0].shape[1] - extra

    def kernel(a, b, c, d, out):
        total = a[:, :n].astype(f32) + b[:, :n].astype(f32)
        total = total + (c[:, :n].astype(f32) + d[:, :n].astype(f32))
        out[:, :n] = total.astype(bf16)
        if extra:
            for k in range(2):
                out[k, n:] = split(sum(split_sum(x[k, n:]) for x in (a, b, c, d)))

    return call(kernel, parts, half(2, n + extra, BLOCK), "add_z", 1 << 20)


def add_y(own, other):
    n = own.shape[1]

    def kernel(a, b, *outs):
        for k in range(4):
            outs[k][...] = (a[k].astype(f32) + b[k].astype(f32)).astype(bf16)

    return call(kernel, (own, other), [half(n, BLOCK)] * 4, "add_y", 1 << 20)


def activate_z(pos, own, other, bias, extra):
    n = own.shape[1] - extra

    def kernel(pos_ref, a, b, bias_ref, out):
        for dy in range(2):
            pre = a[dy, :n].astype(f32) + b[1 - dy, :n].astype(f32)
            pre = pre + bias_ref[pos_ref[block(dy, 0)]]
            out[dy, :n] = jnp.maximum(pre, 0.0).astype(bf16)
            if extra:
                out[dy, n:] = split(split_sum(a[dy, n:]) + split_sum(b[1 - dy, n:]))

    return call(
        kernel,
        (pos, own, other, bias),
        half(2, n + extra, BLOCK),
        "activate_z",
        1 << 20,
        places=[SMEM, VMEM, VMEM, VMEM],
    )


def activate_y(pos, parts, bias):
    def kernel(pos_ref, a, b, c, d, bias_ref, out):
        pre = a[...].astype(f32) + b[...].astype(f32)
        pre = pre + (c[...].astype(f32) + d[...].astype(f32))
        out[...] = jnp.maximum(pre + bias_ref[pos_ref[0]], 0.0).astype(bf16)

    return call(
        kernel,
        (pos, *parts, bias),
        half(*parts[0].shape),
        "activate_y",
        1 << 20,
        places=[SMEM] + [VMEM] * 5,
    )


def stack(parts):
    def kernel(*refs):
        for k in range(4):
            refs[4][k] = refs[k][...]

    return call(kernel, parts, half(4, *parts[0].shape), "stack", 1 << 18)


def read_part(refs, kind, dy, dz):
    if kind == "z":
        return refs[dz][dy]
    return refs[dy][dz]


def decode(pos, active, kind, extra, weights):
    width = 768
    count = len(active)
    n = active[0].shape[1] - extra

    def kernel(pos_ref, *refs):
        g, w = refs[:count], refs[count]
        lat, mine, other = refs[count + 1 : count + 4]
        flat = refs[-1]
        for r in range(LAYERS):
            dy, dz = divmod(r, 4)
            part = read_part(g, kind, dy, dz)
            x = part[:n].astype(f32)
            lat[pos_ref[r]] = (x * x).astype(bf16)
            if extra:
                refs[count + 4][pos_ref[r]] = split_sum(part[n:])[:1]
        for j in range(LAYERS):
            flat[:, j * BLOCK : (j + 1) * BLOCK] = lat[j]
        for k in range(D // width):
            cols = slice(k * width, (k + 1) * width)
            value = jnp.dot(flat[...], w[:, cols], preferred_element_type=f32).astype(bf16)
            mine[:, cols] = value[: n // 2]
            other[:, cols] = value[n // 2 :]

    shapes = [half(LAYERS, n, BLOCK), half(n // 2, D), half(n // 2, D)]
    if extra:
        shapes.append(full(LAYERS, 1, BLOCK))
    return call(
        kernel,
        (pos, *active, weights),
        shapes,
        "decode",
        MATMUL * n // ROWS,
        [pltpu.VMEM((n, F), bf16)],
        20,
        [SMEM] + [VMEM] * (count + 1),
    )


def add_core(pos, own, other):
    n = own.shape[0] // 4

    def kernel(pos_ref, a, b, *refs):
        outs, held = refs[:4], refs[4]
        total = a[...].astype(f32) + b[...].astype(f32)
        for k in range(4):
            held[k] = total[k * n : (k + 1) * n].astype(bf16)
        for k in range(4):
            outs[k][...] = held[lax.rem(pos_ref[9] + k, 4)]

    return call(
        kernel,
        (pos, own, other),
        [half(n, D)] * 4,
        "add_core",
        1 << 20,
        [pltpu.VMEM((4, n, D), bf16)],
        places=[SMEM, VMEM, VMEM],
    )


def add_x(parts):
    def kernel(a, b, c, d, out):
        total = a[...].astype(f32) + b[...].astype(f32)
        out[...] = (total + (c[...].astype(f32) + d[...].astype(f32))).astype(bf16)

    return call(kernel, parts, half(*parts[0].shape), "add_x", 1 << 19)


def error(own, other, bias, acts):
    def kernel(a, b, bias_ref, x, out):
        value = a[...].astype(f32) + b[...].astype(f32) + bias_ref[...]
        out[...] = ((value - x[...].astype(f32)) * (2.0 / ROWS)).astype(bf16)

    return call(kernel, (own, other, bias, acts), half(*own.shape), "error", 1 << 19)


def join(pos, parts):
    n = parts[0].shape[0]

    def kernel(pos_ref, a, b, c, d, out, held):
        for k, piece in enumerate((a, b, c, d)):
            held[lax.rem(pos_ref[9] + 4 - k, 4)] = piece[...].astype(f32)
        out[...] = jnp.concatenate([held[k] for k in range(4)], axis=0).astype(bf16)

    return call(
        kernel,
        (pos, *parts),
        half(4 * n, D),
        "join",
        1 << 19,
        [pltpu.VMEM((4, n, D), f32)],
        places=[SMEM] + [VMEM] * 4,
    )


def backward(pos, near, far, kind, weights):
    n = 2 * near.shape[0]

    def kernel(pos_ref, a, b, w, *refs):
        e = refs[-1]
        e[: n // 2] = a[...]
        e[n // 2 :] = b[...]
        for r in range(LAYERS):
            value = lax.dot_general(
                e[...], w[block_rows(pos_ref, r)], NT, preferred_element_type=f32
            ).astype(bf16)
            store_part(refs, kind, *divmod(r, 4), n, value)

    out = call(
        kernel,
        (pos, near, far, weights),
        part_shapes(n, kind, 0) + [half(n, D)],
        "backward",
        MATMUL * n // ROWS,
        mib=20,
        places=[SMEM] + [VMEM] * 3,
    )
    return out[:-1], out[-1]


def latent_grad_z(pos, own, other, active, total):
    n = own.shape[1]

    def kernel(pos_ref, a, b, x, t, out):
        for dy in range(2):
            back = a[dy].astype(f32) + b[1 - dy].astype(f32) + SCALE * t[pos_ref[block(dy, 0)]]
            out[dy] = (back * (2.0 * x[dy, :n].astype(f32))).astype(bf16)

    return call(
        kernel,
        (pos, own, other, active, total),
        half(*own.shape),
        "latent_grad_z",
        1 << 20,
        places=[SMEM] + [VMEM] * 4,
    )


def latent_grad_y(pos, parts, active, total):
    def kernel(pos_ref, a, b, c, d, x, t, out):
        back = a[...].astype(f32) + b[...].astype(f32)
        back = back + (c[...].astype(f32) + d[...].astype(f32)) + SCALE * t[pos_ref[0]]
        out[...] = (back * (2.0 * x[...].astype(f32))).astype(bf16)

    return call(
        kernel,
        (pos, *parts, active, total),
        half(*parts[0].shape),
        "latent_grad_y",
        1 << 20,
        places=[SMEM] + [VMEM] * 6,
    )


def grad_first(lats, errors, norms, weights):
    width = 768
    count = len(lats)

    def kernel(*refs):
        ls, es = refs[:count], refs[count : 2 * count]
        n, w, out, bias, lhs, rhs = refs[2 * count :]
        sums = jnp.zeros((1, D), f32)
        for e, (start, rows, _) in zip(es, CHUNKS):
            rhs[start : start + rows] = e[...]
            sums = sums + jnp.sum(e[...].astype(f32), axis=0, keepdims=True)
        bias[...] = sums
        for j in range(LAYERS):
            for l, (start, rows, _) in zip(ls, CHUNKS):
                lhs[start : start + rows] = l[j]
            usage = jnp.sum(lhs[...].astype(f32), axis=0, keepdims=True)
            column = (SCALE * jnp.broadcast_to(usage, (8, BLOCK)) / n[j]).T[:, :1]
            rows = pl.ds(j * BLOCK, BLOCK)
            for k in range(D // width):
                cols = slice(k * width, (k + 1) * width)
                g = lax.dot_general(lhs[...], rhs[:, cols], TN, preferred_element_type=f32)
                out[rows, cols] = (g + column * w[rows, cols].astype(f32)).astype(bf16)

    return call(
        kernel,
        (*lats, *errors, norms, weights),
        [half(F, D), full(1, D)],
        "grad_first",
        MATMUL,
        [pltpu.VMEM((ROWS, BLOCK), bf16), pltpu.VMEM((ROWS, D), bf16)],
        26,
    )


def grad_second(pos, dpres, acts, first):
    width = 768
    steps = D // width
    counts = [len(d) for d in dpres]

    def kernel(pos_ref, *refs):
        groups, at = [], 0
        for count in counts:
            groups.append(refs[at : at + count])
            at += count
        a, f, out, bias, lhs, buf, sem = refs[at:]
        copies = []
        for r in range(LAYERS):
            dy, dz = divmod(r, 4)
            for g, (start, rows, kind) in zip(groups, CHUNKS):
                lhs[start : start + rows] = read_part(g, kind, dy, dz)
            bias[pos_ref[r]] = jnp.sum(lhs[...].astype(f32), axis=0, keepdims=True)
            rows = block_rows(pos_ref, r)
            slot = r % 4
            for k in range(steps):
                cols = slice(k * width, (k + 1) * width)
                g = lax.dot_general(lhs[...], a[:, cols], TN, preferred_element_type=f32)
                g = (g + f[rows, cols].astype(f32)).astype(bf16)
                if r >= 4:
                    copies[(r - 4) * steps + k].wait()
                buf[slot, :, cols] = g
                copy = pltpu.make_async_copy(
                    buf.at[slot, :, cols], out.at[rows, cols], sem.at[slot, k]
                )
                copy.start()
                copies.append(copy)
        for copy in copies[-4 * steps :]:
            copy.wait()

    flat = [x for d in dpres for x in d]
    return call(
        kernel,
        (pos, *flat, acts, first),
        [half(F, D), full(LAYERS, 1, BLOCK)],
        "grad_second",
        MATMUL,
        [
            pltpu.VMEM((ROWS, BLOCK), bf16),
            pltpu.VMEM((4, BLOCK, D), bf16),
            pltpu.SemaphoreType.DMA((4, steps)),
        ],
        20,
        [SMEM] + [VMEM] * (len(flat) + 2),
        [HBM, VMEM],
    )


def scatter_z(parts, extra=0):
    got = [move_z(parts[d], d) for d in (2, 1, 3)]
    own = add_z([parts[0]] + got, extra)
    return own, move_y(own)


def scatter_y(parts):
    pieces = add_y(parts[0], move_y(parts[1]))
    return [pieces[0]] + [move_z(pieces[d], d) for d in (2, 1, 3)]


def gather(own, kind):
    got = {d: move_z(own, 4 - d) for d in (2, 1, 3)}
    parts = [own, got[1], got[2], got[3]]
    if kind == "z":
        return parts
    both = stack(parts)
    return [both, move_y(both)]


def body(acts, decoder, enc_bias, dec_bias):
    inputs = acts[0]
    layer = lax.axis_index("layer")
    latent = lax.axis_index("latent")
    core, chip = latent & 1, (latent >> 1) & 3
    blocks = [
        ((layer // 4 + dy) % 2) * 4 + (layer % 4 + dz) % 4 for dy in range(2) for dz in range(4)
    ]
    pos = jnp.stack(blocks + [core, chip]).astype(jnp.int32)
    bias = enc_bias.reshape(LAYERS, 1, BLOCK)
    pieces = [
        lax.dynamic_slice(inputs, (start + core * (n // 2) + chip * (n // 8), 0), (n // 8, D))
        for start, n, _ in CHUNKS
    ]
    inputs, weights, pos, bias, dec_bias, pieces = lax.optimization_barrier(
        (inputs, decoder[0], pos, bias, dec_bias, pieces)
    )

    groups, norms, rows = encode(pos, inputs, weights)
    lats, errors, dpres = [], [], []
    total = None
    for i, (start, n, kind) in enumerate(CHUNKS):
        extra = EXTRA if i == 0 else 0
        if kind == "z":
            active = activate_z(pos, *scatter_z(groups[i], extra), bias, extra)
        else:
            active = activate_y(pos, scatter_y(groups[i]), bias)
        out = decode(pos, gather(active, kind), kind, extra, weights)
        lat, mine, other = out[:3]
        if extra:
            total = out[3]
        parts = add_core(pos, mine, move_core(other))
        own = add_x([parts[0]] + [move_x(parts[d], d) for d in (2, 1, 3)])
        piece = error(own, move_lo(own), dec_bias, pieces[i])
        got = {d: move_x(piece, d) for d in (2, 1, 3)}
        near = join(pos, [piece, got[1], got[2], got[3]])
        back, both = backward(pos, near, move_core(near), kind, weights)
        if kind == "z":
            dpre = latent_grad_z(pos, *scatter_z(back), active, total)
        else:
            dpre = latent_grad_y(pos, scatter_y(back), active, total)
        lats.append(lat)
        errors.append(both)
        dpres.append(gather(dpre, kind))
    first, dec_grad = grad_first(lats, errors, norms, weights)
    grad, enc_grad = grad_second(pos, dpres, rows, first)
    return grad[None], enc_grad.reshape(F), dec_grad, total.reshape(F)


def solution(mesh):
    placed = (P("layer", None, None), P("layer", "latent", None), P("latent"), P("layer", None))
    return jax.shard_map(
        body,
        mesh=mesh,
        in_specs=placed,
        out_specs=(P("layer", "latent", None), P("latent"), P("layer", None), P("latent")),
        check_vma=False,
    )
```

time: 369 us -> 178 us (0.48); the launches traced: 369 us -> 175 us
  waiting for transfers between devices: 268 us -> 45.1 us
  starting transfers between devices: 0.12 us -> 80.1 us
  matrix products: 53.9 us -> 0 us
  Pallas kernels: 0 us -> 41.9 us
  blocking collectives: 21.7 us -> 0 us
  between operations: 13.8 us -> 1.19 us
  other arithmetic: 11.5 us -> 0 us
  local copies, waits for them, and re-layouts: 0.63 us -> 6.24 us
    psum x3 -> x0, waiting for transfers between devices: 268 us -> none  [the longest x1 93 us: body(): lax.psum(part.astype(jnp.bfloat16), 'layer').astype(jnp.float32)]
    ppermute x0 -> x46, starting transfers between devices: none -> 80.1 us  [the longest x24 47.5 us: move_z(): return lax.ppermute(x, 'layer', [(i, i & 4 | i + dz & 3) for i in range(8)])]
    dot_general x5 -> x0, matrix products: 53.9 us -> none  [the longest x1 15.2 us: body(): lax.dot_general(dpre_bf, inputs, contract_first, preferred_element_type=j...]
    ppermute x0 -> x46, waiting for transfers between devices: none -> 45.1 us  [the longest x24 28.7 us: move_z(): return lax.ppermute(x, 'layer', [(i, i & 4 | i + dz & 3) for i in range(8)])]
    pallas_call x0 -> x23, Pallas kernels: none -> 41.9 us  [call(): pl.pallas_call(kernel, in_specs=places or [VMEM] * len(operands), out_spe...]
    psum x1 -> x0, blocking collectives: 21.7 us -> none  [body(): total_norm = lax.psum(norms, 'layer')]
    reduce_sum x2 -> x0, other arithmetic: 5.87 us -> none  [the longest x1 3.05 us: body(): grad_enc_bias = jnp.sum(dpre, axis=0)]
    dot_general x1 -> x0, other arithmetic: 5.58 us -> none  [body(): jnp.einsum('fd,fd->f', weights, weights, preferred_element_type=jnp.float32)]
  transfers between devices with their start and end apart: 3 -> 46, of which waited for: 3 -> 20; matrix products, arithmetic and copies ran while one was open for 4% -> 0% of each run, Pallas kernels for 0% -> 15%
where the time goes in v2:
time: 178 us; the launch traced here: 175 us
  starting transfers between devices  80.1 us (45%)
  waiting for transfers between devices  45.1 us (25%)
  Pallas kernels  41.9 us (24%)
  local copies, waits for them, and re-layouts  6.24 us (4%)
    ppermute x24, starting transfers between devices, move_z(): return lax.ppermute(x, 'layer', [(i, i & 4 | i + dz & 3) for i in range(8)])  47.5 us
    pallas_call x23, Pallas kernels, call(): pl.pallas_call(kernel, in_specs=places or [VMEM] * len(operands), out_spe...  41.9 us
    ppermute x24, waiting for transfers between devices, move_z(): return lax.ppermute(x, 'layer', [(i, i & 4 | i + dz & 3) for i in range(8)])  28.7 us
    ppermute x12, starting transfers between devices, move_x(): lax.ppermute(x, 'latent', [(i, i & 9 | i + 2 * dx & 6) for i in range(16)])  19.5 us
    ppermute x12, waiting for transfers between devices, move_x(): lax.ppermute(x, 'latent', [(i, i & 9 | i + 2 * dx & 6) for i in range(16)])  13.9 us
    ppermute x4, starting transfers between devices, move_y(): return lax.ppermute(x, 'layer', [(i, i ^ 4) for i in range(8)])  10.4 us
    unnamed x12, local copies, waits for them, and re-layouts  5.18 us
  transfers between devices with their start and end apart: 46, of which 20 were waited for; matrix products, arithmetic and copies ran while one was open for 0% of the time, Pallas kernels for 15%

profile of v2, /device:TPU:0, one launch (start us, length us, event | category | flops | bytes accessed | tf_op | source)
XLA Modules:
  0.0 174.5 jit_solution(14153781410314063908)
XLA Ops:
  1.8 3.7 %copy-done = bf16[1,2048,2304]{2,1,0:T(8,128)(2,1)S(1)} copy-done((bf16[1,2048,2304]{2,1,0:T(8,128)(2,1)S(1)}, bf16[1,2048,2304]{2,1,0:T(8,128)(2,1)}, u32[]{:S(2)}) %copy-start) | copy-done | bytes 9437208
  5.5 1.5 copy-done.5
  7.0 6.0 %encode.1 = (bf16[2,208,256]{2,1,0:T(8,128)(2,1)S(1)}, bf16[2,208,256]{2,1,0:T(8,128)(2,1)S(1)}, bf16[2,208,256]{2,1,0:T(8,128)(2,1)S(1)}, bf16[2,208,256]{2,1,0...) custom-call(s32[10]{0:T(128)S(1)} %stack.43.pos_ref, ...), custom_call_target="tpu_custom_call" | custom-call | flops 3623878656 | bytes 9059696 | tf_op jit(solution)/shard_map/encode/pallas_call | solution.py:41
  13.0 4.0 %collective-permute-start.23 = (bf16[2,192,256]{2,1,0:T(8,128)(2,1)S(1)}, bf16[2,192,256]{2,1,0:T(8,128)(2,1)S(1)}, u32[]{:S(2)}, u32[]{:S(2)}) collective-permute-start(bf16[2,192,256]{2,1,0:T(8,128)(2,1)S(1)} %get-tuple-element.72), channel_id=1, source_target_pairs={{0,32},{16,48},{32,0},{48,16},{64,96},{80,112},{96,64},{112,80},{1... | collective-permute-start | bytes 589832 | tf_op jit(solution)/shard_map/ppermute | solution.py:62
  18.0 2.2 %collective-permute-start.25 = (bf16[2,192,256]{2,1,0:T(8,128)(2,1)S(1)}, bf16[2,192,256]{2,1,0:T(8,128)(2,1)S(1)}, u32[]{:S(2)}, u32[]{:S(2)}) collective-permute-start(bf16[2,192,256]{2,1,0:T(8,128)(2,1)S(1)} %get-tuple-element.74), channel_id=1, source_target_pairs={{0,48},{16,0},{32,16},{48,32},{64,112},{80,64},{96,80},{112,96},{1... | collective-permute-start | bytes 589832 | tf_op jit(solution)/shard_map/ppermute | solution.py:62
  21.1 1.6 collective-permute-done.23.b
  22.7 3.7 %collective-permute-start.2 = (bf16[2,208,256]{2,1,0:T(8,128)(2,1)S(1)}, bf16[2,208,256]{2,1,0:T(8,128)(2,1)S(1)}, u32[]{:S(2)}, u32[]{:S(2)}) collective-permute-start(bf16[2,208,256]{2,1,0:T(8,128)(2,1)S(1)} %get-tuple-element.56), channel_id=1, source_target_pairs={{0,48},{16,0},{32,16},{48,32},{64,112},{80,64},{96,80},{112,96},{1... | collective-permute-start | bytes 638984 | tf_op jit(solution)/shard_map/ppermute | solution.py:62
  26.5 4.1 %collective-permute-done.24.c = bf16[2,192,256]{2,1,0:T(8,128)(2,1)S(1)} collective-permute-done((bf16[2,192,256]{2,1,0:T(8,128)(2,1)S(1)}, bf16[2,192,256]{2,1,0:T(8,128)(2,1)S(1)}, u32[]{:S(2)}, u32[]{:S(2)}) %collective-permute-start.24) | collective-permute-done | bytes 196640 | tf_op jit(solution)/shard_map/ppermute | solution.py:62
  30.7 3.3 %collective-permute-start.26 = (bf16[2,192,256]{2,1,0:T(8,128)(2,1)S(1)}, bf16[2,192,256]{2,1,0:T(8,128)(2,1)S(1)}, u32[]{:S(2)}, u32[]{:S(2)}) collective-permute-start(bf16[2,192,256]{2,1,0:T(8,128)(2,1)S(1)} %add_z.6.a), channel_id=1, source_target_pairs={{0,64},{16,80},{32,96},{48,112},{64,0},{80,16},{96,32},{112,48},{1... | collective-permute-start | bytes 589832 | tf_op jit(solution)/shard_map/ppermute | solution.py:58
  34.0 1.3 collective-permute-done.1.c
  36.1 3.3 %collective-permute-start.3 = (bf16[2,208,256]{2,1,0:T(8,128)(2,1)S(1)}, bf16[2,208,256]{2,1,0:T(8,128)(2,1)S(1)}, u32[]{:S(2)}, u32[]{:S(2)}) collective-permute-start(bf16[2,208,256]{2,1,0:T(8,128)(2,1)S(1)} %add_z.4.a), channel_id=1, source_target_pairs={{0,64},{16,80},{32,96},{48,112},{64,0},{80,16},{96,32},{112,48},{1... | collective-permute-start | bytes 638984 | tf_op jit(solution)/shard_map/ppermute | solution.py:58
  41.2 3.0 %collective-permute-start.28 = (bf16[2,192,256]{2,1,0:T(8,128)(2,1)S(1)}, bf16[2,192,256]{2,1,0:T(8,128)(2,1)S(1)}, u32[]{:S(2)}, u32[]{:S(2)}) collective-permute-start(bf16[2,192,256]{2,1,0:T(8,128)(2,1)S(1)} %activate_z.3.refs_0_.x), channel_id=1, source_target_pairs={{0,32},{16,48},{32,0},{48,16},{64,96},{80,112},{96,64},{112,80},{1... | collective-permute-start | bytes 589832 | tf_op jit(solution)/shard_map/ppermute | solution.py:62
  45.4 1.5 collective-permute-start.6
  46.9 2.4 %collective-permute-start.5 = (bf16[2,208,256]{2,1,0:T(8,128)(2,1)S(1)}, bf16[2,208,256]{2,1,0:T(8,128)(2,1)S(1)}, u32[]{:S(2)}, u32[]{:S(2)}) collective-permute-start(bf16[2,208,256]{2,1,0:T(8,128)(2,1)S(1)} %activate_z.2.refs_0_.x), channel_id=1, source_target_pairs={{0,32},{16,48},{32,0},{48,16},{64,96},{80,112},{96,64},{112,80},{1... | collective-permute-start | bytes 638984 | tf_op jit(solution)/shard_map/ppermute | solution.py:62
  49.3 1.3 collective-permute-start.4
  50.6 3.6 %collective-permute-done.28.refs_2_ = bf16[2,192,256]{2,1,0:T(8,128)(2,1)S(1)} collective-permute-done((bf16[2,192,256]{2,1,0:T(8,128)(2,1)S(1)}, bf16[2,192,256]{2,1,0:T(8,128)(2,1)S(1)}, u32[]{:S(2)}, u32[]{:S(2)}) %collective-permute-start.28) | collective-permute-done | bytes 196640 | tf_op jit(solution)/shard_map/ppermute | solution.py:62
  54.3 2.7 %decode.3 = (bf16[8,192,256]{2,1,0:T(8,128)(2,1)S(1)}, bf16[96,2304]{1,0:T(8,128)(2,1)S(1)}, bf16[96,2304]{1,0:T(8,128)(2,1)S(1)}) custom-call(s32[10]{0:T(128)S(1)} %stack.43.pos_ref, bf16[2,192,256]{2,1,0:T(8,128)(2,1)S(1)} %activate_z.3.refs_0_.x, bf16[2,192,256]{2,1,0:T(8,128)(2,1)S(1)} %collective-permute-done.27.refs_1_, ...), custom_call_target="tpu_custom_call" | custom-call | flops 1811939328 | bytes 4529848 | tf_op jit(solution)/shard_map/decode/pallas_call | solution.py:41
  57.3 4.4 %collective-permute-done.5.refs_2_ = bf16[2,208,256]{2,1,0:T(8,128)(2,1)S(1)} collective-permute-done((bf16[2,208,256]{2,1,0:T(8,128)(2,1)S(1)}, bf16[2,208,256]{2,1,0:T(8,128)(2,1)S(1)}, u32[]{:S(2)}, u32[]{:S(2)}) %collective-permute-start.5) | collective-permute-done | bytes 213024 | tf_op jit(solution)/shard_map/ppermute | solution.py:62
  61.7 3.1 %decode.2 = (bf16[8,192,256]{2,1,0:T(8,128)(2,1)S(1)}, bf16[96,2304]{1,0:T(8,128)(2,1)S(1)}, bf16[96,2304]{1,0:T(8,128)(2,1)S(1)}, f32[8,1,256]{2,1,0:T(1,128)}) custom-call(s32[10]{0:T(128)S(1)} %stack.43.pos_ref, bf16[2,208,256]{2,1,0:T(8,128)(2,1)S(1)} %activate_z.2.refs_0_.x, bf16[2,208,256]{2,1,0:T(8,128)(2,1)S(1)} %collective-permute-done.4.refs_1_, ...), custom_call_target="tpu_custom_call" | custom-call | flops 1811939328 | bytes 4529848 | tf_op jit(solution)/shard_map/decode/pallas_call | solution.py:41
  65.6 3.1 %collective-permute-start.31 = (bf16[24,2304]{1,0:T(8,128)(2,1)S(1)}, bf16[24,2304]{1,0:T(8,128)(2,1)S(1)}, u32[]{:S(2)}, u32[]{:S(2)}) collective-permute-start(bf16[24,2304]{1,0:T(8,128)(2,1)S(1)} %get-tuple-element.78), channel_id=1, source_target_pairs={{0,4},{1,5},{2,6},{3,7},{4,0},{5,1},{6,2},{7,3},{8,12},{9,13},{10,... | collective-permute-start | bytes 331784 | tf_op jit(solution)/shard_map/ppermute | solution.py:70
  69.3 2.7 %collective-permute-start.33 = (bf16[24,2304]{1,0:T(8,128)(2,1)S(1)}, bf16[24,2304]{1,0:T(8,128)(2,1)S(1)}, u32[]{:S(2)}, u32[]{:S(2)}) collective-permute-start(bf16[24,2304]{1,0:T(8,128)(2,1)S(1)} %get-tuple-element.80), channel_id=1, source_target_pairs={{0,6},{1,7},{2,0},{3,1},{4,2},{5,3},{6,4},{7,5},{8,14},{9,15},{10,... | collective-permute-start | bytes 331784 | tf_op jit(solution)/shard_map/ppermute | solution.py:70
  73.0 2.2 %collective-permute-done.32.c = bf16[24,2304]{1,0:T(8,128)(2,1)S(1)} collective-permute-done((bf16[24,2304]{1,0:T(8,128)(2,1)S(1)}, bf16[24,2304]{1,0:T(8,128)(2,1)S(1)}, u32[]{:S(2)}, u32[]{:S(2)}) %collective-permute-start.32) | collective-permute-done | bytes 110624 | tf_op jit(solution)/shard_map/ppermute | solution.py:70
  76.9 2.0 %collective-permute-start.8 = (bf16[24,2304]{1,0:T(8,128)(2,1)S(1)}, bf16[24,2304]{1,0:T(8,128)(2,1)S(1)}, u32[]{:S(2)}, u32[]{:S(2)}) collective-permute-start(bf16[24,2304]{1,0:T(8,128)(2,1)S(1)} %get-tuple-element.61), channel_id=1, source_target_pairs={{0,4},{1,5},{2,6},{3,7},{4,0},{5,1},{6,2},{7,3},{8,12},{9,13},{10,... | collective-permute-start | bytes 331784 | tf_op jit(solution)/shard_map/ppermute | solution.py:70
  78.9 1.8 %collective-permute-start.9 = (bf16[24,2304]{1,0:T(8,128)(2,1)S(1)}, bf16[24,2304]{1,0:T(8,128)(2,1)S(1)}, u32[]{:S(2)}, u32[]{:S(2)}) collective-permute-start(bf16[24,2304]{1,0:T(8,128)(2,1)S(1)} %get-tuple-element.62), channel_id=1, source_target_pairs={{0,2},{1,3},{2,4},{3,5},{4,6},{5,7},{6,0},{7,1},{8,10},{9,11},{10,... | collective-permute-start | bytes 331784 | tf_op jit(solution)/shard_map/ppermute | solution.py:70
  80.7 1.4 collective-permute-start.10
  83.2 1.8 %collective-permute-start.36 = (bf16[24,2304]{1,0:T(8,128)(2,1)S(1)}, bf16[24,2304]{1,0:T(8,128)(2,1)S(1)}, u32[]{:S(2)}, u32[]{:S(2)}) collective-permute-start(bf16[24,2304]{1,0:T(8,128)(2,1)S(1)} %error.3.a), channel_id=1, source_target_pairs={{0,4},{1,5},{2,6},{3,7},{4,0},{5,1},{6,2},{7,3},{8,12},{9,13},{10,... | collective-permute-start | bytes 331784 | tf_op jit(solution)/shard_map/ppermute | solution.py:70
  86.8 1.4 collective-permute-start.11
  88.2 1.2 collective-permute-done.37.d
  89.5 1.4 collective-permute-done.35.b
  91.7 3.6 %collective-permute-start.14 = (bf16[24,2304]{1,0:T(8,128)(2,1)S(1)}, bf16[24,2304]{1,0:T(8,128)(2,1)S(1)}, u32[]{:S(2)}, u32[]{:S(2)}) collective-permute-start(bf16[24,2304]{1,0:T(8,128)(2,1)S(1)} %error.2.a), channel_id=1, source_target_pairs={{0,6},{1,7},{2,0},{3,1},{4,2},{5,3},{6,4},{7,5},{8,14},{9,15},{10,... | collective-permute-start | bytes 331784 | tf_op jit(solution)/shard_map/ppermute | solution.py:70
  96.2 3.4 %collective-permute-done.14.d = bf16[24,2304]{1,0:T(8,128)(2,1)S(1)} collective-permute-done((bf16[24,2304]{1,0:T(8,128)(2,1)S(1)}, bf16[24,2304]{1,0:T(8,128)(2,1)S(1)}, u32[]{:S(2)}, u32[]{:S(2)}) %collective-permute-start.14) | collective-permute-done | bytes 110624 | tf_op jit(solution)/shard_map/ppermute | solution.py:70
  99.7 2.3 %collective-permute-done.13.c = bf16[24,2304]{1,0:T(8,128)(2,1)S(1)} collective-permute-done((bf16[24,2304]{1,0:T(8,128)(2,1)S(1)}, bf16[24,2304]{1,0:T(8,128)(2,1)S(1)}, u32[]{:S(2)}, u32[]{:S(2)}) %collective-permute-start.13) | collective-permute-done | bytes 110624 | tf_op jit(solution)/shard_map/ppermute | solution.py:70
  103.8 3.8 %backward.3 = (bf16[2,192,256]{2,1,0:T(8,128)(2,1)S(1)}, bf16[2,192,256]{2,1,0:T(8,128)(2,1)S(1)}, bf16[2,192,256]{2,1,0:T(8,128)(2,1)S(1)}, bf16[2,192,256]{2,1,0:T(8,128)(2,1)S(1)}, bf16[192,2304]{1,0:T(8,128)(2,1)S(1)}) custom-call(s32[10]{0:T(128)S(1)} %stack.43.pos_ref, bf16[96,2304]{1,0:T(8,128)(2,1)S(1)} %join.3.a, ...), custom_call_target="tpu_custom_call" | custom-call | flops 1811939328 | bytes 4529848 | tf_op jit(solution)/shard_map/backward/pallas_call | solution.py:41
  107.6 1.8 %collective-permute-start.39 = (bf16[2,192,256]{2,1,0:T(8,128)(2,1)S(1)}, bf16[2,192,256]{2,1,0:T(8,128)(2,1)S(1)}, u32[]{:S(2)}, u32[]{:S(2)}) collective-permute-start(bf16[2,192,256]{2,1,0:T(8,128)(2,1)S(1)} %get-tuple-element.83), channel_id=1, source_target_pairs={{0,32},{16,48},{32,0},{48,16},{64,96},{80,112},{96,64},{112,80},{1... | collective-permute-start | bytes 589832 | tf_op jit(solution)/shard_map/ppermute | solution.py:62
  109.4 1.3 collective-permute-start.40
  110.7 13.6 %collective-permute-start.41 = (bf16[2,192,256]{2,1,0:T(8,128)(2,1)S(1)}, bf16[2,192,256]{2,1,0:T(8,128)(2,1)S(1)}, u32[]{:S(2)}, u32[]{:S(2)}) collective-permute-start(bf16[2,192,256]{2,1,0:T(8,128)(2,1)S(1)} %get-tuple-element.85), channel_id=1, source_target_pairs={{0,48},{16,0},{32,16},{48,32},{64,112},{80,64},{96,80},{112,96},{1... | collective-permute-start | bytes 589832 | tf_op jit(solution)/shard_map/ppermute | solution.py:62
  124.3 3.7 %backward.2 = (bf16[2,192,256]{2,1,0:T(8,128)(2,1)S(1)}, bf16[2,192,256]{2,1,0:T(8,128)(2,1)S(1)}, bf16[2,192,256]{2,1,0:T(8,128)(2,1)S(1)}, bf16[2,192,256]{2,1,0:T(8,128)(2,1)S(1)}, bf16[192,2304]{1,0:T(8,128)(2,1)S(1)}) custom-call(s32[10]{0:T(128)S(1)} %stack.43.pos_ref, bf16[96,2304]{1,0:T(8,128)(2,1)S(1)} %join.2.a, ...), custom_call_target="tpu_custom_call" | custom-call | flops 1811939328 | bytes 4529848 | tf_op jit(solution)/shard_map/backward/pallas_call | solution.py:41
  129.8 2.2 %collective-permute-start.18 = (bf16[2,192,256]{2,1,0:T(8,128)(2,1)S(1)}, bf16[2,192,256]{2,1,0:T(8,128)(2,1)S(1)}, u32[]{:S(2)}, u32[]{:S(2)}) collective-permute-start(bf16[2,192,256]{2,1,0:T(8,128)(2,1)S(1)} %get-tuple-element.69), channel_id=1, source_target_pairs={{0,48},{16,0},{32,16},{48,32},{64,112},{80,64},{96,80},{112,96},{1... | collective-permute-start | bytes 589832 | tf_op jit(solution)/shard_map/ppermute | solution.py:62
  132.1 1.9 %collective-permute-start.42 = (bf16[2,192,256]{2,1,0:T(8,128)(2,1)S(1)}, bf16[2,192,256]{2,1,0:T(8,128)(2,1)S(1)}, u32[]{:S(2)}, u32[]{:S(2)}) collective-permute-start(bf16[2,192,256]{2,1,0:T(8,128)(2,1)S(1)} %add_z.7.a), channel_id=1, source_target_pairs={{0,64},{16,80},{32,96},{48,112},{64,0},{80,16},{96,32},{112,48},{1... | collective-permute-start | bytes 589832 | tf_op jit(solution)/shard_map/ppermute | solution.py:58
  134.0 3.5 %collective-permute-done.16.b = bf16[2,192,256]{2,1,0:T(8,128)(2,1)S(1)} collective-permute-done((bf16[2,192,256]{2,1,0:T(8,128)(2,1)S(1)}, bf16[2,192,256]{2,1,0:T(8,128)(2,1)S(1)}, u32[]{:S(2)}, u32[]{:S(2)}) %collective-permute-start.16) | collective-permute-done | bytes 196640 | tf_op jit(solution)/shard_map/ppermute | solution.py:62
  137.5 2.8 %collective-permute-done.17.c = bf16[2,192,256]{2,1,0:T(8,128)(2,1)S(1)} collective-permute-done((bf16[2,192,256]{2,1,0:T(8,128)(2,1)S(1)}, bf16[2,192,256]{2,1,0:T(8,128)(2,1)S(1)}, u32[]{:S(2)}, u32[]{:S(2)}) %collective-permute-start.17) | collective-permute-done | bytes 196640 | tf_op jit(solution)/shard_map/ppermute | solution.py:62
  140.4 1.9 %collective-permute-start.19 = (bf16[2,192,256]{2,1,0:T(8,128)(2,1)S(1)}, bf16[2,192,256]{2,1,0:T(8,128)(2,1)S(1)}, u32[]{:S(2)}, u32[]{:S(2)}) collective-permute-start(bf16[2,192,256]{2,1,0:T(8,128)(2,1)S(1)} %add_z.5.a), channel_id=1, source_target_pairs={{0,64},{16,80},{32,96},{48,112},{64,0},{80,16},{96,32},{112,48},{1... | collective-permute-start | bytes 589832 | tf_op jit(solution)/shard_map/ppermute | solution.py:58
  143.1 2.2 %collective-permute-start.44 = (bf16[2,192,256]{2,1,0:T(8,128)(2,1)S(1)}, bf16[2,192,256]{2,1,0:T(8,128)(2,1)S(1)}, u32[]{:S(2)}, u32[]{:S(2)}) collective-permute-start(bf16[2,192,256]{2,1,0:T(8,128)(2,1)S(1)} %latent_grad_z.3.refs_4_), channel_id=1, source_target_pairs={{0,32},{16,48},{32,0},{48,16},{64,96},{80,112},{96,64},{112,80},{1... | collective-permute-start | bytes 589832 | tf_op jit(solution)/shard_map/ppermute | solution.py:62
  146.4 2.5 %collective-permute-done.19.b = bf16[2,192,256]{2,1,0:T(8,128)(2,1)S(1)} collective-permute-done((bf16[2,192,256]{2,1,0:T(8,128)(2,1)S(1)}, bf16[2,192,256]{2,1,0:T(8,128)(2,1)S(1)}, u32[]{:S(2)}, u32[]{:S(2)}) %collective-permute-start.19) | collective-permute-done | bytes 196640 | tf_op jit(solution)/shard_map/ppermute | solution.py:58
  149.6 1.7 collective-permute-start.21
  151.2 5.1 %collective-permute-done.45.refs_7_ = bf16[2,192,256]{2,1,0:T(8,128)(2,1)S(1)} collective-permute-done((bf16[2,192,256]{2,1,0:T(8,128)(2,1)S(1)}, bf16[2,192,256]{2,1,0:T(8,128)(2,1)S(1)}, u32[]{:S(2)}, u32[]{:S(2)}) %collective-permute-start.45) | collective-permute-done | bytes 196640 | tf_op jit(solution)/shard_map/ppermute | solution.py:62
  156.3 6.4 %grad_first.1 = (bf16[2048,2304]{1,0:T(8,128)(2,1)S(1)}, f32[1,2304]{1,0:T(1,128)}) custom-call(bf16[8,192,256]{2,1,0:T(8,128)(2,1)S(1)} %get-tuple-element.87.refs_0_, bf16[8,192,256]{2,1,0:T(8,128)(2,1)S(1)} %get-tuple-element.88.refs_1_, bf16[192,2304]{1,0:T(8,128)(2,1)S(1)} %get-tuple-element.89.refs_2_, ...), custom_call_target="tpu_custom_call" | custom-call | flops 3623878656 | bytes 9059696 | tf_op jit(solution)/shard_map/grad_first/pallas_call | solution.py:41
  164.1 10.2 %grad_second.1 = (bf16[2048,2304]{1,0:T(8,128)(2,1)}, f32[8,1,256]{2,1,0:T(1,128)}) custom-call(s32[10]{0:T(128)S(1)} %stack.43.pos_ref, bf16[2,192,256]{2,1,0:T(8,128)(2,1)S(1)} %latent_grad_z.2.refs_0_, bf16[2,192,256]{2,1,0:T(8,128)(2,1)S(1)} %collective-permute-done.20.refs_1_, bf16[2,192,256]{2,1,0:T(8,128)(2,1)S(1)} %collective-permute-done.21.refs_2_, ...), custom_call_target="tpu_custom_call" | custom-call | flops 3623878656 | bytes 9059696 | tf_op jit(solution)/shard_map/grad_second/pallas_call | solution.py:41
  (81 shorter events, 23.8 us)
Async XLA Ops:
  0.6 38.8 %copy-start.3 = (f32[2048]{0:T(1024)S(1)}, f32[2048]{0:T(1024)}, u32[]{:S(2)}) copy-start(f32[2048]{0:T(1024)} %param.6) | copy-start | bytes 24580
  7.0 47.3 %copy-start.1 = (bf16[1,2048,2304]{2,1,0:T(8,128)(2,1)S(1)}, bf16[1,2048,2304]{2,1,0:T(8,128)(2,1)}, u32[]{:S(2)}) copy-start(bf16[1,2048,2304]{2,1,0:T(8,128)(2,1)} %param.5) | copy-start | bytes 28311556
  13.0 9.8 %collective-permute-start.23 = (bf16[2,192,256]{2,1,0:T(8,128)(2,1)S(1)}, bf16[2,192,256]{2,1,0:T(8,128)(2,1)S(1)}, u32[]{:S(2)}, u32[]{:S(2)}) collective-permute-start(bf16[2,192,256]{2,1,0:T(8,128)(2,1)S(1)} %get-tuple-element.72), channel_id=1, source_target_pairs={{0,32},{16,48},{32,0},{48,16},{64,96},{80,112},{96,64},{112,80},{1... | collective-permute-start | bytes 589832 | tf_op jit(solution)/shard_map/ppermute | solution.py:62
  17.0 13.6 %collective-permute-start.24 = (bf16[2,192,256]{2,1,0:T(8,128)(2,1)S(1)}, bf16[2,192,256]{2,1,0:T(8,128)(2,1)S(1)}, u32[]{:S(2)}, u32[]{:S(2)}) collective-permute-start(bf16[2,192,256]{2,1,0:T(8,128)(2,1)S(1)} %get-tuple-element.73), channel_id=1, source_target_pairs={{0,16},{16,32},{32,48},{48,0},{64,80},{80,96},{96,112},{112,64},{1... | collective-permute-start | bytes 589832 | tf_op jit(solution)/shard_map/ppermute | solution.py:62
  18.0 12.6 %collective-permute-start.25 = (bf16[2,192,256]{2,1,0:T(8,128)(2,1)S(1)}, bf16[2,192,256]{2,1,0:T(8,128)(2,1)S(1)}, u32[]{:S(2)}, u32[]{:S(2)}) collective-permute-start(bf16[2,192,256]{2,1,0:T(8,128)(2,1)S(1)} %get-tuple-element.74), channel_id=1, source_target_pairs={{0,48},{16,0},{32,16},{48,32},{64,112},{80,64},{96,80},{112,96},{1... | collective-permute-start | bytes 589832 | tf_op jit(solution)/shard_map/ppermute | solution.py:62
  20.2 13.8 %collective-permute-start = (bf16[2,208,256]{2,1,0:T(8,128)(2,1)S(1)}, bf16[2,208,256]{2,1,0:T(8,128)(2,1)S(1)}, u32[]{:S(2)}, u32[]{:S(2)}) collective-permute-start(bf16[2,208,256]{2,1,0:T(8,128)(2,1)S(1)} %get-tuple-element.54), channel_id=1, source_target_pairs={{0,32},{16,48},{32,0},{48,16},{64,96},{80,112},{96,64},{112,80},{1... | collective-permute-start | bytes 638984 | tf_op jit(solution)/shard_map/ppermute | solution.py:62
  20.2 15.0 %collective-permute-start.1 = (bf16[2,208,256]{2,1,0:T(8,128)(2,1)S(1)}, bf16[2,208,256]{2,1,0:T(8,128)(2,1)S(1)}, u32[]{:S(2)}, u32[]{:S(2)}) collective-permute-start(bf16[2,208,256]{2,1,0:T(8,128)(2,1)S(1)} %get-tuple-element.55), channel_id=1, source_target_pairs={{0,16},{16,32},{32,48},{48,0},{64,80},{80,96},{96,112},{112,64},{1... | collective-permute-start | bytes 638984 | tf_op jit(solution)/shard_map/ppermute | solution.py:62
  22.7 13.3 %collective-permute-start.2 = (bf16[2,208,256]{2,1,0:T(8,128)(2,1)S(1)}, bf16[2,208,256]{2,1,0:T(8,128)(2,1)S(1)}, u32[]{:S(2)}, u32[]{:S(2)}) collective-permute-start(bf16[2,208,256]{2,1,0:T(8,128)(2,1)S(1)} %get-tuple-element.56), channel_id=1, source_target_pairs={{0,48},{16,0},{32,16},{48,32},{64,112},{80,64},{96,80},{112,96},{1... | collective-permute-start | bytes 638984 | tf_op jit(solution)/shard_map/ppermute | solution.py:62
  30.7 8.7 %collective-permute-start.26 = (bf16[2,192,256]{2,1,0:T(8,128)(2,1)S(1)}, bf16[2,192,256]{2,1,0:T(8,128)(2,1)S(1)}, u32[]{:S(2)}, u32[]{:S(2)}) collective-permute-start(bf16[2,192,256]{2,1,0:T(8,128)(2,1)S(1)} %add_z.6.a), channel_id=1, source_target_pairs={{0,64},{16,80},{32,96},{48,112},{64,0},{80,16},{96,32},{112,48},{1... | collective-permute-start | bytes 589832 | tf_op jit(solution)/shard_map/ppermute | solution.py:58
  36.1 8.6 %collective-permute-start.3 = (bf16[2,208,256]{2,1,0:T(8,128)(2,1)S(1)}, bf16[2,208,256]{2,1,0:T(8,128)(2,1)S(1)}, u32[]{:S(2)}, u32[]{:S(2)}) collective-permute-start(bf16[2,208,256]{2,1,0:T(8,128)(2,1)S(1)} %add_z.4.a), channel_id=1, source_target_pairs={{0,64},{16,80},{32,96},{48,112},{64,0},{80,16},{96,32},{112,48},{1... | collective-permute-start | bytes 638984 | tf_op jit(solution)/shard_map/ppermute | solution.py:58
  40.0 9.3 %collective-permute-start.29 = (bf16[2,192,256]{2,1,0:T(8,128)(2,1)S(1)}, bf16[2,192,256]{2,1,0:T(8,128)(2,1)S(1)}, u32[]{:S(2)}, u32[]{:S(2)}) collective-permute-start(bf16[2,192,256]{2,1,0:T(8,128)(2,1)S(1)} %activate_z.3.refs_0_.x), channel_id=1, source_target_pairs={{0,16},{16,32},{32,48},{48,0},{64,80},{80,96},{96,112},{112,64},{1... | collective-permute-start | bytes 589832 | tf_op jit(solution)/shard_map/ppermute | solution.py:62
  41.2 13.1 %collective-permute-start.28 = (bf16[2,192,256]{2,1,0:T(8,128)(2,1)S(1)}, bf16[2,192,256]{2,1,0:T(8,128)(2,1)S(1)}, u32[]{:S(2)}, u32[]{:S(2)}) collective-permute-start(bf16[2,192,256]{2,1,0:T(8,128)(2,1)S(1)} %activate_z.3.refs_0_.x), channel_id=1, source_target_pairs={{0,32},{16,48},{32,0},{48,16},{64,96},{80,112},{96,64},{112,80},{1... | collective-permute-start | bytes 589832 | tf_op jit(solution)/shard_map/ppermute | solution.py:62
  44.2 10.1 %collective-permute-start.27 = (bf16[2,192,256]{2,1,0:T(8,128)(2,1)S(1)}, bf16[2,192,256]{2,1,0:T(8,128)(2,1)S(1)}, u32[]{:S(2)}, u32[]{:S(2)}) collective-permute-start(bf16[2,192,256]{2,1,0:T(8,128)(2,1)S(1)} %activate_z.3.refs_0_.x), channel_id=1, source_target_pairs={{0,48},{16,0},{32,16},{48,32},{64,112},{80,64},{96,80},{112,96},{1... | collective-permute-start | bytes 589832 | tf_op jit(solution)/shard_map/ppermute | solution.py:62
  45.4 11.9 %collective-permute-start.6 = (bf16[2,208,256]{2,1,0:T(8,128)(2,1)S(1)}, bf16[2,208,256]{2,1,0:T(8,128)(2,1)S(1)}, u32[]{:S(2)}, u32[]{:S(2)}) collective-permute-start(bf16[2,208,256]{2,1,0:T(8,128)(2,1)S(1)} %activate_z.2.refs_0_.x), channel_id=1, source_target_pairs={{0,16},{16,32},{32,48},{48,0},{64,80},{80,96},{96,112},{112,64},{1... | collective-permute-start | bytes 638984 | tf_op jit(solution)/shard_map/ppermute | solution.py:62
  46.9 14.7 %collective-permute-start.5 = (bf16[2,208,256]{2,1,0:T(8,128)(2,1)S(1)}, bf16[2,208,256]{2,1,0:T(8,128)(2,1)S(1)}, u32[]{:S(2)}, u32[]{:S(2)}) collective-permute-start(bf16[2,208,256]{2,1,0:T(8,128)(2,1)S(1)} %activate_z.2.refs_0_.x), channel_id=1, source_target_pairs={{0,32},{16,48},{32,0},{48,16},{64,96},{80,112},{96,64},{112,80},{1... | collective-permute-start | bytes 638984 | tf_op jit(solution)/shard_map/ppermute | solution.py:62
  49.3 12.4 %collective-permute-start.4 = (bf16[2,208,256]{2,1,0:T(8,128)(2,1)S(1)}, bf16[2,208,256]{2,1,0:T(8,128)(2,1)S(1)}, u32[]{:S(2)}, u32[]{:S(2)}) collective-permute-start(bf16[2,208,256]{2,1,0:T(8,128)(2,1)S(1)} %activate_z.2.refs_0_.x), channel_id=1, source_target_pairs={{0,48},{16,0},{32,16},{48,32},{64,112},{80,64},{96,80},{112,96},{1... | collective-permute-start | bytes 638984 | tf_op jit(solution)/shard_map/ppermute | solution.py:62
  56.9 7.9 %collective-permute-start.30 = (bf16[96,2304]{1,0:T(8,128)(2,1)S(1)}, bf16[96,2304]{1,0:T(8,128)(2,1)S(1)}, u32[]{:S(2)}, u32[]{:S(2)}) collective-permute-start(bf16[96,2304]{1,0:T(8,128)(2,1)S(1)} %get-tuple-element.76), channel_id=1, source_target_pairs={{0,1},{1,0},{2,3},{3,2},{4,5},{5,4},{6,7},{7,6},{8,9},{9,8},{10,11... | collective-permute-start | bytes 1327112 | tf_op jit(solution)/shard_map/ppermute | solution.py:66
  64.8 11.3 %collective-permute-start.7 = (bf16[96,2304]{1,0:T(8,128)(2,1)S(1)}, bf16[96,2304]{1,0:T(8,128)(2,1)S(1)}, u32[]{:S(2)}, u32[]{:S(2)}) collective-permute-start(bf16[96,2304]{1,0:T(8,128)(2,1)S(1)} %get-tuple-element.59), channel_id=1, source_target_pairs={{0,1},{1,0},{2,3},{3,2},{4,5},{5,4},{6,7},{7,6},{8,9},{9,8},{10,11... | collective-permute-start | bytes 1327112 | tf_op jit(solution)/shard_map/ppermute | solution.py:66
  65.6 7.4 %collective-permute-start.31 = (bf16[24,2304]{1,0:T(8,128)(2,1)S(1)}, bf16[24,2304]{1,0:T(8,128)(2,1)S(1)}, u32[]{:S(2)}, u32[]{:S(2)}) collective-permute-start(bf16[24,2304]{1,0:T(8,128)(2,1)S(1)} %get-tuple-element.78), channel_id=1, source_target_pairs={{0,4},{1,5},{2,6},{3,7},{4,0},{5,1},{6,2},{7,3},{8,12},{9,13},{10,... | collective-permute-start | bytes 331784 | tf_op jit(solution)/shard_map/ppermute | solution.py:70
  68.7 6.5 %collective-permute-start.32 = (bf16[24,2304]{1,0:T(8,128)(2,1)S(1)}, bf16[24,2304]{1,0:T(8,128)(2,1)S(1)}, u32[]{:S(2)}, u32[]{:S(2)}) collective-permute-start(bf16[24,2304]{1,0:T(8,128)(2,1)S(1)} %get-tuple-element.79), channel_id=1, source_target_pairs={{0,2},{1,3},{2,4},{3,5},{4,6},{5,7},{6,0},{7,1},{8,10},{9,11},{10,... | collective-permute-start | bytes 331784 | tf_op jit(solution)/shard_map/ppermute | solution.py:70
  69.3 6.0 %collective-permute-start.33 = (bf16[24,2304]{1,0:T(8,128)(2,1)S(1)}, bf16[24,2304]{1,0:T(8,128)(2,1)S(1)}, u32[]{:S(2)}, u32[]{:S(2)}) collective-permute-start(bf16[24,2304]{1,0:T(8,128)(2,1)S(1)} %get-tuple-element.80), channel_id=1, source_target_pairs={{0,6},{1,7},{2,0},{3,1},{4,2},{5,3},{6,4},{7,5},{8,14},{9,15},{10,... | collective-permute-start | bytes 331784 | tf_op jit(solution)/shard_map/ppermute | solution.py:70
  75.3 6.8 %collective-permute-start.34 = (bf16[24,2304]{1,0:T(8,128)(2,1)S(1)}, bf16[24,2304]{1,0:T(8,128)(2,1)S(1)}, u32[]{:S(2)}, u32[]{:S(2)}) collective-permute-start(bf16[24,2304]{1,0:T(8,128)(2,1)S(1)} %add_x.3.a), channel_id=1, source_target_pairs={{0,8},{1,9},{2,10},{3,11},{4,12},{5,13},{6,14},{7,15},{8,0},{9,1},... | collective-permute-start | bytes 331784 | tf_op jit(solution)/shard_map/ppermute | solution.py:74
  76.9 8.0 %collective-permute-start.8 = (bf16[24,2304]{1,0:T(8,128)(2,1)S(1)}, bf16[24,2304]{1,0:T(8,128)(2,1)S(1)}, u32[]{:S(2)}, u32[]{:S(2)}) collective-permute-start(bf16[24,2304]{1,0:T(8,128)(2,1)S(1)} %get-tuple-element.61), channel_id=1, source_target_pairs={{0,4},{1,5},{2,6},{3,7},{4,0},{5,1},{6,2},{7,3},{8,12},{9,13},{10,... | collective-permute-start | bytes 331784 | tf_op jit(solution)/shard_map/ppermute | solution.py:70
  78.9 6.7 %collective-permute-start.9 = (bf16[24,2304]{1,0:T(8,128)(2,1)S(1)}, bf16[24,2304]{1,0:T(8,128)(2,1)S(1)}, u32[]{:S(2)}, u32[]{:S(2)}) collective-permute-start(bf16[24,2304]{1,0:T(8,128)(2,1)S(1)} %get-tuple-element.62), channel_id=1, source_target_pairs={{0,2},{1,3},{2,4},{3,5},{4,6},{5,7},{6,0},{7,1},{8,10},{9,11},{10,... | collective-permute-start | bytes 331784 | tf_op jit(solution)/shard_map/ppermute | solution.py:70
  80.7 6.1 %collective-permute-start.10 = (bf16[24,2304]{1,0:T(8,128)(2,1)S(1)}, bf16[24,2304]{1,0:T(8,128)(2,1)S(1)}, u32[]{:S(2)}, u32[]{:S(2)}) collective-permute-start(bf16[24,2304]{1,0:T(8,128)(2,1)S(1)} %get-tuple-element.63), channel_id=1, source_target_pairs={{0,6},{1,7},{2,0},{3,1},{4,2},{5,3},{6,4},{7,5},{8,14},{9,15},{10,... | collective-permute-start | bytes 331784 | tf_op jit(solution)/shard_map/ppermute | solution.py:70
  82.2 7.3 %collective-permute-start.37 = (bf16[24,2304]{1,0:T(8,128)(2,1)S(1)}, bf16[24,2304]{1,0:T(8,128)(2,1)S(1)}, u32[]{:S(2)}, u32[]{:S(2)}) collective-permute-start(bf16[24,2304]{1,0:T(8,128)(2,1)S(1)} %error.3.a), channel_id=1, source_target_pairs={{0,6},{1,7},{2,0},{3,1},{4,2},{5,3},{6,4},{7,5},{8,14},{9,15},{10,... | collective-permute-start | bytes 331784 | tf_op jit(solution)/shard_map/ppermute | solution.py:70
  83.2 6.3 %collective-permute-start.36 = (bf16[24,2304]{1,0:T(8,128)(2,1)S(1)}, bf16[24,2304]{1,0:T(8,128)(2,1)S(1)}, u32[]{:S(2)}, u32[]{:S(2)}) collective-permute-start(bf16[24,2304]{1,0:T(8,128)(2,1)S(1)} %error.3.a), channel_id=1, source_target_pairs={{0,4},{1,5},{2,6},{3,7},{4,0},{5,1},{6,2},{7,3},{8,12},{9,13},{10,... | collective-permute-start | bytes 331784 | tf_op jit(solution)/shard_map/ppermute | solution.py:70
  84.9 6.0 %collective-permute-start.35 = (bf16[24,2304]{1,0:T(8,128)(2,1)S(1)}, bf16[24,2304]{1,0:T(8,128)(2,1)S(1)}, u32[]{:S(2)}, u32[]{:S(2)}) collective-permute-start(bf16[24,2304]{1,0:T(8,128)(2,1)S(1)} %error.3.a), channel_id=1, source_target_pairs={{0,2},{1,3},{2,4},{3,5},{4,6},{5,7},{6,0},{7,1},{8,10},{9,11},{10,... | collective-permute-start | bytes 331784 | tf_op jit(solution)/shard_map/ppermute | solution.py:70
  86.8 4.8 %collective-permute-start.11 = (bf16[24,2304]{1,0:T(8,128)(2,1)S(1)}, bf16[24,2304]{1,0:T(8,128)(2,1)S(1)}, u32[]{:S(2)}, u32[]{:S(2)}) collective-permute-start(bf16[24,2304]{1,0:T(8,128)(2,1)S(1)} %add_x.2.a), channel_id=1, source_target_pairs={{0,8},{1,9},{2,10},{3,11},{4,12},{5,13},{6,14},{7,15},{8,0},{9,1},... | collective-permute-start | bytes 331784 | tf_op jit(solution)/shard_map/ppermute | solution.py:74
  91.5 12.3 %collective-permute-start.38 = (bf16[96,2304]{1,0:T(8,128)(2,1)S(1)}, bf16[96,2304]{1,0:T(8,128)(2,1)S(1)}, u32[]{:S(2)}, u32[]{:S(2)}) collective-permute-start(bf16[96,2304]{1,0:T(8,128)(2,1)S(1)} %join.3.a), channel_id=1, source_target_pairs={{0,1},{1,0},{2,3},{3,2},{4,5},{5,4},{6,7},{7,6},{8,9},{9,8},{10,11... | collective-permute-start | bytes 1327112 | tf_op jit(solution)/shard_map/ppermute | solution.py:66
  91.7 8.0 %collective-permute-start.14 = (bf16[24,2304]{1,0:T(8,128)(2,1)S(1)}, bf16[24,2304]{1,0:T(8,128)(2,1)S(1)}, u32[]{:S(2)}, u32[]{:S(2)}) collective-permute-start(bf16[24,2304]{1,0:T(8,128)(2,1)S(1)} %error.2.a), channel_id=1, source_target_pairs={{0,6},{1,7},{2,0},{3,1},{4,2},{5,3},{6,4},{7,5},{8,14},{9,15},{10,... | collective-permute-start | bytes 331784 | tf_op jit(solution)/shard_map/ppermute | solution.py:70
  95.3 6.6 %collective-permute-start.13 = (bf16[24,2304]{1,0:T(8,128)(2,1)S(1)}, bf16[24,2304]{1,0:T(8,128)(2,1)S(1)}, u32[]{:S(2)}, u32[]{:S(2)}) collective-permute-start(bf16[24,2304]{1,0:T(8,128)(2,1)S(1)} %error.2.a), channel_id=1, source_target_pairs={{0,4},{1,5},{2,6},{3,7},{4,0},{5,1},{6,2},{7,3},{8,12},{9,13},{10,... | collective-permute-start | bytes 331784 | tf_op jit(solution)/shard_map/ppermute | solution.py:70
  95.3 7.8 %collective-permute-start.12 = (bf16[24,2304]{1,0:T(8,128)(2,1)S(1)}, bf16[24,2304]{1,0:T(8,128)(2,1)S(1)}, u32[]{:S(2)}, u32[]{:S(2)}) collective-permute-start(bf16[24,2304]{1,0:T(8,128)(2,1)S(1)} %error.2.a), channel_id=1, source_target_pairs={{0,2},{1,3},{2,4},{3,5},{4,6},{5,7},{6,0},{7,1},{8,10},{9,11},{10,... | collective-permute-start | bytes 331784 | tf_op jit(solution)/shard_map/ppermute | solution.py:70
  103.7 20.6 %collective-permute-start.15 = (bf16[96,2304]{1,0:T(8,128)(2,1)S(1)}, bf16[96,2304]{1,0:T(8,128)(2,1)S(1)}, u32[]{:S(2)}, u32[]{:S(2)}) collective-permute-start(bf16[96,2304]{1,0:T(8,128)(2,1)S(1)} %join.2.a), channel_id=1, source_target_pairs={{0,1},{1,0},{2,3},{3,2},{4,5},{5,4},{6,7},{7,6},{8,9},{9,8},{10,11... | collective-permute-start | bytes 1327112 | tf_op jit(solution)/shard_map/ppermute | solution.py:66
  107.6 22.2 %collective-permute-start.39 = (bf16[2,192,256]{2,1,0:T(8,128)(2,1)S(1)}, bf16[2,192,256]{2,1,0:T(8,128)(2,1)S(1)}, u32[]{:S(2)}, u32[]{:S(2)}) collective-permute-start(bf16[2,192,256]{2,1,0:T(8,128)(2,1)S(1)} %get-tuple-element.83), channel_id=1, source_target_pairs={{0,32},{16,48},{32,0},{48,16},{64,96},{80,112},{96,64},{112,80},{1... | collective-permute-start | bytes 589832 | tf_op jit(solution)/shard_map/ppermute | solution.py:62
  109.4 22.5 %collective-permute-start.40 = (bf16[2,192,256]{2,1,0:T(8,128)(2,1)S(1)}, bf16[2,192,256]{2,1,0:T(8,128)(2,1)S(1)}, u32[]{:S(2)}, u32[]{:S(2)}) collective-permute-start(bf16[2,192,256]{2,1,0:T(8,128)(2,1)S(1)} %get-tuple-element.84), channel_id=1, source_target_pairs={{0,16},{16,32},{32,48},{48,0},{64,80},{80,96},{96,112},{112,64},{1... | collective-permute-start | bytes 589832 | tf_op jit(solution)/shard_map/ppermute | solution.py:62
  110.7 21.3 %collective-permute-start.41 = (bf16[2,192,256]{2,1,0:T(8,128)(2,1)S(1)}, bf16[2,192,256]{2,1,0:T(8,128)(2,1)S(1)}, u32[]{:S(2)}, u32[]{:S(2)}) collective-permute-start(bf16[2,192,256]{2,1,0:T(8,128)(2,1)S(1)} %get-tuple-element.85), channel_id=1, source_target_pairs={{0,48},{16,0},{32,16},{48,32},{64,112},{80,64},{96,80},{112,96},{1... | collective-permute-start | bytes 589832 | tf_op jit(solution)/shard_map/ppermute | solution.py:62
  128.1 9.4 %collective-permute-start.16 = (bf16[2,192,256]{2,1,0:T(8,128)(2,1)S(1)}, bf16[2,192,256]{2,1,0:T(8,128)(2,1)S(1)}, u32[]{:S(2)}, u32[]{:S(2)}) collective-permute-start(bf16[2,192,256]{2,1,0:T(8,128)(2,1)S(1)} %get-tuple-element.67), channel_id=1, source_target_pairs={{0,32},{16,48},{32,0},{48,16},{64,96},{80,112},{96,64},{112,80},{1... | collective-permute-start | bytes 589832 | tf_op jit(solution)/shard_map/ppermute | solution.py:62
  128.7 11.6 %collective-permute-start.17 = (bf16[2,192,256]{2,1,0:T(8,128)(2,1)S(1)}, bf16[2,192,256]{2,1,0:T(8,128)(2,1)S(1)}, u32[]{:S(2)}, u32[]{:S(2)}) collective-permute-start(bf16[2,192,256]{2,1,0:T(8,128)(2,1)S(1)} %get-tuple-element.68), channel_id=1, source_target_pairs={{0,16},{16,32},{32,48},{48,0},{64,80},{80,96},{96,112},{112,64},{1... | collective-permute-start | bytes 589832 | tf_op jit(solution)/shard_map/ppermute | solution.py:62
  129.8 10.5 %collective-permute-start.18 = (bf16[2,192,256]{2,1,0:T(8,128)(2,1)S(1)}, bf16[2,192,256]{2,1,0:T(8,128)(2,1)S(1)}, u32[]{:S(2)}, u32[]{:S(2)}) collective-permute-start(bf16[2,192,256]{2,1,0:T(8,128)(2,1)S(1)} %get-tuple-element.69), channel_id=1, source_target_pairs={{0,48},{16,0},{32,16},{48,32},{64,112},{80,64},{96,80},{112,96},{1... | collective-permute-start | bytes 589832 | tf_op jit(solution)/shard_map/ppermute | solution.py:62
  132.1 10.3 %collective-permute-start.42 = (bf16[2,192,256]{2,1,0:T(8,128)(2,1)S(1)}, bf16[2,192,256]{2,1,0:T(8,128)(2,1)S(1)}, u32[]{:S(2)}, u32[]{:S(2)}) collective-permute-start(bf16[2,192,256]{2,1,0:T(8,128)(2,1)S(1)} %add_z.7.a), channel_id=1, source_target_pairs={{0,64},{16,80},{32,96},{48,112},{64,0},{80,16},{96,32},{112,48},{1... | collective-permute-start | bytes 589832 | tf_op jit(solution)/shard_map/ppermute | solution.py:58
  140.4 8.4 %collective-permute-start.19 = (bf16[2,192,256]{2,1,0:T(8,128)(2,1)S(1)}, bf16[2,192,256]{2,1,0:T(8,128)(2,1)S(1)}, u32[]{:S(2)}, u32[]{:S(2)}) collective-permute-start(bf16[2,192,256]{2,1,0:T(8,128)(2,1)S(1)} %add_z.5.a), channel_id=1, source_target_pairs={{0,64},{16,80},{32,96},{48,112},{64,0},{80,16},{96,32},{112,48},{1... | collective-permute-start | bytes 589832 | tf_op jit(solution)/shard_map/ppermute | solution.py:58
  143.0 13.3 %collective-permute-start.45 = (bf16[2,192,256]{2,1,0:T(8,128)(2,1)S(1)}, bf16[2,192,256]{2,1,0:T(8,128)(2,1)S(1)}, u32[]{:S(2)}, u32[]{:S(2)}) collective-permute-start(bf16[2,192,256]{2,1,0:T(8,128)(2,1)S(1)} %latent_grad_z.3.refs_4_), channel_id=1, source_target_pairs={{0,16},{16,32},{32,48},{48,0},{64,80},{80,96},{96,112},{112,64},{1... | collective-permute-start | bytes 589832 | tf_op jit(solution)/shard_map/ppermute | solution.py:62
  143.1 19.6 %collective-permute-start.44 = (bf16[2,192,256]{2,1,0:T(8,128)(2,1)S(1)}, bf16[2,192,256]{2,1,0:T(8,128)(2,1)S(1)}, u32[]{:S(2)}, u32[]{:S(2)}) collective-permute-start(bf16[2,192,256]{2,1,0:T(8,128)(2,1)S(1)} %latent_grad_z.3.refs_4_), channel_id=1, source_target_pairs={{0,32},{16,48},{32,0},{48,16},{64,96},{80,112},{96,64},{112,80},{1... | collective-permute-start | bytes 589832 | tf_op jit(solution)/shard_map/ppermute | solution.py:62
  145.3 17.4 %collective-permute-start.43 = (bf16[2,192,256]{2,1,0:T(8,128)(2,1)S(1)}, bf16[2,192,256]{2,1,0:T(8,128)(2,1)S(1)}, u32[]{:S(2)}, u32[]{:S(2)}) collective-permute-start(bf16[2,192,256]{2,1,0:T(8,128)(2,1)S(1)} %latent_grad_z.3.refs_4_), channel_id=1, source_target_pairs={{0,48},{16,0},{32,16},{48,32},{64,112},{80,64},{96,80},{112,96},{1... | collective-permute-start | bytes 589832 | tf_op jit(solution)/shard_map/ppermute | solution.py:62
  149.5 14.0 %collective-permute-start.22 = (bf16[2,192,256]{2,1,0:T(8,128)(2,1)S(1)}, bf16[2,192,256]{2,1,0:T(8,128)(2,1)S(1)}, u32[]{:S(2)}, u32[]{:S(2)}) collective-permute-start(bf16[2,192,256]{2,1,0:T(8,128)(2,1)S(1)} %latent_grad_z.2.refs_0_), channel_id=1, source_target_pairs={{0,16},{16,32},{32,48},{48,0},{64,80},{80,96},{96,112},{112,64},{1... | collective-permute-start | bytes 589832 | tf_op jit(solution)/shard_map/ppermute | solution.py:62
  149.6 13.9 %collective-permute-start.21 = (bf16[2,192,256]{2,1,0:T(8,128)(2,1)S(1)}, bf16[2,192,256]{2,1,0:T(8,128)(2,1)S(1)}, u32[]{:S(2)}, u32[]{:S(2)}) collective-permute-start(bf16[2,192,256]{2,1,0:T(8,128)(2,1)S(1)} %latent_grad_z.2.refs_0_), channel_id=1, source_target_pairs={{0,32},{16,48},{32,0},{48,16},{64,96},{80,112},{96,64},{112,80},{1... | collective-permute-start | bytes 589832 | tf_op jit(solution)/shard_map/ppermute | solution.py:62
  156.3 7.8 %collective-permute-start.20 = (bf16[2,192,256]{2,1,0:T(8,128)(2,1)S(1)}, bf16[2,192,256]{2,1,0:T(8,128)(2,1)S(1)}, u32[]{:S(2)}, u32[]{:S(2)}) collective-permute-start(bf16[2,192,256]{2,1,0:T(8,128)(2,1)S(1)} %latent_grad_z.2.refs_0_), channel_id=1, source_target_pairs={{0,48},{16,0},{32,16},{48,32},{64,112},{80,64},{96,80},{112,96},{1... | collective-permute-start | bytes 589832 | tf_op jit(solution)/shard_map/ppermute | solution.py:62
  (4 other events, 80.5 us)

commit v3 on v0

v3 whole, which is shorter than its diff:
```python
import jax
import jax.numpy as jnp
from jax import lax
from jax.experimental import pallas as pl
from jax.experimental.pallas import tpu as pltpu
from jax.sharding import PartitionSpec as P

penalty_weight = 3.0
norm_eps = 1e-06

D = 2304
ROWS = 384
HALF = ROWS // 2
F = 2048
LAYERS = 8
BLOCK = F // LAYERS
CHIPS = 8
PIECE = HALF // CHIPS
EXTRA = 16
GROUPS = ((0, 4), (2, 1, 3), (6, 5, 7))
SCALE = penalty_weight / ROWS
MATMUL = 2 * ROWS * F * D

NEAR = (0, 1, 2, 3)
FAR = (4, 5, 6, 7)
STEPS = (2, 1, 3)

f32 = jnp.float32
bf16 = jnp.bfloat16
NT = (((1,), (1,)), ((), ()))
TN = (((0,), (0,)), ((), ()))
VMEM = pl.BlockSpec(memory_space=pltpu.VMEM)
HBM = pl.BlockSpec(memory_space=pl.ANY)


def half(*shape):
    return jax.ShapeDtypeStruct(shape, bf16)


def full(*shape):
    return jax.ShapeDtypeStruct(shape, f32)


def call(kernel, operands, out_shape, name, flops, scratch=(), mib=4, places=None, outs=None, aliases=None):
    many = isinstance(out_shape, (list, tuple))
    return pl.pallas_call(
        kernel,
        in_specs=places or [VMEM] * len(operands),
        out_specs=outs or ([VMEM] * len(out_shape) if many else VMEM),
        out_shape=out_shape,
        scratch_shapes=list(scratch),
        input_output_aliases=aliases or {},
        compiler_params=pltpu.CompilerParams(vmem_limit_bytes=mib << 20),
        cost_estimate=pl.CostEstimate(flops=flops, bytes_accessed=flops // 400, transcendentals=0),
        name=name,
    )(*operands)


def move_y(x):
    return lax.ppermute(x, "layer", [(i, i ^ 4) for i in range(8)])


def move_z(x, dz):
    return lax.ppermute(x, "layer", [(i, i & 4 | ((i + dz) & 3)) for i in range(8)])


def move_core(x):
    return lax.ppermute(x, "latent", [(i, i ^ 1) for i in range(16)])


def move_lo(x):
    return lax.ppermute(x, "latent", [(i, i ^ 8) for i in range(16)])


def move_x(x, dx):
    return lax.ppermute(x, "latent", [(i, i & 9 | ((i + 2 * dx) & 6)) for i in range(16)])


def near(index, r):
    dy, step = divmod(r, 4)
    return ((index & 4) ^ (4 * dy)) | ((index + step) & 3)


def block_of(r):
    return near(lax.axis_index("layer"), r)


def chip_of(r):
    return near(lax.axis_index("latent") >> 1, r)


def block_rows(r):
    return pl.ds(pl.multiple_of(block_of(r) * BLOCK, BLOCK), BLOCK)


def split_sum(rows):
    return rows[:8].astype(f32) + rows[8:].astype(f32)


def split(value):
    high = value.astype(bf16)
    low = (value - high.astype(f32)).astype(bf16)
    return jnp.concatenate([high, low], axis=0)


def product(rows, weights):
    return lax.dot_general(rows, weights, NT, preferred_element_type=f32).astype(bf16)


def encode_far(acts, weights):
    def kernel(a, w, *refs):
        rows = refs[4]
        c = lax.axis_index("latent") & 1
        for k, source in enumerate((c, 1 - c)):
            rows[k * HALF : (k + 1) * HALF] = a[pl.ds(pl.multiple_of(source * HALF, HALF), HALF)]
        for k, r in enumerate(FAR):
            refs[k][...] = product(rows[...], w[block_rows(r)])

    return call(
        kernel,
        (acts, weights),
        [half(ROWS, BLOCK)] * 4 + [half(ROWS, D)],
        "encode_far",
        MATMUL // 2,
        mib=8,
    )


def encode_near(rows, weights):
    def kernel(a, w, *outs):
        for k, r in enumerate(NEAR):
            outs[k][...] = product(a[...], w[block_rows(r)])

    return call(
        kernel, (rows, weights), [half(ROWS, BLOCK)] * 4, "encode_near", MATMUL // 2, mib=8
    )


def prepare(rows, weights):
    def kernel(a, w, norms, piece, held):
        for r in range(LAYERS):
            wb = w[block_rows(r)]
            squares = jnp.zeros((BLOCK, 128), f32)
            for i in range(D // 128):
                x = wb[:, i * 128 : (i + 1) * 128].astype(f32)
                squares = squares + x * x
            total = lax.dot_general(
                jnp.ones((8, 128), f32),
                squares,
                NT,
                precision=lax.Precision.HIGHEST,
                preferred_element_type=f32,
            )
            norms[r] = jnp.sqrt(total + norm_eps)
        value = a[:HALF].astype(f32)
        for k in range(CHIPS):
            held[k] = value[k * PIECE : (k + 1) * PIECE]
        piece[...] = held[chip_of(0)].astype(bf16)

    return call(
        kernel,
        (rows, weights),
        [full(LAYERS, 8, BLOCK), half(PIECE, D)],
        "prepare",
        1 << 30,
        [pltpu.VMEM((CHIPS, PIECE, D), f32)],
        8,
    )


def add(terms):
    value = terms[0][:ROWS].astype(f32)
    for x in terms[1:]:
        value = value + x[:ROWS].astype(f32)
    return value


def add_extra(terms):
    return sum(split_sum(x[ROWS:]) for x in terms)


def add_z(terms):
    extra = terms[0].shape[0] - ROWS

    def kernel(*refs):
        t, out = refs[:4], refs[4]
        out[:ROWS] = add(t).astype(bf16)
        if extra:
            out[ROWS:] = split(add_extra(t))

    return call(kernel, terms, half(*terms[0].shape), "add_z", 1 << 20)


def activate(terms, bias):
    def kernel(*refs):
        t, (b, out) = refs[:5], refs[5:]
        out[...] = jnp.maximum(add(t) + b[block_of(0)], 0.0).astype(bf16)

    return call(kernel, (*terms, bias), half(ROWS, BLOCK), "activate", 1 << 20)


def decode(active, weights, blocks, before=None, after=()):
    width = 768

    def kernel(*refs):
        g, w, refs = refs[:4], refs[4], refs[5:]
        if before is not None:
            acc, lat, mine, other = refs
        else:
            lat, out = refs[len(after) :]
        for k in range(4):
            x = g[k][...].astype(f32)
            lat[k] = (x * x).astype(bf16)
        for i in range(D // width):
            cols = slice(i * width, (i + 1) * width)
            value = None if before is None else acc[:, cols]
            for k, r in enumerate(blocks):
                term = jnp.dot(lat[k], w[block_rows(r), cols], preferred_element_type=f32)
                value = term if value is None else value + term
            if before is None:
                out[:, cols] = value
            else:
                value = value.astype(bf16)
                mine[:, cols] = value[:HALF]
                other[:, cols] = value[HALF:]

    shapes = [half(4, ROWS, BLOCK)]
    if before is None:
        shapes += [full(ROWS, D)]
    else:
        shapes += [half(HALF, D)] * 2
    operands = (*active, weights, *after) + (() if before is None else (before,))
    return call(kernel, operands, shapes, "decode", MATMUL // 2, mib=20)


def add_core(own, other):
    def kernel(a, b, *refs):
        outs, held = refs[:CHIPS], refs[CHIPS]
        for k in range(CHIPS):
            rows = slice(k * PIECE, (k + 1) * PIECE)
            held[k] = a[rows].astype(f32) + b[rows].astype(f32)
        for k in range(CHIPS):
            outs[k][...] = held[chip_of(k)].astype(bf16)

    return call(
        kernel,
        (own, other),
        [half(PIECE, D)] * CHIPS,
        "add_core",
        1 << 20,
        [pltpu.VMEM((CHIPS, PIECE, D), f32)],
    )


def add_x(terms):
    def kernel(a, b, c, d, out):
        value = a[...].astype(f32) + b[...].astype(f32)
        out[...] = (value + (c[...].astype(f32) + d[...].astype(f32))).astype(bf16)

    return call(kernel, terms, half(PIECE, D), "add_x", 1 << 20)


def error(terms, bias, acts):
    def kernel(*refs):
        t, (b, x, out) = refs[:5], refs[5:]
        value = t[0][...].astype(f32)
        for y in t[1:]:
            value = value + y[...].astype(f32)
        out[...] = ((value + b[...] - x[...].astype(f32)) * (2.0 / ROWS)).astype(bf16)

    return call(kernel, (*terms, bias, acts), half(PIECE, D), "error", 1 << 20)


def join(parts):
    def kernel(*refs):
        out, held = refs[CHIPS:]
        for k in range(CHIPS):
            held[chip_of(k)] = refs[k][...].astype(f32)
        out[...] = jnp.concatenate([held[k] for k in range(CHIPS)], axis=0).astype(bf16)

    return call(
        kernel,
        parts,
        half(HALF, D),
        "join",
        1 << 20,
        [pltpu.VMEM((CHIPS, PIECE, D), f32)],
    )


def backward_far(near_rows, far_rows, rows, norms, weights):
    def kernel(a, b, x, n, w, *refs):
        outs, both = refs[:4], refs[4]
        both[:HALF] = a[...]
        both[HALF:ROWS] = b[...]
        for k, r in enumerate(FAR):
            outs[k][:ROWS] = product(both[:ROWS], w[block_rows(r)])
            outs[k][ROWS:] = split(n[r])
        both[ROWS:] = x[...]

    return call(
        kernel,
        (near_rows, far_rows, rows, norms, weights),
        [half(ROWS + EXTRA, BLOCK)] * 4 + [half(2 * ROWS, D)],
        "backward_far",
        MATMUL // 2,
        mib=8,
    )


def backward_near(both, norms, weights):
    def kernel(e, n, w, *outs):
        for k, r in enumerate(NEAR):
            outs[k][:ROWS] = product(e[:ROWS], w[block_rows(r)])
            outs[k][ROWS:] = split(n[r])

    return call(
        kernel,
        (both, norms, weights),
        [half(ROWS + EXTRA, BLOCK)] * 4,
        "backward_near",
        MATMUL // 2,
        mib=8,
    )


def latent_grad(terms, active):
    def kernel(*refs):
        t, (a, out) = refs[:5], refs[5:]
        total = add_extra(t)
        value = add(t) + SCALE * total[:1]
        out[:ROWS] = (value * (2.0 * a[...].astype(f32))).astype(bf16)
        out[ROWS:] = split(total)

    return call(kernel, (*terms, active), half(ROWS + EXTRA, BLOCK), "latent_grad", 1 << 20)


def gradient(lats, dpres, both, norms, weights, blocks, before=()):
    width = 768
    steps = D // width
    count = len(blocks)

    def kernel(*refs):
        early, late, d = refs[0], refs[1], refs[2 : 2 + count]
        e, n, w = refs[2 + count : 5 + count]
        out, bias, totals, *rest = refs[5 + count + len(before) :]
        lhs, buf, sem = rest[-3:]
        if before:
            bias[...] = refs[6 + count][...]
            totals[...] = refs[7 + count][...]
        else:
            rest[0][...] = jnp.sum(e[:ROWS].astype(f32), axis=0, keepdims=True)
        copies = []
        for k, r in enumerate(blocks):
            l = early[r] if r < 4 else late[r - 4]
            x = d[k][:ROWS]
            lhs[:ROWS] = l
            lhs[ROWS:] = x
            usage = jnp.sum(l.astype(f32), axis=0, keepdims=True)
            column = (SCALE * jnp.broadcast_to(usage, (8, BLOCK)) / n[r]).T[:, :1]
            bias[block_of(r)] = jnp.sum(x.astype(f32), axis=0, keepdims=True)
            totals[block_of(r)] = split_sum(d[k][ROWS:])[:1]
            for i in range(steps):
                cols = slice(i * width, (i + 1) * width)
                g = lax.dot_general(lhs[...], e[:, cols], TN, preferred_element_type=f32)
                g = g + column * w[block_rows(r), cols].astype(f32)
                buf[k, :, cols] = g.astype(bf16)
                copy = pltpu.make_async_copy(
                    buf.at[k, :, cols], out.at[block_rows(r), cols], sem.at[k, i]
                )
                copy.start()
                copies.append(copy)
        for copy in copies:
            copy.wait()

    shapes = [half(F, D), full(LAYERS, 1, BLOCK), full(LAYERS, 1, BLOCK)]
    if not before:
        shapes.append(full(1, D))
    return call(
        kernel,
        (*lats, *[dpres[r] for r in blocks], both, norms, weights, *before),
        shapes,
        "gradient",
        2 * MATMUL * count // LAYERS,
        [
            pltpu.VMEM((2 * ROWS, BLOCK), bf16),
            pltpu.VMEM((count, BLOCK, D), bf16),
            pltpu.SemaphoreType.DMA((count, steps)),
        ],
        12,
        [VMEM] * (5 + count) + ([HBM, VMEM, VMEM] if before else []),
        [HBM] + [VMEM] * (len(shapes) - 1),
        {5 + count: 0} if before else None,
    )


def scatter(terms, ring, pair, add):
    far = [ring(terms[4 + d], d) for d in STEPS]
    near = [ring(terms[d], d) for d in STEPS]
    other = pair(add([terms[4]] + far))
    return [terms[0]] + near + [other]


def gather(own, ring, pair):
    blocks = {0: own, 4: pair(own)}
    for r in (0, 4):
        for d in STEPS:
            blocks[r + d] = ring(blocks[r], 4 - d)
    return blocks


def body(acts, decoder, enc_bias, dec_bias):
    inputs, weights = acts[0], decoder[0]
    bias = enc_bias.reshape(LAYERS, 1, BLOCK)

    *far, rows = encode_far(inputs, weights)
    terms = list(encode_near(rows, weights)) + far
    norms, piece = prepare(rows, weights)
    mine = activate(scatter(terms, move_z, move_y, add_z), bias)
    active = gather(mine, move_z, move_y)
    lat_near, before = decode([active[r] for r in NEAR], weights, NEAR, after=(piece,))
    lat_far, here, there = decode([active[r] for r in FAR], weights, FAR, before)

    pieces = add_core(here, move_core(there))
    own = error(scatter(pieces, move_x, move_lo, add_x), dec_bias, piece)
    got = gather(own, move_x, move_lo)
    here = join([got[r] for r in range(CHIPS)])

    *far, both = backward_far(here, move_core(here), rows, norms, weights)
    terms = list(backward_near(both, norms, weights)) + far
    dpre = latent_grad(scatter(terms, move_z, move_y, add_z), mine)
    dpres = gather(dpre, move_z, move_y)
    out = ()
    for blocks in GROUPS:
        got = gradient((lat_near, lat_far), dpres, both, norms, weights, blocks, out)
        if not out:
            dec_grad = got[3]
        out = tuple(got[:3])
    grad, enc_grad, total = out
    return grad[None], enc_grad.reshape(F), dec_grad, total.reshape(F)


def solution(mesh):
    placed = (P("layer", None, None), P("layer", "latent", None), P("latent"), P("layer", None))
    return jax.shard_map(
        body,
        mesh=mesh,
        in_specs=placed,
        out_specs=(P("layer", "latent", None), P("latent"), P("layer", None), P("latent")),
        check_vma=False,
    )
```

time: 369 us -> 151 us (0.41)
  waiting for transfers between devices: 268 us -> 45.2 us
  starting transfers between devices: 0.12 us -> 70.1 us
  matrix products: 53.9 us -> 0 us
  Pallas kernels: 0 us -> 28.9 us
  blocking collectives: 21.7 us -> 0 us
  between operations: 13.8 us -> 1.03 us
  other arithmetic: 11.5 us -> 0 us
  local copies, waits for them, and re-layouts: 0.63 us -> 5.16 us
    psum x3 -> x0, waiting for transfers between devices: 268 us -> none  [the longest x1 93 us: body(): lax.psum(part.astype(jnp.bfloat16), 'layer').astype(jnp.float32)]
    ppermute x0 -> x44, starting transfers between devices: none -> 70.1 us  [the longest x24 36.2 us: move_z(): return lax.ppermute(x, 'layer', [(i, i & 4 | i + dz & 3) for i in range(8)])]
    dot_general x5 -> x0, matrix products: 53.9 us -> none  [the longest x1 15.2 us: body(): lax.dot_general(dpre_bf, inputs, contract_first, preferred_element_type=j...]
    ppermute x0 -> x44, waiting for transfers between devices: none -> 45.2 us  [the longest x24 25.1 us: move_z(): return lax.ppermute(x, 'layer', [(i, i & 4 | i + dz & 3) for i in range(8)])]
    pallas_call x0 -> x18, Pallas kernels: none -> 28.9 us  [call(): pl.pallas_call(kernel, in_specs=places or [VMEM] * len(operands), out_spe...]
    psum x1 -> x0, blocking collectives: 21.7 us -> none  [body(): total_norm = lax.psum(norms, 'layer')]
    reduce_sum x2 -> x0, other arithmetic: 5.87 us -> none  [the longest x1 3.05 us: body(): grad_enc_bias = jnp.sum(dpre, axis=0)]
    dot_general x1 -> x0, other arithmetic: 5.58 us -> none  [body(): jnp.einsum('fd,fd->f', weights, weights, preferred_element_type=jnp.float32)]
  transfers between devices with their start and end apart: 3 -> 44, of which waited for: 3 -> 28; matrix products, arithmetic and copies ran while one was open for 4% -> 0% of each run, Pallas kernels for 0% -> 11%
where the time goes in v3:
time: 151 us; the launch traced here: 150 us
  starting transfers between devices  70.1 us (46%)
  waiting for transfers between devices  45.2 us (30%)
  Pallas kernels  28.9 us (19%)
  local copies, waits for them, and re-layouts  5.16 us (3%)
    ppermute x24, starting transfers between devices, move_z(): return lax.ppermute(x, 'layer', [(i, i & 4 | i + dz & 3) for i in range(8)])  36.2 us
    pallas_call x18, Pallas kernels, call(): pl.pallas_call(kernel, in_specs=places or [VMEM] * len(operands), out_spe...  28.9 us
    ppermute x24, waiting for transfers between devices, move_z(): return lax.ppermute(x, 'layer', [(i, i & 4 | i + dz & 3) for i in range(8)])  25.1 us
    ppermute x12, starting transfers between devices, move_x(): lax.ppermute(x, 'latent', [(i, i & 9 | i + 2 * dx & 6) for i in range(16)])  20.4 us
    ppermute x4, starting transfers between devices, move_y(): return lax.ppermute(x, 'layer', [(i, i ^ 4) for i in range(8)])  11.5 us
    ppermute x12, waiting for transfers between devices, move_x(): lax.ppermute(x, 'latent', [(i, i & 9 | i + 2 * dx & 6) for i in range(16)])  9.11 us
    unnamed x10, local copies, waits for them, and re-layouts  5.16 us
    ppermute x2, waiting for transfers between devices, move_core(): return lax.ppermute(x, 'latent', [(i, i ^ 1) for i in range(16)])  4.83 us
  transfers between devices with their start and end apart: 44, of which 28 were waited for; matrix products, arithmetic and copies ran while one was open for 0% of the time, Pallas kernels for 11%

profile of v3, /device:TPU:0, one launch (start us, length us, event | category | flops | bytes accessed | tf_op | source)
XLA Modules:
  0.0 150.3 jit_solution(17468907781416720233)
XLA Ops:
  0.6 3.7 %copy-done = bf16[1,2048,2304]{2,1,0:T(8,128)(2,1)S(1)} copy-done((bf16[1,2048,2304]{2,1,0:T(8,128)(2,1)S(1)}, bf16[1,2048,2304]{2,1,0:T(8,128)(2,1)}, u32[]{:S(2)}) %copy-start) | copy-done | bytes 9437208
  4.3 1.5 copy-done.2
  5.8 2.0 %encode_far.1 = (bf16[384,256]{1,0:T(8,128)(2,1)S(1)}, bf16[384,256]{1,0:T(8,128)(2,1)S(1)}, bf16[384,256]{1,0:T(8,128)(2,1)S(1)}, bf16[384,256]{1,0:T(8,128)(2,1)S(1)}, bf16[384,2304]{1,0:T(8,128)(2,1)S(1)}) custom-call(bf16[384,2304]{1,0:T(8,128)(2,1)S(1)} %bitcast.16, bf16[2048,2304]{1,0:T(8,128)(2,1)S(1)} %bitcast.6), custom_call_target="tpu_custom_call" | custom-call | flops 1811939328 | bytes 4529848 | tf_op jit(solution)/shard_map/encode_far/pallas_call | solution.py:46
  7.8 4.0 %collective-permute-start.3 = (bf16[384,256]{1,0:T(8,128)(2,1)S(1)}, bf16[384,256]{1,0:T(8,128)(2,1)S(1)}, u32[]{:S(2)}, u32[]{:S(2)}) collective-permute-start(bf16[384,256]{1,0:T(8,128)(2,1)S(1)} %get-tuple-element.53), channel_id=1, source_target_pairs={{0,32},{16,48},{32,0},{48,16},{64,96},{80,112},{96,64},{112,80},{1... | collective-permute-start | bytes 589832 | tf_op jit(solution)/shard_map/ppermute | solution.py:64
  12.9 2.2 %collective-permute-start.5 = (bf16[384,256]{1,0:T(8,128)(2,1)S(1)}, bf16[384,256]{1,0:T(8,128)(2,1)S(1)}, u32[]{:S(2)}, u32[]{:S(2)}) collective-permute-start(bf16[384,256]{1,0:T(8,128)(2,1)S(1)} %get-tuple-element.55), channel_id=1, source_target_pairs={{0,48},{16,0},{32,16},{48,32},{64,112},{80,64},{96,80},{112,96},{1... | collective-permute-start | bytes 589832 | tf_op jit(solution)/shard_map/ppermute | solution.py:64
  15.1 2.0 %encode_near.1 = (bf16[384,256]{1,0:T(8,128)(2,1)S(1)}, bf16[384,256]{1,0:T(8,128)(2,1)S(1)}, bf16[384,256]{1,0:T(8,128)(2,1)S(1)}, bf16[384,256]{1,0:T(8,128)(2,1)S(1)}) custom-call(bf16[384,2304]{1,0:T(8,128)(2,1)S(1)} %get-tuple-element.47.a.x, bf16[2048,2304]{1,0:T(8,128)(2,1)S(1)} %bitcast.7), custom_call_target="tpu_custom_call" | custom-call | flops 1811939328 | bytes 4529848 | tf_op jit(solution)/shard_map/encode_near/pallas_call | solution.py:46
  18.1 3.3 %collective-permute-start.2 = (bf16[384,256]{1,0:T(8,128)(2,1)S(1)}, bf16[384,256]{1,0:T(8,128)(2,1)S(1)}, u32[]{:S(2)}, u32[]{:S(2)}) collective-permute-start(bf16[384,256]{1,0:T(8,128)(2,1)S(1)} %get-tuple-element.51), channel_id=1, source_target_pairs={{0,48},{16,0},{32,16},{48,32},{64,112},{80,64},{96,80},{112,96},{1... | collective-permute-start | bytes 589832 | tf_op jit(solution)/shard_map/ppermute | solution.py:64
  21.3 3.3 %collective-permute-done.4.refs_2_ = bf16[384,256]{1,0:T(8,128)(2,1)S(1)} collective-permute-done((bf16[384,256]{1,0:T(8,128)(2,1)S(1)}, bf16[384,256]{1,0:T(8,128)(2,1)S(1)}, u32[]{:S(2)}, u32[]{:S(2)}) %collective-permute-start.4) | collective-permute-done | bytes 196640 | tf_op jit(solution)/shard_map/ppermute | solution.py:64
  24.7 3.3 %collective-permute-start.6 = (bf16[384,256]{1,0:T(8,128)(2,1)S(1)}, bf16[384,256]{1,0:T(8,128)(2,1)S(1)}, u32[]{:S(2)}, u32[]{:S(2)}) collective-permute-start(bf16[384,256]{1,0:T(8,128)(2,1)S(1)} %add_z.2), channel_id=1, source_target_pairs={{0,64},{16,80},{32,96},{48,112},{64,0},{80,16},{96,32},{112,48},{1... | collective-permute-start | bytes 589832 | tf_op jit(solution)/shard_map/ppermute | solution.py:60
  28.0 1.4 collective-permute-done.1.refs_2_
  30.2 1.8 %collective-permute-done.6.refs_4_ = bf16[384,256]{1,0:T(8,128)(2,1)S(1)} collective-permute-done((bf16[384,256]{1,0:T(8,128)(2,1)S(1)}, bf16[384,256]{1,0:T(8,128)(2,1)S(1)}, u32[]{:S(2)}, u32[]{:S(2)}) %collective-permute-start.6) | collective-permute-done | bytes 196640 | tf_op jit(solution)/shard_map/ppermute | solution.py:60
  32.1 3.3 %collective-permute-start.10 = (bf16[384,256]{1,0:T(8,128)(2,1)S(1)}, bf16[384,256]{1,0:T(8,128)(2,1)S(1)}, u32[]{:S(2)}, u32[]{:S(2)}) collective-permute-start(bf16[384,256]{1,0:T(8,128)(2,1)S(1)} %activate.1.refs_0_.refs_5_), channel_id=1, source_target_pairs={{0,64},{16,80},{32,96},{48,112},{64,0},{80,16},{96,32},{112,48},{1... | collective-permute-start | bytes 589832 | tf_op jit(solution)/shard_map/ppermute | solution.py:60
  35.4 3.8 %collective-permute-start.7 = (bf16[384,256]{1,0:T(8,128)(2,1)S(1)}, bf16[384,256]{1,0:T(8,128)(2,1)S(1)}, u32[]{:S(2)}, u32[]{:S(2)}) collective-permute-start(bf16[384,256]{1,0:T(8,128)(2,1)S(1)} %activate.1.refs_0_.refs_5_), channel_id=1, source_target_pairs={{0,48},{16,0},{32,16},{48,32},{64,112},{80,64},{96,80},{112,96},{1... | collective-permute-start | bytes 589832 | tf_op jit(solution)/shard_map/ppermute | solution.py:64
  40.0 3.1 %collective-permute-start.11 = (bf16[384,256]{1,0:T(8,128)(2,1)S(1)}, bf16[384,256]{1,0:T(8,128)(2,1)S(1)}, u32[]{:S(2)}, u32[]{:S(2)}) collective-permute-start(bf16[384,256]{1,0:T(8,128)(2,1)S(1)} %collective-permute-done.10.refs_0_), channel_id=1, source_target_pairs={{0,48},{16,0},{32,16},{48,32},{64,112},{80,64},{96,80},{112,96},{1... | collective-permute-start | bytes 589832 | tf_op jit(solution)/shard_map/ppermute | solution.py:64
  43.1 1.6 %collective-permute-start.12 = (bf16[384,256]{1,0:T(8,128)(2,1)S(1)}, bf16[384,256]{1,0:T(8,128)(2,1)S(1)}, u32[]{:S(2)}, u32[]{:S(2)}) collective-permute-start(bf16[384,256]{1,0:T(8,128)(2,1)S(1)} %collective-permute-done.10.refs_0_), channel_id=1, source_target_pairs={{0,32},{16,48},{32,0},{48,16},{64,96},{80,112},{96,64},{112,80},{1... | collective-permute-start | bytes 589832 | tf_op jit(solution)/shard_map/ppermute | solution.py:64
  44.7 3.6 %collective-permute-done.7.refs_1_ = bf16[384,256]{1,0:T(8,128)(2,1)S(1)} collective-permute-done((bf16[384,256]{1,0:T(8,128)(2,1)S(1)}, bf16[384,256]{1,0:T(8,128)(2,1)S(1)}, u32[]{:S(2)}, u32[]{:S(2)}) %collective-permute-start.7) | collective-permute-done | bytes 196640 | tf_op jit(solution)/shard_map/ppermute | solution.py:64
  48.3 2.5 %prepare.1 = (f32[8,8,256]{2,1,0:T(8,128)S(1)}, bf16[24,2304]{1,0:T(8,128)(2,1)S(1)}) custom-call(bf16[384,2304]{1,0:T(8,128)(2,1)S(1)} %get-tuple-element.47.a.x, bf16[2048,2304]{1,0:T(8,128)(2,1)S(1)} %bitcast.8), custom_call_target="tpu_custom_call" | custom-call | flops 1073741824 | bytes 2684354 | tf_op jit(solution)/shard_map/prepare/pallas_call | solution.py:46
  52.0 2.0 %decode.2 = (bf16[4,384,256]{2,1,0:T(8,128)(2,1)S(1)}, f32[384,2304]{1,0:T(8,128)S(1)}) custom-call(bf16[384,256]{1,0:T(8,128)(2,1)S(1)} %activate.1.refs_0_.refs_5_, bf16[384,256]{1,0:T(8,128)(2,1)S(1)} %collective-permute-done.7.refs_1_, bf16[384,256]{1,0:T(8,128)(2,1)S(1)} %collective-permute-done.8.refs_2_, ...), custom_call_target="tpu_custom_call" | custom-call | flops 1811939328 | bytes 4529848 | tf_op jit(solution)/shard_map/decode/pallas_call | solution.py:46
  54.3 2.0 %collective-permute-done.13.refs_3_ = bf16[384,256]{1,0:T(8,128)(2,1)S(1)} collective-permute-done((bf16[384,256]{1,0:T(8,128)(2,1)S(1)}, bf16[384,256]{1,0:T(8,128)(2,1)S(1)}, u32[]{:S(2)}, u32[]{:S(2)}) %collective-permute-start.13) | collective-permute-done | bytes 196640 | tf_op jit(solution)/shard_map/ppermute | solution.py:64
  56.3 2.0 %decode.3 = (bf16[4,384,256]{2,1,0:T(8,128)(2,1)S(1)}, bf16[192,2304]{1,0:T(8,128)(2,1)S(1)}, bf16[192,2304]{1,0:T(8,128)(2,1)S(1)}) custom-call(bf16[384,256]{1,0:T(8,128)(2,1)S(1)} %collective-permute-done.10.refs_0_, bf16[384,256]{1,0:T(8,128)(2,1)S(1)} %collective-permute-done.11.refs_1_, bf16[384,256]{1,0:T(8,128)(2,1)S(1)} %collective-permute-done.12.refs_2_, ...), custom_call_target="tpu_custom_call" | custom-call | flops 1811939328 | bytes 4529848 | tf_op jit(solution)/shard_map/decode/pallas_call | solution.py:46
  58.5 2.4 %collective-permute-done.14.b = bf16[192,2304]{1,0:T(8,128)(2,1)S(1)} collective-permute-done((bf16[192,2304]{1,0:T(8,128)(2,1)S(1)}, bf16[192,2304]{1,0:T(8,128)(2,1)S(1)}, u32[]{:S(2)}, u32[]{:S(2)}) %collective-permute-start.14) | collective-permute-done | bytes 884768 | tf_op jit(solution)/shard_map/ppermute | solution.py:68
  61.1 3.1 %collective-permute-start.18 = (bf16[24,2304]{1,0:T(8,128)(2,1)S(1)}, bf16[24,2304]{1,0:T(8,128)(2,1)S(1)}, u32[]{:S(2)}, u32[]{:S(2)}) collective-permute-start(bf16[24,2304]{1,0:T(8,128)(2,1)S(1)} %get-tuple-element.67), channel_id=1, source_target_pairs={{0,4},{1,5},{2,6},{3,7},{4,0},{5,1},{6,2},{7,3},{8,12},{9,13},{10,... | collective-permute-start | bytes 331784 | tf_op jit(solution)/shard_map/ppermute | solution.py:76
  64.8 2.7 %collective-permute-start.20 = (bf16[24,2304]{1,0:T(8,128)(2,1)S(1)}, bf16[24,2304]{1,0:T(8,128)(2,1)S(1)}, u32[]{:S(2)}, u32[]{:S(2)}) collective-permute-start(bf16[24,2304]{1,0:T(8,128)(2,1)S(1)} %get-tuple-element.69), channel_id=1, source_target_pairs={{0,6},{1,7},{2,0},{3,1},{4,2},{5,3},{6,4},{7,5},{8,14},{9,15},{10,... | collective-permute-start | bytes 331784 | tf_op jit(solution)/shard_map/ppermute | solution.py:76
  68.4 3.0 %collective-permute-start.17 = (bf16[24,2304]{1,0:T(8,128)(2,1)S(1)}, bf16[24,2304]{1,0:T(8,128)(2,1)S(1)}, u32[]{:S(2)}, u32[]{:S(2)}) collective-permute-start(bf16[24,2304]{1,0:T(8,128)(2,1)S(1)} %get-tuple-element.65), channel_id=1, source_target_pairs={{0,6},{1,7},{2,0},{3,1},{4,2},{5,3},{6,4},{7,5},{8,14},{9,15},{10,... | collective-permute-start | bytes 331784 | tf_op jit(solution)/shard_map/ppermute | solution.py:76
  75.4 2.0 %collective-permute-done.21.refs_4_ = bf16[24,2304]{1,0:T(8,128)(2,1)S(1)} collective-permute-done((bf16[24,2304]{1,0:T(8,128)(2,1)S(1)}, bf16[24,2304]{1,0:T(8,128)(2,1)S(1)}, u32[]{:S(2)}, u32[]{:S(2)}) %collective-permute-start.21) | collective-permute-done | bytes 110624 | tf_op jit(solution)/shard_map/ppermute | solution.py:72
  78.2 4.6 %collective-permute-start.22 = (bf16[24,2304]{1,0:T(8,128)(2,1)S(1)}, bf16[24,2304]{1,0:T(8,128)(2,1)S(1)}, u32[]{:S(2)}, u32[]{:S(2)}) collective-permute-start(bf16[24,2304]{1,0:T(8,128)(2,1)S(1)} %error.1.refs_0_), channel_id=1, source_target_pairs={{0,6},{1,7},{2,0},{3,1},{4,2},{5,3},{6,4},{7,5},{8,14},{9,15},{10,... | collective-permute-start | bytes 331784 | tf_op jit(solution)/shard_map/ppermute | solution.py:76
  83.7 3.2 %collective-permute-start.26 = (bf16[24,2304]{1,0:T(8,128)(2,1)S(1)}, bf16[24,2304]{1,0:T(8,128)(2,1)S(1)}, u32[]{:S(2)}, u32[]{:S(2)}) collective-permute-start(bf16[24,2304]{1,0:T(8,128)(2,1)S(1)} %collective-permute-done.25.refs_4_), channel_id=1, source_target_pairs={{0,6},{1,7},{2,0},{3,1},{4,2},{5,3},{6,4},{7,5},{8,14},{9,15},{10,... | collective-permute-start | bytes 331784 | tf_op jit(solution)/shard_map/ppermute | solution.py:76
  86.9 1.5 collective-permute-start.27
  90.9 2.3 %collective-permute-done.27.refs_6_ = bf16[24,2304]{1,0:T(8,128)(2,1)S(1)} collective-permute-done((bf16[24,2304]{1,0:T(8,128)(2,1)S(1)}, bf16[24,2304]{1,0:T(8,128)(2,1)S(1)}, u32[]{:S(2)}, u32[]{:S(2)}) %collective-permute-start.27) | collective-permute-done | bytes 110624 | tf_op jit(solution)/shard_map/ppermute | solution.py:76
  94.9 2.4 %collective-permute-done.29.b = bf16[192,2304]{1,0:T(8,128)(2,1)S(1)} collective-permute-done((bf16[192,2304]{1,0:T(8,128)(2,1)S(1)}, bf16[192,2304]{1,0:T(8,128)(2,1)S(1)}, u32[]{:S(2)}, u32[]{:S(2)}) %collective-permute-start.29) | collective-permute-done | bytes 884768 | tf_op jit(solution)/shard_map/ppermute | solution.py:68
  97.3 2.1 %backward_far.1 = (bf16[400,256]{1,0:T(8,128)(2,1)S(1)}, bf16[400,256]{1,0:T(8,128)(2,1)S(1)}, bf16[400,256]{1,0:T(8,128)(2,1)S(1)}, bf16[400,256]{1,0:T(8,128)(2,1)S(1)}, bf16[768,2304]{1,0:T(8,128)(2,1)S(1)}) custom-call(bf16[192,2304]{1,0:T(8,128)(2,1)S(1)} %join.1.a, bf16[192,2304]{1,0:T(8,128)(2,1)S(1)} %collective-permute-done.29.b, ...), custom_call_target="tpu_custom_call" | custom-call | flops 1811939328 | bytes 4529848 | tf_op jit(solution)/shard_map/backward_far/pallas_call | solution.py:46
  99.4 1.9 %collective-permute-start.33 = (bf16[400,256]{1,0:T(8,128)(2,1)S(1)}, bf16[400,256]{1,0:T(8,128)(2,1)S(1)}, u32[]{:S(2)}, u32[]{:S(2)}) collective-permute-start(bf16[400,256]{1,0:T(8,128)(2,1)S(1)} %get-tuple-element.77), channel_id=1, source_target_pairs={{0,32},{16,48},{32,0},{48,16},{64,96},{80,112},{96,64},{112,80},{1... | collective-permute-start | bytes 614408 | tf_op jit(solution)/shard_map/ppermute | solution.py:64
  101.7 2.8 %collective-permute-start.35 = (bf16[400,256]{1,0:T(8,128)(2,1)S(1)}, bf16[400,256]{1,0:T(8,128)(2,1)S(1)}, u32[]{:S(2)}, u32[]{:S(2)}) collective-permute-start(bf16[400,256]{1,0:T(8,128)(2,1)S(1)} %get-tuple-element.79), channel_id=1, source_target_pairs={{0,48},{16,0},{32,16},{48,32},{64,112},{80,64},{96,80},{112,96},{1... | collective-permute-start | bytes 614408 | tf_op jit(solution)/shard_map/ppermute | solution.py:64
  104.5 2.0 %backward_near.1 = (bf16[400,256]{1,0:T(8,128)(2,1)S(1)}, bf16[400,256]{1,0:T(8,128)(2,1)S(1)}, bf16[400,256]{1,0:T(8,128)(2,1)S(1)}, bf16[400,256]{1,0:T(8,128)(2,1)S(1)}) custom-call(bf16[768,2304]{1,0:T(8,128)(2,1)S(1)} %get-tuple-element.71.e.refs_4_.refs_5_, f32[8,8,256]{2,1,0:T(8,128)S(1)} %get-tuple-element.70.n.refs_5_.refs_6_, ...), custom_call_target="tpu_custom_call" | custom-call | flops 1811939328 | bytes 4529848 | tf_op jit(solution)/shard_map/backward_near/pallas_call | solution.py:46
  107.5 1.4 collective-permute-done.33.refs_1_
  109.0 1.4 collective-permute-start.32
  110.4 3.0 %collective-permute-done.34.refs_2_ = bf16[400,256]{1,0:T(8,128)(2,1)S(1)} collective-permute-done((bf16[400,256]{1,0:T(8,128)(2,1)S(1)}, bf16[400,256]{1,0:T(8,128)(2,1)S(1)}, u32[]{:S(2)}, u32[]{:S(2)}) %collective-permute-start.34) | collective-permute-done | bytes 204832 | tf_op jit(solution)/shard_map/ppermute | solution.py:64
  113.5 2.5 %collective-permute-start.36 = (bf16[400,256]{1,0:T(8,128)(2,1)S(1)}, bf16[400,256]{1,0:T(8,128)(2,1)S(1)}, u32[]{:S(2)}, u32[]{:S(2)}) collective-permute-start(bf16[400,256]{1,0:T(8,128)(2,1)S(1)} %add_z.3), channel_id=1, source_target_pairs={{0,64},{16,80},{32,96},{48,112},{64,0},{80,16},{96,32},{112,48},{1... | collective-permute-start | bytes 614408 | tf_op jit(solution)/shard_map/ppermute | solution.py:60
  116.0 1.8 %collective-permute-done.30.refs_1_ = bf16[400,256]{1,0:T(8,128)(2,1)S(1)} collective-permute-done((bf16[400,256]{1,0:T(8,128)(2,1)S(1)}, bf16[400,256]{1,0:T(8,128)(2,1)S(1)}, u32[]{:S(2)}, u32[]{:S(2)}) %collective-permute-start.30) | collective-permute-done | bytes 204832 | tf_op jit(solution)/shard_map/ppermute | solution.py:64
  117.8 3.5 %collective-permute-done.31.refs_2_ = bf16[400,256]{1,0:T(8,128)(2,1)S(1)} collective-permute-done((bf16[400,256]{1,0:T(8,128)(2,1)S(1)}, bf16[400,256]{1,0:T(8,128)(2,1)S(1)}, u32[]{:S(2)}, u32[]{:S(2)}) %collective-permute-start.31) | collective-permute-done | bytes 204832 | tf_op jit(solution)/shard_map/ppermute | solution.py:64
  122.0 2.5 %collective-permute-start.37 = (bf16[400,256]{1,0:T(8,128)(2,1)S(1)}, bf16[400,256]{1,0:T(8,128)(2,1)S(1)}, u32[]{:S(2)}, u32[]{:S(2)}) collective-permute-start(bf16[400,256]{1,0:T(8,128)(2,1)S(1)} %latent_grad.1.refs_2_), channel_id=1, source_target_pairs={{0,64},{16,80},{32,96},{48,112},{64,0},{80,16},{96,32},{112,48},{1... | collective-permute-start | bytes 614408 | tf_op jit(solution)/shard_map/ppermute | solution.py:60
  125.6 2.6 %collective-permute-start.42 = (bf16[400,256]{1,0:T(8,128)(2,1)S(1)}, bf16[400,256]{1,0:T(8,128)(2,1)S(1)}, u32[]{:S(2)}, u32[]{:S(2)}) collective-permute-start(bf16[400,256]{1,0:T(8,128)(2,1)S(1)} %latent_grad.1.refs_2_), channel_id=1, source_target_pairs={{0,48},{16,0},{32,16},{48,32},{64,112},{80,64},{96,80},{112,96},{1... | collective-permute-start | bytes 614408 | tf_op jit(solution)/shard_map/ppermute | solution.py:64
  128.3 1.8 %collective-permute-done.37.refs_3_ = bf16[400,256]{1,0:T(8,128)(2,1)S(1)} collective-permute-done((bf16[400,256]{1,0:T(8,128)(2,1)S(1)}, bf16[400,256]{1,0:T(8,128)(2,1)S(1)}, u32[]{:S(2)}, u32[]{:S(2)}) %collective-permute-start.37) | collective-permute-done | bytes 204832 | tf_op jit(solution)/shard_map/ppermute | solution.py:60
  130.1 1.7 %collective-permute-start.38 = (bf16[400,256]{1,0:T(8,128)(2,1)S(1)}, bf16[400,256]{1,0:T(8,128)(2,1)S(1)}, u32[]{:S(2)}, u32[]{:S(2)}) collective-permute-start(bf16[400,256]{1,0:T(8,128)(2,1)S(1)} %collective-permute-done.37.refs_3_), channel_id=1, source_target_pairs={{0,32},{16,48},{32,0},{48,16},{64,96},{80,112},{96,64},{112,80},{1... | collective-permute-start | bytes 614408 | tf_op jit(solution)/shard_map/ppermute | solution.py:64
  133.0 4.0 %gradient.3 = (bf16[2048,2304]{1,0:T(8,128)(2,1)}, f32[8,1,256]{2,1,0:T(1,128)S(1)}, f32[8,1,256]{2,1,0:T(1,128)S(1)}, f32[1,2304]{1,0:T(1,128)}) custom-call(bf16[4,384,256]{2,1,0:T(8,128)(2,1)S(1)} %get-tuple-element.57.refs_0_, bf16[4,384,256]{2,1,0:T(8,128)(2,1)S(1)} %get-tuple-element.59.refs_1_, bf16[400,256]{1,0:T(8,128)(2,1)S(1)} %latent_grad.1.refs_2_, ...), custom_call_target="tpu_custom_call" | custom-call | flops 1811939328 | bytes 4529848 | tf_op jit(solution)/shard_map/gradient/pallas_call | solution.py:46
  138.4 4.2 %gradient.4 = (bf16[2048,2304]{1,0:T(8,128)(2,1)}, f32[8,1,256]{2,1,0:T(1,128)S(1)}, f32[8,1,256]{2,1,0:T(1,128)S(1)}) custom-call(bf16[4,384,256]{2,1,0:T(8,128)(2,1)S(1)} %get-tuple-element.57.refs_0_, bf16[4,384,256]{2,1,0:T(8,128)(2,1)S(1)} %get-tuple-element.59.refs_1_, ...), custom_call_target="tpu_custom_call", output_to_operand_aliasing={{0}: (8, {})} | custom-call | flops 2717908992 | bytes 6794772 | tf_op jit(solution)/shard_map/gradient/pallas_call | solution.py:46
  143.2 2.2 %collective-permute-done.40.refs_4_ = bf16[400,256]{1,0:T(8,128)(2,1)S(1)} collective-permute-done((bf16[400,256]{1,0:T(8,128)(2,1)S(1)}, bf16[400,256]{1,0:T(8,128)(2,1)S(1)}, u32[]{:S(2)}, u32[]{:S(2)}) %collective-permute-start.40) | collective-permute-done | bytes 204832 | tf_op jit(solution)/shard_map/ppermute | solution.py:64
  145.3 4.8 %gradient.5 = (bf16[2048,2304]{1,0:T(8,128)(2,1)}, f32[8,1,256]{2,1,0:T(1,128)}, f32[8,1,256]{2,1,0:T(1,128)}) custom-call(bf16[4,384,256]{2,1,0:T(8,128)(2,1)S(1)} %get-tuple-element.57.refs_0_, bf16[4,384,256]{2,1,0:T(8,128)(2,1)S(1)} %get-tuple-element.59.refs_1_, ...), custom_call_target="tpu_custom_call", output_to_operand_aliasing={{0}: (8, {})} | custom-call | flops 2717908992 | bytes 6794772 | tf_op jit(solution)/shard_map/gradient/pallas_call | solution.py:46
  (68 shorter events, 23.5 us)
Async XLA Ops:
  0.6 3.7 %copy-start = (bf16[1,2048,2304]{2,1,0:T(8,128)(2,1)S(1)}, bf16[1,2048,2304]{2,1,0:T(8,128)(2,1)}, u32[]{:S(2)}) copy-start(bf16[1,2048,2304]{2,1,0:T(8,128)(2,1)} %param.5) | copy-start | bytes 28311556
  5.8 9.3 %copy-start.1 = (bf16[1,2048,2304]{2,1,0:T(8,128)(2,1)S(1)}, bf16[1,2048,2304]{2,1,0:T(8,128)(2,1)}, u32[]{:S(2)}) copy-start(bf16[1,2048,2304]{2,1,0:T(8,128)(2,1)} %param.5) | copy-start | bytes 28311556
  5.8 26.2 %copy-start.4 = (f32[2048]{0:T(1024)S(1)}, f32[2048]{0:T(1024)}, u32[]{:S(2)}) copy-start(f32[2048]{0:T(1024)} %param.6) | copy-start | bytes 24580
  7.8 10.2 %collective-permute-start.3 = (bf16[384,256]{1,0:T(8,128)(2,1)S(1)}, bf16[384,256]{1,0:T(8,128)(2,1)S(1)}, u32[]{:S(2)}, u32[]{:S(2)}) collective-permute-start(bf16[384,256]{1,0:T(8,128)(2,1)S(1)} %get-tuple-element.53), channel_id=1, source_target_pairs={{0,32},{16,48},{32,0},{48,16},{64,96},{80,112},{96,64},{112,80},{1... | collective-permute-start | bytes 589832 | tf_op jit(solution)/shard_map/ppermute | solution.py:64
  11.9 12.7 %collective-permute-start.4 = (bf16[384,256]{1,0:T(8,128)(2,1)S(1)}, bf16[384,256]{1,0:T(8,128)(2,1)S(1)}, u32[]{:S(2)}, u32[]{:S(2)}) collective-permute-start(bf16[384,256]{1,0:T(8,128)(2,1)S(1)} %get-tuple-element.54), channel_id=1, source_target_pairs={{0,16},{16,32},{32,48},{48,0},{64,80},{80,96},{96,112},{112,64},{1... | collective-permute-start | bytes 589832 | tf_op jit(solution)/shard_map/ppermute | solution.py:64
  12.9 11.7 %collective-permute-start.5 = (bf16[384,256]{1,0:T(8,128)(2,1)S(1)}, bf16[384,256]{1,0:T(8,128)(2,1)S(1)}, u32[]{:S(2)}, u32[]{:S(2)}) collective-permute-start(bf16[384,256]{1,0:T(8,128)(2,1)S(1)} %get-tuple-element.55), channel_id=1, source_target_pairs={{0,48},{16,0},{32,16},{48,32},{64,112},{80,64},{96,80},{112,96},{1... | collective-permute-start | bytes 589832 | tf_op jit(solution)/shard_map/ppermute | solution.py:64
  17.1 10.8 %collective-permute-start = (bf16[384,256]{1,0:T(8,128)(2,1)S(1)}, bf16[384,256]{1,0:T(8,128)(2,1)S(1)}, u32[]{:S(2)}, u32[]{:S(2)}) collective-permute-start(bf16[384,256]{1,0:T(8,128)(2,1)S(1)} %get-tuple-element.49), channel_id=1, source_target_pairs={{0,32},{16,48},{32,0},{48,16},{64,96},{80,112},{96,64},{112,80},{1... | collective-permute-start | bytes 589832 | tf_op jit(solution)/shard_map/ppermute | solution.py:64
  17.2 12.2 %collective-permute-start.1 = (bf16[384,256]{1,0:T(8,128)(2,1)S(1)}, bf16[384,256]{1,0:T(8,128)(2,1)S(1)}, u32[]{:S(2)}, u32[]{:S(2)}) collective-permute-start(bf16[384,256]{1,0:T(8,128)(2,1)S(1)} %get-tuple-element.50), channel_id=1, source_target_pairs={{0,16},{16,32},{32,48},{48,0},{64,80},{80,96},{96,112},{112,64},{1... | collective-permute-start | bytes 589832 | tf_op jit(solution)/shard_map/ppermute | solution.py:64
  18.1 12.1 %collective-permute-start.2 = (bf16[384,256]{1,0:T(8,128)(2,1)S(1)}, bf16[384,256]{1,0:T(8,128)(2,1)S(1)}, u32[]{:S(2)}, u32[]{:S(2)}) collective-permute-start(bf16[384,256]{1,0:T(8,128)(2,1)S(1)} %get-tuple-element.51), channel_id=1, source_target_pairs={{0,48},{16,0},{32,16},{48,32},{64,112},{80,64},{96,80},{112,96},{1... | collective-permute-start | bytes 589832 | tf_op jit(solution)/shard_map/ppermute | solution.py:64
  24.7 7.3 %collective-permute-start.6 = (bf16[384,256]{1,0:T(8,128)(2,1)S(1)}, bf16[384,256]{1,0:T(8,128)(2,1)S(1)}, u32[]{:S(2)}, u32[]{:S(2)}) collective-permute-start(bf16[384,256]{1,0:T(8,128)(2,1)S(1)} %add_z.2), channel_id=1, source_target_pairs={{0,64},{16,80},{32,96},{48,112},{64,0},{80,16},{96,32},{112,48},{1... | collective-permute-start | bytes 589832 | tf_op jit(solution)/shard_map/ppermute | solution.py:60
  32.1 7.9 %collective-permute-start.10 = (bf16[384,256]{1,0:T(8,128)(2,1)S(1)}, bf16[384,256]{1,0:T(8,128)(2,1)S(1)}, u32[]{:S(2)}, u32[]{:S(2)}) collective-permute-start(bf16[384,256]{1,0:T(8,128)(2,1)S(1)} %activate.1.refs_0_.refs_5_), channel_id=1, source_target_pairs={{0,64},{16,80},{32,96},{48,112},{64,0},{80,16},{96,32},{112,48},{1... | collective-permute-start | bytes 589832 | tf_op jit(solution)/shard_map/ppermute | solution.py:60
  35.4 13.0 %collective-permute-start.7 = (bf16[384,256]{1,0:T(8,128)(2,1)S(1)}, bf16[384,256]{1,0:T(8,128)(2,1)S(1)}, u32[]{:S(2)}, u32[]{:S(2)}) collective-permute-start(bf16[384,256]{1,0:T(8,128)(2,1)S(1)} %activate.1.refs_0_.refs_5_), channel_id=1, source_target_pairs={{0,48},{16,0},{32,16},{48,32},{64,112},{80,64},{96,80},{112,96},{1... | collective-permute-start | bytes 589832 | tf_op jit(solution)/shard_map/ppermute | solution.py:64
  39.2 11.7 %collective-permute-start.8 = (bf16[384,256]{1,0:T(8,128)(2,1)S(1)}, bf16[384,256]{1,0:T(8,128)(2,1)S(1)}, u32[]{:S(2)}, u32[]{:S(2)}) collective-permute-start(bf16[384,256]{1,0:T(8,128)(2,1)S(1)} %activate.1.refs_0_.refs_5_), channel_id=1, source_target_pairs={{0,32},{16,48},{32,0},{48,16},{64,96},{80,112},{96,64},{112,80},{1... | collective-permute-start | bytes 589832 | tf_op jit(solution)/shard_map/ppermute | solution.py:64
  39.2 12.9 %collective-permute-start.9 = (bf16[384,256]{1,0:T(8,128)(2,1)S(1)}, bf16[384,256]{1,0:T(8,128)(2,1)S(1)}, u32[]{:S(2)}, u32[]{:S(2)}) collective-permute-start(bf16[384,256]{1,0:T(8,128)(2,1)S(1)} %activate.1.refs_0_.refs_5_), channel_id=1, source_target_pairs={{0,16},{16,32},{32,48},{48,0},{64,80},{80,96},{96,112},{112,64},{1... | collective-permute-start | bytes 589832 | tf_op jit(solution)/shard_map/ppermute | solution.py:64
  40.0 14.1 %collective-permute-start.11 = (bf16[384,256]{1,0:T(8,128)(2,1)S(1)}, bf16[384,256]{1,0:T(8,128)(2,1)S(1)}, u32[]{:S(2)}, u32[]{:S(2)}) collective-permute-start(bf16[384,256]{1,0:T(8,128)(2,1)S(1)} %collective-permute-done.10.refs_0_), channel_id=1, source_target_pairs={{0,48},{16,0},{32,16},{48,32},{64,112},{80,64},{96,80},{112,96},{1... | collective-permute-start | bytes 589832 | tf_op jit(solution)/shard_map/ppermute | solution.py:64
  43.1 11.2 %collective-permute-start.12 = (bf16[384,256]{1,0:T(8,128)(2,1)S(1)}, bf16[384,256]{1,0:T(8,128)(2,1)S(1)}, u32[]{:S(2)}, u32[]{:S(2)}) collective-permute-start(bf16[384,256]{1,0:T(8,128)(2,1)S(1)} %collective-permute-done.10.refs_0_), channel_id=1, source_target_pairs={{0,32},{16,48},{32,0},{48,16},{64,96},{80,112},{96,64},{112,80},{1... | collective-permute-start | bytes 589832 | tf_op jit(solution)/shard_map/ppermute | solution.py:64
  48.3 8.0 %collective-permute-start.13 = (bf16[384,256]{1,0:T(8,128)(2,1)S(1)}, bf16[384,256]{1,0:T(8,128)(2,1)S(1)}, u32[]{:S(2)}, u32[]{:S(2)}) collective-permute-start(bf16[384,256]{1,0:T(8,128)(2,1)S(1)} %collective-permute-done.10.refs_0_), channel_id=1, source_target_pairs={{0,16},{16,32},{32,48},{48,0},{64,80},{80,96},{96,112},{112,64},{1... | collective-permute-start | bytes 589832 | tf_op jit(solution)/shard_map/ppermute | solution.py:64
  54.1 23.3 %copy-start.3 = (f32[1,2304]{1,0:T(1,128)S(1)}, f32[1,2304]{1,0:T(1,128)}, u32[]{:S(2)}) copy-start(f32[1,2304]{1,0:T(1,128)} %refs_5_.1) | copy-start | bytes 27652
  58.4 2.5 %collective-permute-start.14 = (bf16[192,2304]{1,0:T(8,128)(2,1)S(1)}, bf16[192,2304]{1,0:T(8,128)(2,1)S(1)}, u32[]{:S(2)}, u32[]{:S(2)}) collective-permute-start(bf16[192,2304]{1,0:T(8,128)(2,1)S(1)} %get-tuple-element.61), channel_id=1, source_target_pairs={{0,1},{1,0},{2,3},{3,2},{4,5},{5,4},{6,7},{7,6},{8,9},{9,8},{10,11... | collective-permute-start | bytes 2654216 | tf_op jit(solution)/shard_map/ppermute | solution.py:68
  61.1 7.2 %collective-permute-start.18 = (bf16[24,2304]{1,0:T(8,128)(2,1)S(1)}, bf16[24,2304]{1,0:T(8,128)(2,1)S(1)}, u32[]{:S(2)}, u32[]{:S(2)}) collective-permute-start(bf16[24,2304]{1,0:T(8,128)(2,1)S(1)} %get-tuple-element.67), channel_id=1, source_target_pairs={{0,4},{1,5},{2,6},{3,7},{4,0},{5,1},{6,2},{7,3},{8,12},{9,13},{10,... | collective-permute-start | bytes 331784 | tf_op jit(solution)/shard_map/ppermute | solution.py:76
  64.3 7.1 %collective-permute-start.19 = (bf16[24,2304]{1,0:T(8,128)(2,1)S(1)}, bf16[24,2304]{1,0:T(8,128)(2,1)S(1)}, u32[]{:S(2)}, u32[]{:S(2)}) collective-permute-start(bf16[24,2304]{1,0:T(8,128)(2,1)S(1)} %get-tuple-element.68), channel_id=1, source_target_pairs={{0,2},{1,3},{2,4},{3,5},{4,6},{5,7},{6,0},{7,1},{8,10},{9,11},{10,... | collective-permute-start | bytes 331784 | tf_op jit(solution)/shard_map/ppermute | solution.py:76
  64.8 7.6 %collective-permute-start.20 = (bf16[24,2304]{1,0:T(8,128)(2,1)S(1)}, bf16[24,2304]{1,0:T(8,128)(2,1)S(1)}, u32[]{:S(2)}, u32[]{:S(2)}) collective-permute-start(bf16[24,2304]{1,0:T(8,128)(2,1)S(1)} %get-tuple-element.69), channel_id=1, source_target_pairs={{0,6},{1,7},{2,0},{3,1},{4,2},{5,3},{6,4},{7,5},{8,14},{9,15},{10,... | collective-permute-start | bytes 331784 | tf_op jit(solution)/shard_map/ppermute | solution.py:76
  67.5 7.0 %collective-permute-start.15 = (bf16[24,2304]{1,0:T(8,128)(2,1)S(1)}, bf16[24,2304]{1,0:T(8,128)(2,1)S(1)}, u32[]{:S(2)}, u32[]{:S(2)}) collective-permute-start(bf16[24,2304]{1,0:T(8,128)(2,1)S(1)} %get-tuple-element.63), channel_id=1, source_target_pairs={{0,4},{1,5},{2,6},{3,7},{4,0},{5,1},{6,2},{7,3},{8,12},{9,13},{10,... | collective-permute-start | bytes 331784 | tf_op jit(solution)/shard_map/ppermute | solution.py:76
  67.5 7.8 %collective-permute-start.16 = (bf16[24,2304]{1,0:T(8,128)(2,1)S(1)}, bf16[24,2304]{1,0:T(8,128)(2,1)S(1)}, u32[]{:S(2)}, u32[]{:S(2)}) collective-permute-start(bf16[24,2304]{1,0:T(8,128)(2,1)S(1)} %get-tuple-element.64), channel_id=1, source_target_pairs={{0,2},{1,3},{2,4},{3,5},{4,6},{5,7},{6,0},{7,1},{8,10},{9,11},{10,... | collective-permute-start | bytes 331784 | tf_op jit(solution)/shard_map/ppermute | solution.py:76
  68.4 7.0 %collective-permute-start.17 = (bf16[24,2304]{1,0:T(8,128)(2,1)S(1)}, bf16[24,2304]{1,0:T(8,128)(2,1)S(1)}, u32[]{:S(2)}, u32[]{:S(2)}) collective-permute-start(bf16[24,2304]{1,0:T(8,128)(2,1)S(1)} %get-tuple-element.65), channel_id=1, source_target_pairs={{0,6},{1,7},{2,0},{3,1},{4,2},{5,3},{6,4},{7,5},{8,14},{9,15},{10,... | collective-permute-start | bytes 331784 | tf_op jit(solution)/shard_map/ppermute | solution.py:76
  72.5 4.8 %collective-permute-start.21 = (bf16[24,2304]{1,0:T(8,128)(2,1)S(1)}, bf16[24,2304]{1,0:T(8,128)(2,1)S(1)}, u32[]{:S(2)}, u32[]{:S(2)}) collective-permute-start(bf16[24,2304]{1,0:T(8,128)(2,1)S(1)} %add_x.1), channel_id=1, source_target_pairs={{0,8},{1,9},{2,10},{3,11},{4,12},{5,13},{6,14},{7,15},{8,0},{9,1},... | collective-permute-start | bytes 331784 | tf_op jit(solution)/shard_map/ppermute | solution.py:72
  77.5 6.3 %collective-permute-start.25 = (bf16[24,2304]{1,0:T(8,128)(2,1)S(1)}, bf16[24,2304]{1,0:T(8,128)(2,1)S(1)}, u32[]{:S(2)}, u32[]{:S(2)}) collective-permute-start(bf16[24,2304]{1,0:T(8,128)(2,1)S(1)} %error.1.refs_0_), channel_id=1, source_target_pairs={{0,8},{1,9},{2,10},{3,11},{4,12},{5,13},{6,14},{7,15},{8,0},{9,1},... | collective-permute-start | bytes 331784 | tf_op jit(solution)/shard_map/ppermute | solution.py:72
  78.2 10.2 %collective-permute-start.22 = (bf16[24,2304]{1,0:T(8,128)(2,1)S(1)}, bf16[24,2304]{1,0:T(8,128)(2,1)S(1)}, u32[]{:S(2)}, u32[]{:S(2)}) collective-permute-start(bf16[24,2304]{1,0:T(8,128)(2,1)S(1)} %error.1.refs_0_), channel_id=1, source_target_pairs={{0,6},{1,7},{2,0},{3,1},{4,2},{5,3},{6,4},{7,5},{8,14},{9,15},{10,... | collective-permute-start | bytes 331784 | tf_op jit(solution)/shard_map/ppermute | solution.py:76
  82.9 6.9 %collective-permute-start.23 = (bf16[24,2304]{1,0:T(8,128)(2,1)S(1)}, bf16[24,2304]{1,0:T(8,128)(2,1)S(1)}, u32[]{:S(2)}, u32[]{:S(2)}) collective-permute-start(bf16[24,2304]{1,0:T(8,128)(2,1)S(1)} %error.1.refs_0_), channel_id=1, source_target_pairs={{0,4},{1,5},{2,6},{3,7},{4,0},{5,1},{6,2},{7,3},{8,12},{9,13},{10,... | collective-permute-start | bytes 331784 | tf_op jit(solution)/shard_map/ppermute | solution.py:76
  82.9 8.0 %collective-permute-start.24 = (bf16[24,2304]{1,0:T(8,128)(2,1)S(1)}, bf16[24,2304]{1,0:T(8,128)(2,1)S(1)}, u32[]{:S(2)}, u32[]{:S(2)}) collective-permute-start(bf16[24,2304]{1,0:T(8,128)(2,1)S(1)} %error.1.refs_0_), channel_id=1, source_target_pairs={{0,2},{1,3},{2,4},{3,5},{4,6},{5,7},{6,0},{7,1},{8,10},{9,11},{10,... | collective-permute-start | bytes 331784 | tf_op jit(solution)/shard_map/ppermute | solution.py:76
  83.7 7.1 %collective-permute-start.26 = (bf16[24,2304]{1,0:T(8,128)(2,1)S(1)}, bf16[24,2304]{1,0:T(8,128)(2,1)S(1)}, u32[]{:S(2)}, u32[]{:S(2)}) collective-permute-start(bf16[24,2304]{1,0:T(8,128)(2,1)S(1)} %collective-permute-done.25.refs_4_), channel_id=1, source_target_pairs={{0,6},{1,7},{2,0},{3,1},{4,2},{5,3},{6,4},{7,5},{8,14},{9,15},{10,... | collective-permute-start | bytes 331784 | tf_op jit(solution)/shard_map/ppermute | solution.py:76
  86.9 6.3 %collective-permute-start.27 = (bf16[24,2304]{1,0:T(8,128)(2,1)S(1)}, bf16[24,2304]{1,0:T(8,128)(2,1)S(1)}, u32[]{:S(2)}, u32[]{:S(2)}) collective-permute-start(bf16[24,2304]{1,0:T(8,128)(2,1)S(1)} %collective-permute-done.25.refs_4_), channel_id=1, source_target_pairs={{0,4},{1,5},{2,6},{3,7},{4,0},{5,1},{6,2},{7,3},{8,12},{9,13},{10,... | collective-permute-start | bytes 331784 | tf_op jit(solution)/shard_map/ppermute | solution.py:76
  88.4 6.0 %collective-permute-start.28 = (bf16[24,2304]{1,0:T(8,128)(2,1)S(1)}, bf16[24,2304]{1,0:T(8,128)(2,1)S(1)}, u32[]{:S(2)}, u32[]{:S(2)}) collective-permute-start(bf16[24,2304]{1,0:T(8,128)(2,1)S(1)} %collective-permute-done.25.refs_4_), channel_id=1, source_target_pairs={{0,2},{1,3},{2,4},{3,5},{4,6},{5,7},{6,0},{7,1},{8,10},{9,11},{10,... | collective-permute-start | bytes 331784 | tf_op jit(solution)/shard_map/ppermute | solution.py:76
  94.6 2.7 %collective-permute-start.29 = (bf16[192,2304]{1,0:T(8,128)(2,1)S(1)}, bf16[192,2304]{1,0:T(8,128)(2,1)S(1)}, u32[]{:S(2)}, u32[]{:S(2)}) collective-permute-start(bf16[192,2304]{1,0:T(8,128)(2,1)S(1)} %join.1.a), channel_id=1, source_target_pairs={{0,1},{1,0},{2,3},{3,2},{4,5},{5,4},{6,7},{7,6},{8,9},{9,8},{10,11... | collective-permute-start | bytes 2654216 | tf_op jit(solution)/shard_map/ppermute | solution.py:68
  99.4 9.6 %collective-permute-start.33 = (bf16[400,256]{1,0:T(8,128)(2,1)S(1)}, bf16[400,256]{1,0:T(8,128)(2,1)S(1)}, u32[]{:S(2)}, u32[]{:S(2)}) collective-permute-start(bf16[400,256]{1,0:T(8,128)(2,1)S(1)} %get-tuple-element.77), channel_id=1, source_target_pairs={{0,32},{16,48},{32,0},{48,16},{64,96},{80,112},{96,64},{112,80},{1... | collective-permute-start | bytes 614408 | tf_op jit(solution)/shard_map/ppermute | solution.py:64
  101.3 12.1 %collective-permute-start.34 = (bf16[400,256]{1,0:T(8,128)(2,1)S(1)}, bf16[400,256]{1,0:T(8,128)(2,1)S(1)}, u32[]{:S(2)}, u32[]{:S(2)}) collective-permute-start(bf16[400,256]{1,0:T(8,128)(2,1)S(1)} %get-tuple-element.78), channel_id=1, source_target_pairs={{0,16},{16,32},{32,48},{48,0},{64,80},{80,96},{96,112},{112,64},{1... | collective-permute-start | bytes 614408 | tf_op jit(solution)/shard_map/ppermute | solution.py:64
  101.7 11.7 %collective-permute-start.35 = (bf16[400,256]{1,0:T(8,128)(2,1)S(1)}, bf16[400,256]{1,0:T(8,128)(2,1)S(1)}, u32[]{:S(2)}, u32[]{:S(2)}) collective-permute-start(bf16[400,256]{1,0:T(8,128)(2,1)S(1)} %get-tuple-element.79), channel_id=1, source_target_pairs={{0,48},{16,0},{32,16},{48,32},{64,112},{80,64},{96,80},{112,96},{1... | collective-permute-start | bytes 614408 | tf_op jit(solution)/shard_map/ppermute | solution.py:64
  106.6 11.2 %collective-permute-start.30 = (bf16[400,256]{1,0:T(8,128)(2,1)S(1)}, bf16[400,256]{1,0:T(8,128)(2,1)S(1)}, u32[]{:S(2)}, u32[]{:S(2)}) collective-permute-start(bf16[400,256]{1,0:T(8,128)(2,1)S(1)} %get-tuple-element.73), channel_id=1, source_target_pairs={{0,32},{16,48},{32,0},{48,16},{64,96},{80,112},{96,64},{112,80},{1... | collective-permute-start | bytes 614408 | tf_op jit(solution)/shard_map/ppermute | solution.py:64
  107.1 14.1 %collective-permute-start.31 = (bf16[400,256]{1,0:T(8,128)(2,1)S(1)}, bf16[400,256]{1,0:T(8,128)(2,1)S(1)}, u32[]{:S(2)}, u32[]{:S(2)}) collective-permute-start(bf16[400,256]{1,0:T(8,128)(2,1)S(1)} %get-tuple-element.74), channel_id=1, source_target_pairs={{0,16},{16,32},{32,48},{48,0},{64,80},{80,96},{96,112},{112,64},{1... | collective-permute-start | bytes 614408 | tf_op jit(solution)/shard_map/ppermute | solution.py:64
  109.0 12.3 %collective-permute-start.32 = (bf16[400,256]{1,0:T(8,128)(2,1)S(1)}, bf16[400,256]{1,0:T(8,128)(2,1)S(1)}, u32[]{:S(2)}, u32[]{:S(2)}) collective-permute-start(bf16[400,256]{1,0:T(8,128)(2,1)S(1)} %get-tuple-element.75), channel_id=1, source_target_pairs={{0,48},{16,0},{32,16},{48,32},{64,112},{80,64},{96,80},{112,96},{1... | collective-permute-start | bytes 614408 | tf_op jit(solution)/shard_map/ppermute | solution.py:64
  113.5 8.3 %collective-permute-start.36 = (bf16[400,256]{1,0:T(8,128)(2,1)S(1)}, bf16[400,256]{1,0:T(8,128)(2,1)S(1)}, u32[]{:S(2)}, u32[]{:S(2)}) collective-permute-start(bf16[400,256]{1,0:T(8,128)(2,1)S(1)} %add_z.3), channel_id=1, source_target_pairs={{0,64},{16,80},{32,96},{48,112},{64,0},{80,16},{96,32},{112,48},{1... | collective-permute-start | bytes 614408 | tf_op jit(solution)/shard_map/ppermute | solution.py:60
  122.0 8.0 %collective-permute-start.37 = (bf16[400,256]{1,0:T(8,128)(2,1)S(1)}, bf16[400,256]{1,0:T(8,128)(2,1)S(1)}, u32[]{:S(2)}, u32[]{:S(2)}) collective-permute-start(bf16[400,256]{1,0:T(8,128)(2,1)S(1)} %latent_grad.1.refs_2_), channel_id=1, source_target_pairs={{0,64},{16,80},{32,96},{48,112},{64,0},{80,16},{96,32},{112,48},{1... | collective-permute-start | bytes 614408 | tf_op jit(solution)/shard_map/ppermute | solution.py:60
  124.5 12.5 %collective-permute-start.41 = (bf16[400,256]{1,0:T(8,128)(2,1)S(1)}, bf16[400,256]{1,0:T(8,128)(2,1)S(1)}, u32[]{:S(2)}, u32[]{:S(2)}) collective-permute-start(bf16[400,256]{1,0:T(8,128)(2,1)S(1)} %latent_grad.1.refs_2_), channel_id=1, source_target_pairs={{0,32},{16,48},{32,0},{48,16},{64,96},{80,112},{96,64},{112,80},{1... | collective-permute-start | bytes 614408 | tf_op jit(solution)/shard_map/ppermute | solution.py:64
  125.6 12.8 %collective-permute-start.42 = (bf16[400,256]{1,0:T(8,128)(2,1)S(1)}, bf16[400,256]{1,0:T(8,128)(2,1)S(1)}, u32[]{:S(2)}, u32[]{:S(2)}) collective-permute-start(bf16[400,256]{1,0:T(8,128)(2,1)S(1)} %latent_grad.1.refs_2_), channel_id=1, source_target_pairs={{0,48},{16,0},{32,16},{48,32},{64,112},{80,64},{96,80},{112,96},{1... | collective-permute-start | bytes 614408 | tf_op jit(solution)/shard_map/ppermute | solution.py:64
  128.2 10.2 %collective-permute-start.43 = (bf16[400,256]{1,0:T(8,128)(2,1)S(1)}, bf16[400,256]{1,0:T(8,128)(2,1)S(1)}, u32[]{:S(2)}, u32[]{:S(2)}) collective-permute-start(bf16[400,256]{1,0:T(8,128)(2,1)S(1)} %latent_grad.1.refs_2_), channel_id=1, source_target_pairs={{0,16},{16,32},{32,48},{48,0},{64,80},{80,96},{96,112},{112,64},{1... | collective-permute-start | bytes 614408 | tf_op jit(solution)/shard_map/ppermute | solution.py:64
  130.1 12.8 %collective-permute-start.38 = (bf16[400,256]{1,0:T(8,128)(2,1)S(1)}, bf16[400,256]{1,0:T(8,128)(2,1)S(1)}, u32[]{:S(2)}, u32[]{:S(2)}) collective-permute-start(bf16[400,256]{1,0:T(8,128)(2,1)S(1)} %collective-permute-done.37.refs_3_), channel_id=1, source_target_pairs={{0,32},{16,48},{32,0},{48,16},{64,96},{80,112},{96,64},{112,80},{1... | collective-permute-start | bytes 614408 | tf_op jit(solution)/shard_map/ppermute | solution.py:64
  131.7 11.5 %collective-permute-start.39 = (bf16[400,256]{1,0:T(8,128)(2,1)S(1)}, bf16[400,256]{1,0:T(8,128)(2,1)S(1)}, u32[]{:S(2)}, u32[]{:S(2)}) collective-permute-start(bf16[400,256]{1,0:T(8,128)(2,1)S(1)} %collective-permute-done.37.refs_3_), channel_id=1, source_target_pairs={{0,48},{16,0},{32,16},{48,32},{64,112},{80,64},{96,80},{112,96},{1... | collective-permute-start | bytes 614408 | tf_op jit(solution)/shard_map/ppermute | solution.py:64
  137.0 8.3 %collective-permute-start.40 = (bf16[400,256]{1,0:T(8,128)(2,1)S(1)}, bf16[400,256]{1,0:T(8,128)(2,1)S(1)}, u32[]{:S(2)}, u32[]{:S(2)}) collective-permute-start(bf16[400,256]{1,0:T(8,128)(2,1)S(1)} %collective-permute-done.37.refs_3_), channel_id=1, source_target_pairs={{0,16},{16,32},{32,48},{48,0},{64,80},{80,96},{96,112},{112,64},{1... | collective-permute-start | bytes 614408 | tf_op jit(solution)/shard_map/ppermute | solution.py:64
  (1 other events, 1.5 us)

commit v4 on v3

--- a/solution.py
+++ b/solution.py
@@ -17,13 +17,14 @@
 CHIPS = 8
 PIECE = HALF // CHIPS
 EXTRA = 16
-GROUPS = ((0, 4), (2, 1, 3), (6, 5, 7))
+GROUPS = ((0,), (4, 2, 1, 3), (5, 7, 6))
+READY = (4, 5, 6, 7)
 SCALE = penalty_weight / ROWS
 MATMUL = 2 * ROWS * F * D
 
 NEAR = (0, 1, 2, 3)
 FAR = (4, 5, 6, 7)
-STEPS = (2, 1, 3)
+SIDES = (1, 3)
 
 f32 = jnp.float32
 bf16 = jnp.bfloat16
@@ -60,8 +61,8 @@
     return lax.ppermute(x, "layer", [(i, i ^ 4) for i in range(8)])
 
 
-def move_z(x, dz):
-    return lax.ppermute(x, "layer", [(i, i & 4 | ((i + dz) & 3)) for i in range(8)])
+def move_z(x, r):
+    return lax.ppermute(x, "layer", [(i, i ^ r) for i in range(8)])
 
 
 def move_core(x):
@@ -72,21 +73,16 @@
     return lax.ppermute(x, "latent", [(i, i ^ 8) for i in range(16)])
 
 
-def move_x(x, dx):
-    return lax.ppermute(x, "latent", [(i, i & 9 | ((i + 2 * dx) & 6)) for i in range(16)])
-
-
-def near(index, r):
-    dy, step = divmod(r, 4)
-    return ((index & 4) ^ (4 * dy)) | ((index + step) & 3)
+def move_x(x, r):
+    return lax.ppermute(x, "latent", [(i, i ^ (2 * r)) for i in range(16)])
 
 
 def block_of(r):
-    return near(lax.axis_index("layer"), r)
+    return lax.axis_index("layer") ^ r
 
 
 def chip_of(r):
-    return near(lax.axis_index("latent") >> 1, r)
+    return (lax.axis_index("latent") >> 1) ^ r
 
 
 def block_rows(r):
@@ -183,7 +179,7 @@
     extra = terms[0].shape[0] - ROWS
 
     def kernel(*refs):
-        t, out = refs[:4], refs[4]
+        *t, out = refs
         out[:ROWS] = add(t).astype(bf16)
         if extra:
             out[ROWS:] = split(add_extra(t))
@@ -253,9 +249,12 @@
 
 
 def add_x(terms):
-    def kernel(a, b, c, d, out):
-        value = a[...].astype(f32) + b[...].astype(f32)
-        out[...] = (value + (c[...].astype(f32) + d[...].astype(f32))).astype(bf16)
+    def kernel(*refs):
+        *t, out = refs
+        value = t[0][...].astype(f32)
+        for x in t[1:]:
+            value = value + x[...].astype(f32)
+        out[...] = value.astype(bf16)
 
     return call(kernel, terms, half(PIECE, D), "add_x", 1 << 20)
 
@@ -273,26 +272,28 @@
 
 def join(parts):
     def kernel(*refs):
-        out, held = refs[CHIPS:]
-        for k in range(CHIPS):
-            held[chip_of(k)] = refs[k][...].astype(f32)
-        out[...] = jnp.concatenate([held[k] for k in range(CHIPS)], axis=0).astype(bf16)
+        out, held = refs[4:]
+        for k in range(4):
+            held[chip_of(k) & 3] = refs[k][...].astype(f32)
+        out[...] = jnp.concatenate([held[k] for k in range(4)], axis=0).astype(bf16)
 
     return call(
         kernel,
         parts,
-        half(HALF, D),
+        half(4 * PIECE, D),
         "join",
         1 << 20,
-        [pltpu.VMEM((CHIPS, PIECE, D), f32)],
-    )
-
-
-def backward_far(near_rows, far_rows, rows, norms, weights):
-    def kernel(a, b, x, n, w, *refs):
-        outs, both = refs[:4], refs[4]
-        both[:HALF] = a[...]
-        both[HALF:ROWS] = b[...]
+        [pltpu.VMEM((4, PIECE, D), f32)],
+    )
+
+
+def backward_far(parts, rows, norms, weights):
+    def kernel(*refs):
+        p, (x, n, w), outs, both = refs[:4], refs[4:7], refs[7:11], refs[11]
+        low = lax.axis_index("latent") >> 3
+        for k in range(4):
+            at = (k // 2) * HALF + (low ^ (k % 2)) * (HALF // 2)
+            both[pl.ds(pl.multiple_of(at, HALF // 2), HALF // 2)] = p[k][...]
         for k, r in enumerate(FAR):
             outs[k][:ROWS] = product(both[:ROWS], w[block_rows(r)])
             outs[k][ROWS:] = split(n[r])
@@ -300,7 +301,7 @@
 
     return call(
         kernel,
-        (near_rows, far_rows, rows, norms, weights),
+        (*parts, rows, norms, weights),
         [half(ROWS + EXTRA, BLOCK)] * 4 + [half(2 * ROWS, D)],
         "backward_far",
         MATMUL // 2,
@@ -324,46 +325,93 @@
     )
 
 
-def latent_grad(terms, active):
-    def kernel(*refs):
-        t, (a, out) = refs[:5], refs[5:]
+def latent_grad(terms, active, ready):
+    def kernel(*refs):
+        t, (a, _, out) = refs[:5], refs[5:]
         total = add_extra(t)
         value = add(t) + SCALE * total[:1]
         out[:ROWS] = (value * (2.0 * a[...].astype(f32))).astype(bf16)
         out[ROWS:] = split(total)
 
-    return call(kernel, (*terms, active), half(ROWS + EXTRA, BLOCK), "latent_grad", 1 << 20)
-
-
-def gradient(lats, dpres, both, norms, weights, blocks, before=()):
+    return call(
+        kernel,
+        (*terms, active, ready),
+        half(ROWS + EXTRA, BLOCK),
+        "latent_grad",
+        1 << 20,
+        places=[VMEM] * 6 + [HBM],
+    )
+
+
+def prepare_gradient(lats, both, norms, weights):
+    width = 768
+
+    def kernel(early, late, e, n, w, out):
+        for k, r in enumerate(READY):
+            l = early[r] if r < 4 else late[r - 4]
+            column = penalty(l, n[r])
+            for i in range(D // width):
+                cols = slice(i * width, (i + 1) * width)
+                g = lax.dot_general(l, e[:ROWS, cols], TN, preferred_element_type=f32)
+                out[k, :, cols] = (g + column * w[block_rows(r), cols].astype(f32)).astype(bf16)
+
+    return call(
+        kernel,
+        (*lats, both, norms, weights),
+        half(len(READY), BLOCK, D),
+        "prepare_gradient",
+        MATMUL * len(READY) // LAYERS,
+        mib=8,
+    )
+
+
+def penalty(lat, norms):
+    usage = jnp.sum(lat.astype(f32), axis=0, keepdims=True)
+    return (SCALE * jnp.broadcast_to(usage, (8, BLOCK)) / norms).T[:, :1]
+
+
+def gradient(lats, dpres, both, norms, weights, ready, blocks, before=None, last=False):
     width = 768
     steps = D // width
     count = len(blocks)
-
-    def kernel(*refs):
-        early, late, d = refs[0], refs[1], refs[2 : 2 + count]
-        e, n, w = refs[2 + count : 5 + count]
-        out, bias, totals, *rest = refs[5 + count + len(before) :]
-        lhs, buf, sem = rest[-3:]
-        if before:
-            bias[...] = refs[6 + count][...]
-            totals[...] = refs[7 + count][...]
-        else:
-            rest[0][...] = jnp.sum(e[:ROWS].astype(f32), axis=0, keepdims=True)
+    used = tuple(range(LAYERS)) if last else blocks
+    first = before is None
+
+    def kernel(early, late, *refs):
+        d = dict(zip(used, refs))
+        e, n, w, p = refs[len(used) : len(used) + 4]
+        refs = refs[len(used) + 4 + (not first) :]
+        out, lhs, buf, sem = refs[0], *refs[-3:]
         copies = []
+        if first:
+            bias, held, bias_sem = refs[1:4]
+            held[...] = jnp.sum(e[:ROWS].astype(f32), axis=0, keepdims=True)
+            copies.append(pltpu.make_async_copy(held, bias, bias_sem.at[0]))
+        if last:
+            enc, totals, held, sums, bias_sem = refs[1:6]
+            for r in range(LAYERS):
+                x = d[r][:ROWS].astype(f32)
+                held[block_of(r)] = jnp.sum(x, axis=0, keepdims=True)
+                sums[block_of(r)] = split_sum(d[r][ROWS:])[:1]
+            copies.append(pltpu.make_async_copy(held, enc, bias_sem.at[0]))
+            copies.append(pltpu.make_async_copy(sums, totals, bias_sem.at[1]))
+        for copy in copies:
+            copy.start()
         for k, r in enumerate(blocks):
-            l = early[r] if r < 4 else late[r - 4]
-            x = d[k][:ROWS]
-            lhs[:ROWS] = l
-            lhs[ROWS:] = x
-            usage = jnp.sum(l.astype(f32), axis=0, keepdims=True)
-            column = (SCALE * jnp.broadcast_to(usage, (8, BLOCK)) / n[r]).T[:, :1]
-            bias[block_of(r)] = jnp.sum(x.astype(f32), axis=0, keepdims=True)
-            totals[block_of(r)] = split_sum(d[k][ROWS:])[:1]
+            if r not in READY:
+                l = early[r] if r < 4 else late[r - 4]
+                lhs[:ROWS] = l
+                lhs[ROWS:] = d[r][:ROWS]
+                column = penalty(l, n[r])
             for i in range(steps):
                 cols = slice(i * width, (i + 1) * width)
-                g = lax.dot_general(lhs[...], e[:, cols], TN, preferred_element_type=f32)
-                g = g + column * w[block_rows(r), cols].astype(f32)
+                if r in READY:
+                    x = d[r][:ROWS]
+                    g = lax.dot_general(x, e[ROWS:, cols], TN, preferred_element_type=f32)
+                    g = g + p[READY.index(r), :, cols].astype(f32)
+                else:
+                    g = lax.dot_general(lhs[...], e[:, cols], TN, preferred_element_type=f32)
+                    g = g + column * w[block_rows(r), cols].astype(f32)
                 buf[k, :, cols] = g.astype(bf16)
                 copy = pltpu.make_async_copy(
                     buf.at[k, :, cols], out.at[block_rows(r), cols], sem.at[k, i]
@@ -373,39 +421,47 @@
         for copy in copies:
             copy.wait()
 
-    shapes = [half(F, D), full(LAYERS, 1, BLOCK), full(LAYERS, 1, BLOCK)]
-    if not before:
+    shapes, scratch = [half(F, D)], []
+    if first:
         shapes.append(full(1, D))
-    return call(
-        kernel,
-        (*lats, *[dpres[r] for r in blocks], both, norms, weights, *before),
+        scratch += [pltpu.VMEM((1, D), f32), pltpu.SemaphoreType.DMA((1,))]
+    if last:
+        shapes += [full(LAYERS, 1, BLOCK)] * 2
+        scratch += [pltpu.VMEM((LAYERS, 1, BLOCK), f32)] * 2 + [pltpu.SemaphoreType.DMA((2,))]
+    operands = (*lats, *[dpres[r] for r in used], both, norms, weights, ready)
+    return call(
+        kernel,
+        operands if first else (*operands, before),
         shapes,
         "gradient",
         2 * MATMUL * count // LAYERS,
-        [
+        scratch
+        + [
             pltpu.VMEM((2 * ROWS, BLOCK), bf16),
             pltpu.VMEM((count, BLOCK, D), bf16),
             pltpu.SemaphoreType.DMA((count, steps)),
         ],
         12,
-        [VMEM] * (5 + count) + ([HBM, VMEM, VMEM] if before else []),
-        [HBM] + [VMEM] * (len(shapes) - 1),
-        {5 + count: 0} if before else None,
+        [VMEM] * len(operands) + ([] if first else [HBM]),
+        [HBM] * len(shapes),
+        None if first else {len(operands): 0},
     )
 
 
 def scatter(terms, ring, pair, add):
-    far = [ring(terms[4 + d], d) for d in STEPS]
-    near = [ring(terms[d], d) for d in STEPS]
+    cross = pair(terms[6])
+    far = [ring(terms[4 + d], d) for d in SIDES]
+    near = [ring(terms[d], d) for d in SIDES]
     other = pair(add([terms[4]] + far))
-    return [terms[0]] + near + [other]
+    return [terms[0]] + near + [ring(add([terms[2], cross]), 2), other]
 
 
 def gather(own, ring, pair):
-    blocks = {0: own, 4: pair(own)}
+    blocks = {0: own, 4: pair(own), 2: ring(own, 2)}
     for r in (0, 4):
-        for d in STEPS:
-            blocks[r + d] = ring(blocks[r], 4 - d)
+        for d in SIDES:
+            blocks[r + d] = ring(blocks[r], d)
+    blocks[6] = pair(blocks[2])
     return blocks
 
 
@@ -418,25 +474,28 @@
     norms, piece = prepare(rows, weights)
     mine = activate(scatter(terms, move_z, move_y, add_z), bias)
     active = gather(mine, move_z, move_y)
-    lat_near, before = decode([active[r] for r in NEAR], weights, NEAR, after=(piece,))
+    lat_near, before = decode([active[r] for r in NEAR], weights, NEAR)
     lat_far, here, there = decode([active[r] for r in FAR], weights, FAR, before)
 
     pieces = add_core(here, move_core(there))
     own = error(scatter(pieces, move_x, move_lo, add_x), dec_bias, piece)
     got = gather(own, move_x, move_lo)
-    here = join([got[r] for r in range(CHIPS)])
-
-    *far, both = backward_far(here, move_core(here), rows, norms, weights)
+    here = [join([got[r] for r in blocks]) for blocks in (NEAR, FAR)]
+    errors = here + [move_core(x) for x in here]
+
+    *far, both = backward_far(errors, rows, norms, weights)
     terms = list(backward_near(both, norms, weights)) + far
-    dpre = latent_grad(scatter(terms, move_z, move_y, add_z), mine)
+    ready = prepare_gradient((lat_near, lat_far), both, norms, weights)
+    dpre = latent_grad(scatter(terms, move_z, move_y, add_z), mine, ready)
     dpres = gather(dpre, move_z, move_y)
-    out = ()
-    for blocks in GROUPS:
-        got = gradient((lat_near, lat_far), dpres, both, norms, weights, blocks, out)
-        if not out:
-            dec_grad = got[3]
-        out = tuple(got[:3])
-    grad, enc_grad, total = out
+    grad = None
+    for i, blocks in enumerate(GROUPS):
+        last = i == len(GROUPS) - 1
+        out = gradient((lat_near, lat_far), dpres, both, norms, weights, ready, blocks, grad, last)
+        grad = out[0]
+        if i == 0:
+            dec_grad = out[1]
+    enc_grad, total = out[1:]
     return grad[None], enc_grad.reshape(F), dec_grad, total.reshape(F)
 
 

time: 151 us -> 125 us (0.83)
  waiting for transfers between devices: 45.2 us -> 27.4 us
  starting transfers between devices: 70.1 us -> 62 us
    ppermute x36 -> x30, waiting for transfers between devices: 34.2 us -> 17.1 us  [the longest x20 12.5 us: move_z(): return lax.ppermute(x, 'layer', [(i, i ^ r) for i in range(8)])]
    ppermute x36 -> x30, starting transfers between devices: 56.7 us -> 43.1 us  [the longest x20 27.6 us: move_z(): return lax.ppermute(x, 'layer', [(i, i ^ r) for i in range(8)])]
    ppermute x4 -> x8, starting transfers between devices: 11.5 us -> 14.9 us  [move_y(): return lax.ppermute(x, 'layer', [(i, i ^ 4) for i in range(8)])]
    ppermute x2 -> x4, starting transfers between devices: 1.49 us -> 3.78 us  [move_lo(): return lax.ppermute(x, 'latent', [(i, i ^ 8) for i in range(16)])]
    ppermute x4 -> x8, waiting for transfers between devices: 4.11 us -> 5.39 us  [move_y(): return lax.ppermute(x, 'layer', [(i, i ^ 4) for i in range(8)])]
    ppermute x2 -> x3, waiting for transfers between devices: 4.83 us -> 4.18 us  [move_core(): return lax.ppermute(x, 'latent', [(i, i ^ 1) for i in range(16)])]
    pallas_call x18 -> x23, Pallas kernels: 28.9 us -> 28.6 us  [call(): pl.pallas_call(kernel, in_specs=places or [VMEM] * len(operands), out_spe...]
  transfers between devices with their start and end apart: 44 -> 45, of which waited for: 28 -> 15; matrix products, arithmetic and copies ran while one was open for 0% -> 0% of each run, Pallas kernels for 11% -> 15%
where the time goes in v4:
time: 125 us; the launch traced here: 124 us
  starting transfers between devices  62 us (50%)
  Pallas kernels  28.6 us (23%)
  waiting for transfers between devices  27.4 us (22%)
  local copies, waits for them, and re-layouts  5.16 us (4%)
    pallas_call x23, Pallas kernels, call(): pl.pallas_call(kernel, in_specs=places or [VMEM] * len(operands), out_spe...  28.6 us
    ppermute x20, starting transfers between devices, move_z(): return lax.ppermute(x, 'layer', [(i, i ^ r) for i in range(8)])  27.6 us
    ppermute x10, starting transfers between devices, move_x(): return lax.ppermute(x, 'latent', [(i, i ^ 2 * r) for i in range(16)])  15.5 us
    ppermute x8, starting transfers between devices, move_y(): return lax.ppermute(x, 'layer', [(i, i ^ 4) for i in range(8)])  14.9 us
    ppermute x20, waiting for transfers between devices, move_z(): return lax.ppermute(x, 'layer', [(i, i ^ r) for i in range(8)])  12.5 us
    ppermute x8, waiting for transfers between devices, move_y(): return lax.ppermute(x, 'layer', [(i, i ^ 4) for i in range(8)])  5.39 us
    unnamed x10, local copies, waits for them, and re-layouts  5.16 us
    ppermute x10, waiting for transfers between devices, move_x(): return lax.ppermute(x, 'latent', [(i, i ^ 2 * r) for i in range(16)])  4.59 us
  transfers between devices with their start and end apart: 45, of which 15 were waited for; matrix products, arithmetic and copies ran while one was open for 0% of the time, Pallas kernels for 15%

profile of v4, /device:TPU:0, one launch (start us, length us, event | category | flops | bytes accessed | tf_op | source)
XLA Modules:
  0.0 124.2 jit_solution(1518412911746469456)
XLA Ops:
  0.6 3.7 %copy-done = bf16[1,2048,2304]{2,1,0:T(8,128)(2,1)S(1)} copy-done((bf16[1,2048,2304]{2,1,0:T(8,128)(2,1)S(1)}, bf16[1,2048,2304]{2,1,0:T(8,128)(2,1)}, u32[]{:S(2)}) %copy-start) | copy-done | bytes 9437208
  4.3 1.5 %copy-done.2 = bf16[1,384,2304]{2,1,0:T(8,128)(2,1)S(1)} copy-done((bf16[1,384,2304]{2,1,0:T(8,128)(2,1)S(1)}, bf16[1,384,2304]{2,1,0:T(8,128)(2,1)}, u32[]{:S(2)}) %copy-start.2) | copy-done | bytes 1769496
  5.8 2.0 %encode_far.1 = (bf16[384,256]{1,0:T(8,128)(2,1)S(1)}, bf16[384,256]{1,0:T(8,128)(2,1)S(1)}, bf16[384,256]{1,0:T(8,128)(2,1)S(1)}, bf16[384,256]{1,0:T(8,128)(2,1)S(1)}, bf16[384,2304]{1,0:T(8,128)(2,1)S(1)}) custom-call(bf16[384,2304]{1,0:T(8,128)(2,1)S(1)} %bitcast.17, bf16[2048,2304]{1,0:T(8,128)(2,1)S(1)} %bitcast.6), custom_call_target="tpu_custom_call" | custom-call | flops 1811939328 | bytes 4529848 | tf_op jit(solution)/shard_map/encode_far/pallas_call | solution.py:47
  7.8 2.1 %collective-permute-start.4 = (bf16[384,256]{1,0:T(8,128)(2,1)S(1)}, bf16[384,256]{1,0:T(8,128)(2,1)S(1)}, u32[]{:S(2)}, u32[]{:S(2)}) collective-permute-start(bf16[384,256]{1,0:T(8,128)(2,1)S(1)} %get-tuple-element.49), channel_id=1, source_target_pairs={{0,16},{16,0},{32,48},{48,32},{64,80},{80,64},{96,112},{112,96},{1... | collective-permute-start | bytes 589832 | tf_op jit(solution)/shard_map/ppermute | solution.py:65
  9.9 2.5 %collective-permute-start.5 = (bf16[384,256]{1,0:T(8,128)(2,1)S(1)}, bf16[384,256]{1,0:T(8,128)(2,1)S(1)}, u32[]{:S(2)}, u32[]{:S(2)}) collective-permute-start(bf16[384,256]{1,0:T(8,128)(2,1)S(1)} %get-tuple-element.50), channel_id=1, source_target_pairs={{0,48},{16,32},{32,16},{48,0},{64,112},{80,96},{96,80},{112,64},{1... | collective-permute-start | bytes 589832 | tf_op jit(solution)/shard_map/ppermute | solution.py:65
  12.4 3.2 %collective-permute-start.2 = (bf16[384,256]{1,0:T(8,128)(2,1)S(1)}, bf16[384,256]{1,0:T(8,128)(2,1)S(1)}, u32[]{:S(2)}, u32[]{:S(2)}) collective-permute-start(bf16[384,256]{1,0:T(8,128)(2,1)S(1)} %get-tuple-element.47), channel_id=1, source_target_pairs={{0,64},{16,80},{32,96},{48,112},{64,0},{80,16},{96,32},{112,48},{1... | collective-permute-start | bytes 589832 | tf_op jit(solution)/shard_map/ppermute | solution.py:61
  15.6 2.0 %encode_near.1 = (bf16[384,256]{1,0:T(8,128)(2,1)S(1)}, bf16[384,256]{1,0:T(8,128)(2,1)S(1)}, bf16[384,256]{1,0:T(8,128)(2,1)S(1)}, bf16[384,256]{1,0:T(8,128)(2,1)S(1)}) custom-call(bf16[384,2304]{1,0:T(8,128)(2,1)S(1)} %get-tuple-element.42.a.refs_4_, bf16[2048,2304]{1,0:T(8,128)(2,1)S(1)} %bitcast.7), custom_call_target="tpu_custom_call" | custom-call | flops 1811939328 | bytes 4529848 | tf_op jit(solution)/shard_map/encode_near/pallas_call | solution.py:47
  19.4 1.4 %collective-permute-start.6 = (bf16[384,256]{1,0:T(8,128)(2,1)S(1)}, bf16[384,256]{1,0:T(8,128)(2,1)S(1)}, u32[]{:S(2)}, u32[]{:S(2)}) collective-permute-start(bf16[384,256]{1,0:T(8,128)(2,1)S(1)} %add_z.5), channel_id=1, source_target_pairs={{0,64},{16,80},{32,96},{48,112},{64,0},{80,16},{96,32},{112,48},{1... | collective-permute-start | bytes 589832 | tf_op jit(solution)/shard_map/ppermute | solution.py:61
  20.9 2.9 %collective-permute-start.3 = (bf16[384,256]{1,0:T(8,128)(2,1)S(1)}, bf16[384,256]{1,0:T(8,128)(2,1)S(1)}, u32[]{:S(2)}, u32[]{:S(2)}) collective-permute-start(bf16[384,256]{1,0:T(8,128)(2,1)S(1)} %add_z.4), channel_id=1, source_target_pairs={{0,32},{16,48},{32,0},{48,16},{64,96},{80,112},{96,64},{112,80},{1... | collective-permute-start | bytes 589832 | tf_op jit(solution)/shard_map/ppermute | solution.py:65
  23.8 6.0 %collective-permute-done.1.refs_2_ = bf16[384,256]{1,0:T(8,128)(2,1)S(1)} collective-permute-done((bf16[384,256]{1,0:T(8,128)(2,1)S(1)}, bf16[384,256]{1,0:T(8,128)(2,1)S(1)}, u32[]{:S(2)}, u32[]{:S(2)}) %collective-permute-start.1) | collective-permute-done | bytes 196640 | tf_op jit(solution)/shard_map/ppermute | solution.py:65
  30.7 2.3 %collective-permute-start.8 = (bf16[384,256]{1,0:T(8,128)(2,1)S(1)}, bf16[384,256]{1,0:T(8,128)(2,1)S(1)}, u32[]{:S(2)}, u32[]{:S(2)}) collective-permute-start(bf16[384,256]{1,0:T(8,128)(2,1)S(1)} %activate.1.refs_0_.refs_5_), channel_id=1, source_target_pairs={{0,32},{16,48},{32,0},{48,16},{64,96},{80,112},{96,64},{112,80},{1... | collective-permute-start | bytes 589832 | tf_op jit(solution)/shard_map/ppermute | solution.py:65
  33.1 1.4 %collective-permute-start.9 = (bf16[384,256]{1,0:T(8,128)(2,1)S(1)}, bf16[384,256]{1,0:T(8,128)(2,1)S(1)}, u32[]{:S(2)}, u32[]{:S(2)}) collective-permute-start(bf16[384,256]{1,0:T(8,128)(2,1)S(1)} %activate.1.refs_0_.refs_5_), channel_id=1, source_target_pairs={{0,48},{16,32},{32,16},{48,0},{64,112},{80,96},{96,80},{112,64},{1... | collective-permute-start | bytes 589832 | tf_op jit(solution)/shard_map/ppermute | solution.py:65
  34.4 2.8 %collective-permute-done.10.refs_0_ = bf16[384,256]{1,0:T(8,128)(2,1)S(1)} collective-permute-done((bf16[384,256]{1,0:T(8,128)(2,1)S(1)}, bf16[384,256]{1,0:T(8,128)(2,1)S(1)}, u32[]{:S(2)}, u32[]{:S(2)}) %collective-permute-start.10) | collective-permute-done | bytes 196640 | tf_op jit(solution)/shard_map/ppermute | solution.py:61
  38.5 1.5 %collective-permute-done.8.refs_2_ = bf16[384,256]{1,0:T(8,128)(2,1)S(1)} collective-permute-done((bf16[384,256]{1,0:T(8,128)(2,1)S(1)}, bf16[384,256]{1,0:T(8,128)(2,1)S(1)}, u32[]{:S(2)}, u32[]{:S(2)}) %collective-permute-start.8) | collective-permute-done | bytes 196640 | tf_op jit(solution)/shard_map/ppermute | solution.py:65
  40.0 2.6 %collective-permute-start.12 = (bf16[384,256]{1,0:T(8,128)(2,1)S(1)}, bf16[384,256]{1,0:T(8,128)(2,1)S(1)}, u32[]{:S(2)}, u32[]{:S(2)}) collective-permute-start(bf16[384,256]{1,0:T(8,128)(2,1)S(1)} %collective-permute-done.8.refs_2_), channel_id=1, source_target_pairs={{0,64},{16,80},{32,96},{48,112},{64,0},{80,16},{96,32},{112,48},{1... | collective-permute-start | bytes 589832 | tf_op jit(solution)/shard_map/ppermute | solution.py:61
  42.6 2.0 %decode.2 = (bf16[4,384,256]{2,1,0:T(8,128)(2,1)S(1)}, f32[384,2304]{1,0:T(8,128)S(1)}) custom-call(bf16[384,256]{1,0:T(8,128)(2,1)S(1)} %activate.1.refs_0_.refs_5_, bf16[384,256]{1,0:T(8,128)(2,1)S(1)} %collective-permute-done.7.refs_1_, bf16[384,256]{1,0:T(8,128)(2,1)S(1)} %collective-permute-done.8.refs_2_, ...), custom_call_target="tpu_custom_call" | custom-call | flops 1811939328 | bytes 4529848 | tf_op jit(solution)/shard_map/decode/pallas_call | solution.py:47
  44.6 2.6 %collective-permute-done.12.refs_2_ = bf16[384,256]{1,0:T(8,128)(2,1)S(1)} collective-permute-done((bf16[384,256]{1,0:T(8,128)(2,1)S(1)}, bf16[384,256]{1,0:T(8,128)(2,1)S(1)}, u32[]{:S(2)}, u32[]{:S(2)}) %collective-permute-start.12) | collective-permute-done | bytes 196640 | tf_op jit(solution)/shard_map/ppermute | solution.py:61
  47.2 2.0 %decode.3 = (bf16[4,384,256]{2,1,0:T(8,128)(2,1)S(1)}, bf16[192,2304]{1,0:T(8,128)(2,1)S(1)}, bf16[192,2304]{1,0:T(8,128)(2,1)S(1)}) custom-call(bf16[384,256]{1,0:T(8,128)(2,1)S(1)} %collective-permute-done.10.refs_0_, bf16[384,256]{1,0:T(8,128)(2,1)S(1)} %collective-permute-done.11.refs_1_, bf16[384,256]{1,0:T(8,128)(2,1)S(1)} %collective-permute-done.12.refs_2_, ...), custom_call_target="tpu_custom_call" | custom-call | flops 1811939328 | bytes 4529848 | tf_op jit(solution)/shard_map/decode/pallas_call | solution.py:47
  49.3 2.4 %collective-permute-done.14.b = bf16[192,2304]{1,0:T(8,128)(2,1)S(1)} collective-permute-done((bf16[192,2304]{1,0:T(8,128)(2,1)S(1)}, bf16[192,2304]{1,0:T(8,128)(2,1)S(1)}, u32[]{:S(2)}, u32[]{:S(2)}) %collective-permute-start.14) | collective-permute-done | bytes 884768 | tf_op jit(solution)/shard_map/ppermute | solution.py:69
  52.0 1.4 %collective-permute-start.17 = (bf16[24,2304]{1,0:T(8,128)(2,1)S(1)}, bf16[24,2304]{1,0:T(8,128)(2,1)S(1)}, u32[]{:S(2)}, u32[]{:S(2)}) collective-permute-start(bf16[24,2304]{1,0:T(8,128)(2,1)S(1)} %get-tuple-element.60), channel_id=1, source_target_pairs={{0,8},{1,9},{2,10},{3,11},{4,12},{5,13},{6,14},{7,15},{8,0},{9,1},... | collective-permute-start | bytes 331784 | tf_op jit(solution)/shard_map/ppermute | solution.py:73
  53.4 1.5 %collective-permute-start.19 = (bf16[24,2304]{1,0:T(8,128)(2,1)S(1)}, bf16[24,2304]{1,0:T(8,128)(2,1)S(1)}, u32[]{:S(2)}, u32[]{:S(2)}) collective-permute-start(bf16[24,2304]{1,0:T(8,128)(2,1)S(1)} %get-tuple-element.62), channel_id=1, source_target_pairs={{0,2},{1,3},{2,0},{3,1},{4,6},{5,7},{6,4},{7,5},{8,10},{9,11},{10,... | collective-permute-start | bytes 331784 | tf_op jit(solution)/shard_map/ppermute | solution.py:77
  54.9 2.1 %collective-permute-start.20 = (bf16[24,2304]{1,0:T(8,128)(2,1)S(1)}, bf16[24,2304]{1,0:T(8,128)(2,1)S(1)}, u32[]{:S(2)}, u32[]{:S(2)}) collective-permute-start(bf16[24,2304]{1,0:T(8,128)(2,1)S(1)} %get-tuple-element.63), channel_id=1, source_target_pairs={{0,6},{1,7},{2,4},{3,5},{4,2},{5,3},{6,0},{7,1},{8,14},{9,15},{10,... | collective-permute-start | bytes 331784 | tf_op jit(solution)/shard_map/ppermute | solution.py:77
  58.2 3.1 %collective-permute-start.18 = (bf16[24,2304]{1,0:T(8,128)(2,1)S(1)}, bf16[24,2304]{1,0:T(8,128)(2,1)S(1)}, u32[]{:S(2)}, u32[]{:S(2)}) collective-permute-start(bf16[24,2304]{1,0:T(8,128)(2,1)S(1)} %add_x.2), channel_id=1, source_target_pairs={{0,4},{1,5},{2,6},{3,7},{4,0},{5,1},{6,2},{7,3},{8,12},{9,13},{10,... | collective-permute-start | bytes 331784 | tf_op jit(solution)/shard_map/ppermute | solution.py:77
  62.2 2.5 %prepare.1 = (f32[8,8,256]{2,1,0:T(8,128)S(1)}, bf16[24,2304]{1,0:T(8,128)(2,1)S(1)}) custom-call(bf16[384,2304]{1,0:T(8,128)(2,1)S(1)} %get-tuple-element.42.a.refs_4_, bf16[2048,2304]{1,0:T(8,128)(2,1)S(1)} %bitcast.10), custom_call_target="tpu_custom_call" | custom-call | flops 1073741824 | bytes 2684354 | tf_op jit(solution)/shard_map/prepare/pallas_call | solution.py:47
  67.2 2.2 %collective-permute-start.23 = (bf16[24,2304]{1,0:T(8,128)(2,1)S(1)}, bf16[24,2304]{1,0:T(8,128)(2,1)S(1)}, u32[]{:S(2)}, u32[]{:S(2)}) collective-permute-start(bf16[24,2304]{1,0:T(8,128)(2,1)S(1)} %error.1.refs_0_), channel_id=1, source_target_pairs={{0,4},{1,5},{2,6},{3,7},{4,0},{5,1},{6,2},{7,3},{8,12},{9,13},{10,... | collective-permute-start | bytes 331784 | tf_op jit(solution)/shard_map/ppermute | solution.py:77
  71.2 3.6 %collective-permute-start.28 = (bf16[24,2304]{1,0:T(8,128)(2,1)S(1)}, bf16[24,2304]{1,0:T(8,128)(2,1)S(1)}, u32[]{:S(2)}, u32[]{:S(2)}) collective-permute-start(bf16[24,2304]{1,0:T(8,128)(2,1)S(1)} %collective-permute-done.25.refs_0_), channel_id=1, source_target_pairs={{0,6},{1,7},{2,4},{3,5},{4,2},{5,3},{6,0},{7,1},{8,14},{9,15},{10,... | collective-permute-start | bytes 331784 | tf_op jit(solution)/shard_map/ppermute | solution.py:77
  75.9 1.7 %collective-permute-done.28.refs_3_ = bf16[24,2304]{1,0:T(8,128)(2,1)S(1)} collective-permute-done((bf16[24,2304]{1,0:T(8,128)(2,1)S(1)}, bf16[24,2304]{1,0:T(8,128)(2,1)S(1)}, u32[]{:S(2)}, u32[]{:S(2)}) %collective-permute-start.28) | collective-permute-done | bytes 110624 | tf_op jit(solution)/shard_map/ppermute | solution.py:77
  77.5 2.0 %collective-permute-done.26.refs_1_ = bf16[24,2304]{1,0:T(8,128)(2,1)S(1)} collective-permute-done((bf16[24,2304]{1,0:T(8,128)(2,1)S(1)}, bf16[24,2304]{1,0:T(8,128)(2,1)S(1)}, u32[]{:S(2)}, u32[]{:S(2)}) %collective-permute-start.26) | collective-permute-done | bytes 110624 | tf_op jit(solution)/shard_map/ppermute | solution.py:77
  79.8 1.8 %collective-permute-done.30.refs_3_ = bf16[96,2304]{1,0:T(8,128)(2,1)S(1)} collective-permute-done((bf16[96,2304]{1,0:T(8,128)(2,1)S(1)}, bf16[96,2304]{1,0:T(8,128)(2,1)S(1)}, u32[]{:S(2)}, u32[]{:S(2)}) %collective-permute-start.30) | collective-permute-done | bytes 442400 | tf_op jit(solution)/shard_map/ppermute | solution.py:69
  81.6 2.1 %backward_far.1 = (bf16[400,256]{1,0:T(8,128)(2,1)S(1)}, bf16[400,256]{1,0:T(8,128)(2,1)S(1)}, bf16[400,256]{1,0:T(8,128)(2,1)S(1)}, bf16[400,256]{1,0:T(8,128)(2,1)S(1)}, bf16[768,2304]{1,0:T(8,128)(2,1)S(1)}) custom-call(bf16[96,2304]{1,0:T(8,128)(2,1)S(1)} %join.2.refs_0_, bf16[96,2304]{1,0:T(8,128)(2,1)S(1)} %join.3.refs_1_, ...), custom_call_target="tpu_custom_call" | custom-call | flops 1811939328 | bytes 4529848 | tf_op jit(solution)/shard_map/backward_far/pallas_call | solution.py:47
  84.4 1.7 %collective-permute-start.36 = (bf16[400,256]{1,0:T(8,128)(2,1)S(1)}, bf16[400,256]{1,0:T(8,128)(2,1)S(1)}, u32[]{:S(2)}, u32[]{:S(2)}) collective-permute-start(bf16[400,256]{1,0:T(8,128)(2,1)S(1)} %get-tuple-element.74), channel_id=1, source_target_pairs={{0,48},{16,32},{32,16},{48,0},{64,112},{80,96},{96,80},{112,64},{1... | collective-permute-start | bytes 614408 | tf_op jit(solution)/shard_map/ppermute | solution.py:65
  86.1 1.8 %collective-permute-start.33 = (bf16[400,256]{1,0:T(8,128)(2,1)S(1)}, bf16[400,256]{1,0:T(8,128)(2,1)S(1)}, u32[]{:S(2)}, u32[]{:S(2)}) collective-permute-start(bf16[400,256]{1,0:T(8,128)(2,1)S(1)} %get-tuple-element.71), channel_id=1, source_target_pairs={{0,64},{16,80},{32,96},{48,112},{64,0},{80,16},{96,32},{112,48},{1... | collective-permute-start | bytes 614408 | tf_op jit(solution)/shard_map/ppermute | solution.py:61
  87.9 2.0 %backward_near.1 = (bf16[400,256]{1,0:T(8,128)(2,1)S(1)}, bf16[400,256]{1,0:T(8,128)(2,1)S(1)}, bf16[400,256]{1,0:T(8,128)(2,1)S(1)}, bf16[400,256]{1,0:T(8,128)(2,1)S(1)}) custom-call(bf16[768,2304]{1,0:T(8,128)(2,1)S(1)} %get-tuple-element.66.e.refs_1_.refs_4_.refs_8_, f32[8,8,256]{2,1,0:T(8,128)S(1)} %get-tuple-element.65.refs_5_.n.refs_2_.refs_9_, ...), custom_call_target="tpu_custom_call" | custom-call | flops 1811939328 | bytes 4529848 | tf_op jit(solution)/shard_map/backward_near/pallas_call | solution.py:47
  90.3 2.4 %collective-permute-start.32 = (bf16[400,256]{1,0:T(8,128)(2,1)S(1)}, bf16[400,256]{1,0:T(8,128)(2,1)S(1)}, u32[]{:S(2)}, u32[]{:S(2)}) collective-permute-start(bf16[400,256]{1,0:T(8,128)(2,1)S(1)} %get-tuple-element.69), channel_id=1, source_target_pairs={{0,48},{16,32},{32,16},{48,0},{64,112},{80,96},{96,80},{112,64},{1... | collective-permute-start | bytes 614408 | tf_op jit(solution)/shard_map/ppermute | solution.py:65
  92.8 1.7 %collective-permute-start.37 = (bf16[400,256]{1,0:T(8,128)(2,1)S(1)}, bf16[400,256]{1,0:T(8,128)(2,1)S(1)}, u32[]{:S(2)}, u32[]{:S(2)}) collective-permute-start(bf16[400,256]{1,0:T(8,128)(2,1)S(1)} %add_z.7), channel_id=1, source_target_pairs={{0,64},{16,80},{32,96},{48,112},{64,0},{80,16},{96,32},{112,48},{1... | collective-permute-start | bytes 614408 | tf_op jit(solution)/shard_map/ppermute | solution.py:61
  94.6 1.8 %collective-permute-start.34 = (bf16[400,256]{1,0:T(8,128)(2,1)S(1)}, bf16[400,256]{1,0:T(8,128)(2,1)S(1)}, u32[]{:S(2)}, u32[]{:S(2)}) collective-permute-start(bf16[400,256]{1,0:T(8,128)(2,1)S(1)} %add_z.6), channel_id=1, source_target_pairs={{0,32},{16,48},{32,0},{48,16},{64,96},{80,112},{96,64},{112,80},{1... | collective-permute-start | bytes 614408 | tf_op jit(solution)/shard_map/ppermute | solution.py:65
  96.4 2.7 %prepare_gradient.1.refs_6_.refs_4_.refs_7_.refs_11_ = bf16[4,256,2304]{2,1,0:T(8,128)(2,1)S(1)} custom-call(bf16[4,384,256]{2,1,0:T(8,128)(2,1)S(1)} %get-tuple-element.51.early, bf16[4,384,256]{2,1,0:T(8,128)(2,1)S(1)} %get-tuple-element.53.late, bf16[768,2304]{1,0:T(8,128)(2,1)S(1)} %get-tuple-element.66.e.refs_1_.refs_4_.refs_8_, ...), custom_call_target="tpu_custom_call" | custom-call | flops 1811939328 | bytes 4529848 | tf_op jit(solution)/shard_map/prepare_gradient/pallas_call | solution.py:47
  99.1 1.5 %collective-permute-done.32.refs_2_ = bf16[400,256]{1,0:T(8,128)(2,1)S(1)} collective-permute-done((bf16[400,256]{1,0:T(8,128)(2,1)S(1)}, bf16[400,256]{1,0:T(8,128)(2,1)S(1)}, u32[]{:S(2)}, u32[]{:S(2)}) %collective-permute-start.32) | collective-permute-done | bytes 204832 | tf_op jit(solution)/shard_map/ppermute | solution.py:65
  100.6 1.5 %collective-permute-done.34.refs_3_ = bf16[400,256]{1,0:T(8,128)(2,1)S(1)} collective-permute-done((bf16[400,256]{1,0:T(8,128)(2,1)S(1)}, bf16[400,256]{1,0:T(8,128)(2,1)S(1)}, u32[]{:S(2)}, u32[]{:S(2)}) %collective-permute-start.34) | collective-permute-done | bytes 204832 | tf_op jit(solution)/shard_map/ppermute | solution.py:65
  102.3 1.9 %collective-permute-start.41 = (bf16[400,256]{1,0:T(8,128)(2,1)S(1)}, bf16[400,256]{1,0:T(8,128)(2,1)S(1)}, u32[]{:S(2)}, u32[]{:S(2)}) collective-permute-start(bf16[400,256]{1,0:T(8,128)(2,1)S(1)} %latent_grad.1.refs_0_), channel_id=1, source_target_pairs={{0,64},{16,80},{32,96},{48,112},{64,0},{80,16},{96,32},{112,48},{1... | collective-permute-start | bytes 614408 | tf_op jit(solution)/shard_map/ppermute | solution.py:61
  104.3 1.7 %collective-permute-start.39 = (bf16[400,256]{1,0:T(8,128)(2,1)S(1)}, bf16[400,256]{1,0:T(8,128)(2,1)S(1)}, u32[]{:S(2)}, u32[]{:S(2)}) collective-permute-start(bf16[400,256]{1,0:T(8,128)(2,1)S(1)} %latent_grad.1.refs_0_), channel_id=1, source_target_pairs={{0,32},{16,48},{32,0},{48,16},{64,96},{80,112},{96,64},{112,80},{1... | collective-permute-start | bytes 614408 | tf_op jit(solution)/shard_map/ppermute | solution.py:65
  106.0 1.3 %collective-permute-start.40 = (bf16[400,256]{1,0:T(8,128)(2,1)S(1)}, bf16[400,256]{1,0:T(8,128)(2,1)S(1)}, u32[]{:S(2)}, u32[]{:S(2)}) collective-permute-start(bf16[400,256]{1,0:T(8,128)(2,1)S(1)} %latent_grad.1.refs_0_), channel_id=1, source_target_pairs={{0,48},{16,32},{32,16},{48,0},{64,112},{80,96},{96,80},{112,64},{1... | collective-permute-start | bytes 614408 | tf_op jit(solution)/shard_map/ppermute | solution.py:65
  107.8 2.2 %gradient.3 = (bf16[2048,2304]{1,0:T(8,128)(2,1)}, f32[1,2304]{1,0:T(1,128)}) custom-call(bf16[4,384,256]{2,1,0:T(8,128)(2,1)S(1)} %get-tuple-element.51.early, bf16[4,384,256]{2,1,0:T(8,128)(2,1)S(1)} %get-tuple-element.53.late, bf16[400,256]{1,0:T(8,128)(2,1)S(1)} %latent_grad.1.refs_0_, bf16[768,2304]{1,0:T(8,128)(2,1)S(1)} %get-tuple-element.66.e.refs_1_.refs_4_.refs_8_, ...), custom_call_target="tpu_custom_call" | custom-call | flops 905969664 | bytes 2264924 | tf_op jit(solution)/shard_map/gradient/pallas_call | solution.py:47
  110.0 1.9 %collective-permute-start.44 = (bf16[400,256]{1,0:T(8,128)(2,1)S(1)}, bf16[400,256]{1,0:T(8,128)(2,1)S(1)}, u32[]{:S(2)}, u32[]{:S(2)}) collective-permute-start(bf16[400,256]{1,0:T(8,128)(2,1)S(1)} %collective-permute-done.41.refs_0_.refs_4_), channel_id=1, source_target_pairs={{0,48},{16,32},{32,16},{48,0},{64,112},{80,96},{96,80},{112,64},{1... | collective-permute-start | bytes 614408 | tf_op jit(solution)/shard_map/ppermute | solution.py:65
  113.4 1.5 %collective-permute-start.43 = (bf16[400,256]{1,0:T(8,128)(2,1)S(1)}, bf16[400,256]{1,0:T(8,128)(2,1)S(1)}, u32[]{:S(2)}, u32[]{:S(2)}) collective-permute-start(bf16[400,256]{1,0:T(8,128)(2,1)S(1)} %collective-permute-done.39.refs_1_.refs_2_), channel_id=1, source_target_pairs={{0,64},{16,80},{32,96},{48,112},{64,0},{80,16},{96,32},{112,48},{1... | collective-permute-start | bytes 614408 | tf_op jit(solution)/shard_map/ppermute | solution.py:61
  114.9 1.4 %collective-permute-done.40.refs_3_ = bf16[400,256]{1,0:T(8,128)(2,1)S(1)} collective-permute-done((bf16[400,256]{1,0:T(8,128)(2,1)S(1)}, bf16[400,256]{1,0:T(8,128)(2,1)S(1)}, u32[]{:S(2)}, u32[]{:S(2)}) %collective-permute-start.40) | collective-permute-done | bytes 204832 | tf_op jit(solution)/shard_map/ppermute | solution.py:65
  116.4 4.6 %gradient.4.refs_12_ = bf16[2048,2304]{1,0:T(8,128)(2,1)} custom-call(bf16[4,384,256]{2,1,0:T(8,128)(2,1)S(1)} %get-tuple-element.51.early, bf16[4,384,256]{2,1,0:T(8,128)(2,1)S(1)} %get-tuple-element.53.late, bf16[400,256]{1,0:T(8,128)(2,1)S(1)} %collective-permute-done.41.refs_0_.refs_4_, ...), custom_call_target="tpu_custom_call", output_to_operand_aliasing={{}: (10, {})} | custom-call | flops 3623878656 | bytes 9059696 | tf_op jit(solution)/shard_map/gradient/pallas_call | solution.py:47
  121.1 3.0 %gradient.5 = (bf16[2048,2304]{1,0:T(8,128)(2,1)}, f32[8,1,256]{2,1,0:T(1,128)}, f32[8,1,256]{2,1,0:T(1,128)}) custom-call(bf16[4,384,256]{2,1,0:T(8,128)(2,1)S(1)} %get-tuple-element.51.early, bf16[4,384,256]{2,1,0:T(8,128)(2,1)S(1)} %get-tuple-element.53.late, bf16[400,256]{1,0:T(8,128)(2,1)S(1)} %latent_grad.1.refs_0_, ...), custom_call_target="tpu_custom_call", output_to_operand_aliasing={{0}: (14, {})} | custom-call | flops 2717908992 | bytes 6794772 | tf_op jit(solution)/shard_map/gradient/pallas_call | solution.py:47
  (75 shorter events, 15.5 us)
Async XLA Ops:
  5.8 9.8 %copy-start.1 = (bf16[1,2048,2304]{2,1,0:T(8,128)(2,1)S(1)}, bf16[1,2048,2304]{2,1,0:T(8,128)(2,1)}, u32[]{:S(2)}) copy-start(bf16[1,2048,2304]{2,1,0:T(8,128)(2,1)} %param.5) | copy-start | bytes 28311556
  7.8 11.5 %collective-permute-start.4 = (bf16[384,256]{1,0:T(8,128)(2,1)S(1)}, bf16[384,256]{1,0:T(8,128)(2,1)S(1)}, u32[]{:S(2)}, u32[]{:S(2)}) collective-permute-start(bf16[384,256]{1,0:T(8,128)(2,1)S(1)} %get-tuple-element.49), channel_id=1, source_target_pairs={{0,16},{16,0},{32,48},{48,32},{64,80},{80,64},{96,112},{112,96},{1... | collective-permute-start | bytes 589832 | tf_op jit(solution)/shard_map/ppermute | solution.py:65
  9.9 9.5 %collective-permute-start.5 = (bf16[384,256]{1,0:T(8,128)(2,1)S(1)}, bf16[384,256]{1,0:T(8,128)(2,1)S(1)}, u32[]{:S(2)}, u32[]{:S(2)}) collective-permute-start(bf16[384,256]{1,0:T(8,128)(2,1)S(1)} %get-tuple-element.50), channel_id=1, source_target_pairs={{0,48},{16,32},{32,16},{48,0},{64,112},{80,96},{96,80},{112,64},{1... | collective-permute-start | bytes 589832 | tf_op jit(solution)/shard_map/ppermute | solution.py:65
  12.4 8.4 %collective-permute-start.2 = (bf16[384,256]{1,0:T(8,128)(2,1)S(1)}, bf16[384,256]{1,0:T(8,128)(2,1)S(1)}, u32[]{:S(2)}, u32[]{:S(2)}) collective-permute-start(bf16[384,256]{1,0:T(8,128)(2,1)S(1)} %get-tuple-element.47), channel_id=1, source_target_pairs={{0,64},{16,80},{32,96},{48,112},{64,0},{80,16},{96,32},{112,48},{1... | collective-permute-start | bytes 589832 | tf_op jit(solution)/shard_map/ppermute | solution.py:61
  15.6 14.2 %copy-start.4 = (f32[2048]{0:T(1024)S(1)}, f32[2048]{0:T(1024)}, u32[]{:S(2)}) copy-start(f32[2048]{0:T(1024)} %param.6) | copy-start | bytes 24580
  17.6 6.2 %collective-permute-start = (bf16[384,256]{1,0:T(8,128)(2,1)S(1)}, bf16[384,256]{1,0:T(8,128)(2,1)S(1)}, u32[]{:S(2)}, u32[]{:S(2)}) collective-permute-start(bf16[384,256]{1,0:T(8,128)(2,1)S(1)} %get-tuple-element.44), channel_id=1, source_target_pairs={{0,16},{16,0},{32,48},{48,32},{64,80},{80,64},{96,112},{112,96},{1... | collective-permute-start | bytes 589832 | tf_op jit(solution)/shard_map/ppermute | solution.py:65
  18.7 11.1 %collective-permute-start.1 = (bf16[384,256]{1,0:T(8,128)(2,1)S(1)}, bf16[384,256]{1,0:T(8,128)(2,1)S(1)}, u32[]{:S(2)}, u32[]{:S(2)}) collective-permute-start(bf16[384,256]{1,0:T(8,128)(2,1)S(1)} %get-tuple-element.45), channel_id=1, source_target_pairs={{0,48},{16,32},{32,16},{48,0},{64,112},{80,96},{96,80},{112,64},{1... | collective-permute-start | bytes 589832 | tf_op jit(solution)/shard_map/ppermute | solution.py:65
  19.4 10.4 %collective-permute-start.6 = (bf16[384,256]{1,0:T(8,128)(2,1)S(1)}, bf16[384,256]{1,0:T(8,128)(2,1)S(1)}, u32[]{:S(2)}, u32[]{:S(2)}) collective-permute-start(bf16[384,256]{1,0:T(8,128)(2,1)S(1)} %add_z.5), channel_id=1, source_target_pairs={{0,64},{16,80},{32,96},{48,112},{64,0},{80,16},{96,32},{112,48},{1... | collective-permute-start | bytes 589832 | tf_op jit(solution)/shard_map/ppermute | solution.py:61
  20.9 9.0 %collective-permute-start.3 = (bf16[384,256]{1,0:T(8,128)(2,1)S(1)}, bf16[384,256]{1,0:T(8,128)(2,1)S(1)}, u32[]{:S(2)}, u32[]{:S(2)}) collective-permute-start(bf16[384,256]{1,0:T(8,128)(2,1)S(1)} %add_z.4), channel_id=1, source_target_pairs={{0,32},{16,48},{32,0},{48,16},{64,96},{80,112},{96,64},{112,80},{1... | collective-permute-start | bytes 589832 | tf_op jit(solution)/shard_map/ppermute | solution.py:65
  30.0 7.3 %collective-permute-start.10 = (bf16[384,256]{1,0:T(8,128)(2,1)S(1)}, bf16[384,256]{1,0:T(8,128)(2,1)S(1)}, u32[]{:S(2)}, u32[]{:S(2)}) collective-permute-start(bf16[384,256]{1,0:T(8,128)(2,1)S(1)} %activate.1.refs_0_.refs_5_), channel_id=1, source_target_pairs={{0,64},{16,80},{32,96},{48,112},{64,0},{80,16},{96,32},{112,48},{1... | collective-permute-start | bytes 589832 | tf_op jit(solution)/shard_map/ppermute | solution.py:61
  30.7 9.3 %collective-permute-start.8 = (bf16[384,256]{1,0:T(8,128)(2,1)S(1)}, bf16[384,256]{1,0:T(8,128)(2,1)S(1)}, u32[]{:S(2)}, u32[]{:S(2)}) collective-permute-start(bf16[384,256]{1,0:T(8,128)(2,1)S(1)} %activate.1.refs_0_.refs_5_), channel_id=1, source_target_pairs={{0,32},{16,48},{32,0},{48,16},{64,96},{80,112},{96,64},{112,80},{1... | collective-permute-start | bytes 589832 | tf_op jit(solution)/shard_map/ppermute | solution.py:65
  33.1 9.5 %collective-permute-start.9 = (bf16[384,256]{1,0:T(8,128)(2,1)S(1)}, bf16[384,256]{1,0:T(8,128)(2,1)S(1)}, u32[]{:S(2)}, u32[]{:S(2)}) collective-permute-start(bf16[384,256]{1,0:T(8,128)(2,1)S(1)} %activate.1.refs_0_.refs_5_), channel_id=1, source_target_pairs={{0,48},{16,32},{32,16},{48,0},{64,112},{80,96},{96,80},{112,64},{1... | collective-permute-start | bytes 589832 | tf_op jit(solution)/shard_map/ppermute | solution.py:65
  34.4 8.2 %collective-permute-start.7 = (bf16[384,256]{1,0:T(8,128)(2,1)S(1)}, bf16[384,256]{1,0:T(8,128)(2,1)S(1)}, u32[]{:S(2)}, u32[]{:S(2)}) collective-permute-start(bf16[384,256]{1,0:T(8,128)(2,1)S(1)} %activate.1.refs_0_.refs_5_), channel_id=1, source_target_pairs={{0,16},{16,0},{32,48},{48,32},{64,80},{80,64},{96,112},{112,96},{1... | collective-permute-start | bytes 589832 | tf_op jit(solution)/shard_map/ppermute | solution.py:65
  37.2 7.4 %collective-permute-start.13 = (bf16[384,256]{1,0:T(8,128)(2,1)S(1)}, bf16[384,256]{1,0:T(8,128)(2,1)S(1)}, u32[]{:S(2)}, u32[]{:S(2)}) collective-permute-start(bf16[384,256]{1,0:T(8,128)(2,1)S(1)} %collective-permute-done.10.refs_0_), channel_id=1, source_target_pairs={{0,48},{16,32},{32,16},{48,0},{64,112},{80,96},{96,80},{112,64},{1... | collective-permute-start | bytes 589832 | tf_op jit(solution)/shard_map/ppermute | solution.py:65
  38.5 6.1 %collective-permute-start.11 = (bf16[384,256]{1,0:T(8,128)(2,1)S(1)}, bf16[384,256]{1,0:T(8,128)(2,1)S(1)}, u32[]{:S(2)}, u32[]{:S(2)}) collective-permute-start(bf16[384,256]{1,0:T(8,128)(2,1)S(1)} %collective-permute-done.10.refs_0_), channel_id=1, source_target_pairs={{0,16},{16,0},{32,48},{48,32},{64,80},{80,64},{96,112},{112,96},{1... | collective-permute-start | bytes 589832 | tf_op jit(solution)/shard_map/ppermute | solution.py:65
  40.0 7.2 %collective-permute-start.12 = (bf16[384,256]{1,0:T(8,128)(2,1)S(1)}, bf16[384,256]{1,0:T(8,128)(2,1)S(1)}, u32[]{:S(2)}, u32[]{:S(2)}) collective-permute-start(bf16[384,256]{1,0:T(8,128)(2,1)S(1)} %collective-permute-done.8.refs_2_), channel_id=1, source_target_pairs={{0,64},{16,80},{32,96},{48,112},{64,0},{80,16},{96,32},{112,48},{1... | collective-permute-start | bytes 589832 | tf_op jit(solution)/shard_map/ppermute | solution.py:61
  49.2 2.5 %collective-permute-start.14 = (bf16[192,2304]{1,0:T(8,128)(2,1)S(1)}, bf16[192,2304]{1,0:T(8,128)(2,1)S(1)}, u32[]{:S(2)}, u32[]{:S(2)}) collective-permute-start(bf16[192,2304]{1,0:T(8,128)(2,1)S(1)} %get-tuple-element.55), channel_id=1, source_target_pairs={{0,1},{1,0},{2,3},{3,2},{4,5},{5,4},{6,7},{7,6},{8,9},{9,8},{10,11... | collective-permute-start | bytes 2654216 | tf_op jit(solution)/shard_map/ppermute | solution.py:69
  52.0 6.2 %collective-permute-start.17 = (bf16[24,2304]{1,0:T(8,128)(2,1)S(1)}, bf16[24,2304]{1,0:T(8,128)(2,1)S(1)}, u32[]{:S(2)}, u32[]{:S(2)}) collective-permute-start(bf16[24,2304]{1,0:T(8,128)(2,1)S(1)} %get-tuple-element.60), channel_id=1, source_target_pairs={{0,8},{1,9},{2,10},{3,11},{4,12},{5,13},{6,14},{7,15},{8,0},{9,1},... | collective-permute-start | bytes 331784 | tf_op jit(solution)/shard_map/ppermute | solution.py:73
  53.4 8.0 %collective-permute-start.19 = (bf16[24,2304]{1,0:T(8,128)(2,1)S(1)}, bf16[24,2304]{1,0:T(8,128)(2,1)S(1)}, u32[]{:S(2)}, u32[]{:S(2)}) collective-permute-start(bf16[24,2304]{1,0:T(8,128)(2,1)S(1)} %get-tuple-element.62), channel_id=1, source_target_pairs={{0,2},{1,3},{2,0},{3,1},{4,6},{5,7},{6,4},{7,5},{8,10},{9,11},{10,... | collective-permute-start | bytes 331784 | tf_op jit(solution)/shard_map/ppermute | solution.py:77
  54.9 6.5 %collective-permute-start.20 = (bf16[24,2304]{1,0:T(8,128)(2,1)S(1)}, bf16[24,2304]{1,0:T(8,128)(2,1)S(1)}, u32[]{:S(2)}, u32[]{:S(2)}) collective-permute-start(bf16[24,2304]{1,0:T(8,128)(2,1)S(1)} %get-tuple-element.63), channel_id=1, source_target_pairs={{0,6},{1,7},{2,4},{3,5},{4,2},{5,3},{6,0},{7,1},{8,14},{9,15},{10,... | collective-permute-start | bytes 331784 | tf_op jit(solution)/shard_map/ppermute | solution.py:77
  57.0 7.8 %collective-permute-start.15 = (bf16[24,2304]{1,0:T(8,128)(2,1)S(1)}, bf16[24,2304]{1,0:T(8,128)(2,1)S(1)}, u32[]{:S(2)}, u32[]{:S(2)}) collective-permute-start(bf16[24,2304]{1,0:T(8,128)(2,1)S(1)} %get-tuple-element.57), channel_id=1, source_target_pairs={{0,2},{1,3},{2,0},{3,1},{4,6},{5,7},{6,4},{7,5},{8,10},{9,11},{10,... | collective-permute-start | bytes 331784 | tf_op jit(solution)/shard_map/ppermute | solution.py:77
  57.6 8.1 %collective-permute-start.16 = (bf16[24,2304]{1,0:T(8,128)(2,1)S(1)}, bf16[24,2304]{1,0:T(8,128)(2,1)S(1)}, u32[]{:S(2)}, u32[]{:S(2)}) collective-permute-start(bf16[24,2304]{1,0:T(8,128)(2,1)S(1)} %get-tuple-element.58), channel_id=1, source_target_pairs={{0,6},{1,7},{2,4},{3,5},{4,2},{5,3},{6,0},{7,1},{8,14},{9,15},{10,... | collective-permute-start | bytes 331784 | tf_op jit(solution)/shard_map/ppermute | solution.py:77
  58.2 7.4 %collective-permute-start.18 = (bf16[24,2304]{1,0:T(8,128)(2,1)S(1)}, bf16[24,2304]{1,0:T(8,128)(2,1)S(1)}, u32[]{:S(2)}, u32[]{:S(2)}) collective-permute-start(bf16[24,2304]{1,0:T(8,128)(2,1)S(1)} %add_x.2), channel_id=1, source_target_pairs={{0,4},{1,5},{2,6},{3,7},{4,0},{5,1},{6,2},{7,3},{8,12},{9,13},{10,... | collective-permute-start | bytes 331784 | tf_op jit(solution)/shard_map/ppermute | solution.py:77
  61.4 4.8 %copy-start.3 = (f32[1,2304]{1,0:T(1,128)S(1)}, f32[1,2304]{1,0:T(1,128)}, u32[]{:S(2)}) copy-start(f32[1,2304]{1,0:T(1,128)} %refs_5_.1) | copy-start | bytes 27652
  61.4 4.8 %collective-permute-start.21 = (bf16[24,2304]{1,0:T(8,128)(2,1)S(1)}, bf16[24,2304]{1,0:T(8,128)(2,1)S(1)}, u32[]{:S(2)}, u32[]{:S(2)}) collective-permute-start(bf16[24,2304]{1,0:T(8,128)(2,1)S(1)} %add_x.3), channel_id=1, source_target_pairs={{0,8},{1,9},{2,10},{3,11},{4,12},{5,13},{6,14},{7,15},{8,0},{9,1},... | collective-permute-start | bytes 331784 | tf_op jit(solution)/shard_map/ppermute | solution.py:73
  66.4 4.8 %collective-permute-start.25 = (bf16[24,2304]{1,0:T(8,128)(2,1)S(1)}, bf16[24,2304]{1,0:T(8,128)(2,1)S(1)}, u32[]{:S(2)}, u32[]{:S(2)}) collective-permute-start(bf16[24,2304]{1,0:T(8,128)(2,1)S(1)} %error.1.refs_0_), channel_id=1, source_target_pairs={{0,8},{1,9},{2,10},{3,11},{4,12},{5,13},{6,14},{7,15},{8,0},{9,1},... | collective-permute-start | bytes 331784 | tf_op jit(solution)/shard_map/ppermute | solution.py:73
  67.2 7.7 %collective-permute-start.23 = (bf16[24,2304]{1,0:T(8,128)(2,1)S(1)}, bf16[24,2304]{1,0:T(8,128)(2,1)S(1)}, u32[]{:S(2)}, u32[]{:S(2)}) collective-permute-start(bf16[24,2304]{1,0:T(8,128)(2,1)S(1)} %error.1.refs_0_), channel_id=1, source_target_pairs={{0,4},{1,5},{2,6},{3,7},{4,0},{5,1},{6,2},{7,3},{8,12},{9,13},{10,... | collective-permute-start | bytes 331784 | tf_op jit(solution)/shard_map/ppermute | solution.py:77
  69.3 6.3 %collective-permute-start.24 = (bf16[24,2304]{1,0:T(8,128)(2,1)S(1)}, bf16[24,2304]{1,0:T(8,128)(2,1)S(1)}, u32[]{:S(2)}, u32[]{:S(2)}) collective-permute-start(bf16[24,2304]{1,0:T(8,128)(2,1)S(1)} %error.1.refs_0_), channel_id=1, source_target_pairs={{0,6},{1,7},{2,4},{3,5},{4,2},{5,3},{6,0},{7,1},{8,14},{9,15},{10,... | collective-permute-start | bytes 331784 | tf_op jit(solution)/shard_map/ppermute | solution.py:77
  70.4 5.2 %collective-permute-start.22 = (bf16[24,2304]{1,0:T(8,128)(2,1)S(1)}, bf16[24,2304]{1,0:T(8,128)(2,1)S(1)}, u32[]{:S(2)}, u32[]{:S(2)}) collective-permute-start(bf16[24,2304]{1,0:T(8,128)(2,1)S(1)} %error.1.refs_0_), channel_id=1, source_target_pairs={{0,2},{1,3},{2,0},{3,1},{4,6},{5,7},{6,4},{7,5},{8,10},{9,11},{10,... | collective-permute-start | bytes 331784 | tf_op jit(solution)/shard_map/ppermute | solution.py:77
  71.2 6.3 %collective-permute-start.28 = (bf16[24,2304]{1,0:T(8,128)(2,1)S(1)}, bf16[24,2304]{1,0:T(8,128)(2,1)S(1)}, u32[]{:S(2)}, u32[]{:S(2)}) collective-permute-start(bf16[24,2304]{1,0:T(8,128)(2,1)S(1)} %collective-permute-done.25.refs_0_), channel_id=1, source_target_pairs={{0,6},{1,7},{2,4},{3,5},{4,2},{5,3},{6,0},{7,1},{8,14},{9,15},{10,... | collective-permute-start | bytes 331784 | tf_op jit(solution)/shard_map/ppermute | solution.py:77
  74.8 4.7 %collective-permute-start.26 = (bf16[24,2304]{1,0:T(8,128)(2,1)S(1)}, bf16[24,2304]{1,0:T(8,128)(2,1)S(1)}, u32[]{:S(2)}, u32[]{:S(2)}) collective-permute-start(bf16[24,2304]{1,0:T(8,128)(2,1)S(1)} %collective-permute-done.25.refs_0_), channel_id=1, source_target_pairs={{0,2},{1,3},{2,0},{3,1},{4,6},{5,7},{6,4},{7,5},{8,10},{9,11},{10,... | collective-permute-start | bytes 331784 | tf_op jit(solution)/shard_map/ppermute | solution.py:77
  74.8 4.7 %collective-permute-start.27 = (bf16[24,2304]{1,0:T(8,128)(2,1)S(1)}, bf16[24,2304]{1,0:T(8,128)(2,1)S(1)}, u32[]{:S(2)}, u32[]{:S(2)}) collective-permute-start(bf16[24,2304]{1,0:T(8,128)(2,1)S(1)} %collective-permute-done.23.refs_2_), channel_id=1, source_target_pairs={{0,8},{1,9},{2,10},{3,11},{4,12},{5,13},{6,14},{7,15},{8,0},{9,1},... | collective-permute-start | bytes 331784 | tf_op jit(solution)/shard_map/ppermute | solution.py:73
  75.8 4.0 %collective-permute-start.29 = (bf16[96,2304]{1,0:T(8,128)(2,1)S(1)}, bf16[96,2304]{1,0:T(8,128)(2,1)S(1)}, u32[]{:S(2)}, u32[]{:S(2)}) collective-permute-start(bf16[96,2304]{1,0:T(8,128)(2,1)S(1)} %join.2.refs_0_), channel_id=1, source_target_pairs={{0,1},{1,0},{2,3},{3,2},{4,5},{5,4},{6,7},{7,6},{8,9},{9,8},{10,11... | collective-permute-start | bytes 1327112 | tf_op jit(solution)/shard_map/ppermute | solution.py:69
  79.7 1.9 %collective-permute-start.30 = (bf16[96,2304]{1,0:T(8,128)(2,1)S(1)}, bf16[96,2304]{1,0:T(8,128)(2,1)S(1)}, u32[]{:S(2)}, u32[]{:S(2)}) collective-permute-start(bf16[96,2304]{1,0:T(8,128)(2,1)S(1)} %join.3.refs_1_), channel_id=1, source_target_pairs={{0,1},{1,0},{2,3},{3,2},{4,5},{5,4},{6,7},{7,6},{8,9},{9,8},{10,11... | collective-permute-start | bytes 1327112 | tf_op jit(solution)/shard_map/ppermute | solution.py:69
  83.7 9.0 %collective-permute-start.35 = (bf16[400,256]{1,0:T(8,128)(2,1)S(1)}, bf16[400,256]{1,0:T(8,128)(2,1)S(1)}, u32[]{:S(2)}, u32[]{:S(2)}) collective-permute-start(bf16[400,256]{1,0:T(8,128)(2,1)S(1)} %get-tuple-element.73), channel_id=1, source_target_pairs={{0,16},{16,0},{32,48},{48,32},{64,80},{80,64},{96,112},{112,96},{1... | collective-permute-start | bytes 614408 | tf_op jit(solution)/shard_map/ppermute | solution.py:65
  84.4 8.3 %collective-permute-start.36 = (bf16[400,256]{1,0:T(8,128)(2,1)S(1)}, bf16[400,256]{1,0:T(8,128)(2,1)S(1)}, u32[]{:S(2)}, u32[]{:S(2)}) collective-permute-start(bf16[400,256]{1,0:T(8,128)(2,1)S(1)} %get-tuple-element.74), channel_id=1, source_target_pairs={{0,48},{16,32},{32,16},{48,0},{64,112},{80,96},{96,80},{112,64},{1... | collective-permute-start | bytes 614408 | tf_op jit(solution)/shard_map/ppermute | solution.py:65
  86.1 8.4 %collective-permute-start.33 = (bf16[400,256]{1,0:T(8,128)(2,1)S(1)}, bf16[400,256]{1,0:T(8,128)(2,1)S(1)}, u32[]{:S(2)}, u32[]{:S(2)}) collective-permute-start(bf16[400,256]{1,0:T(8,128)(2,1)S(1)} %get-tuple-element.71), channel_id=1, source_target_pairs={{0,64},{16,80},{32,96},{48,112},{64,0},{80,16},{96,32},{112,48},{1... | collective-permute-start | bytes 614408 | tf_op jit(solution)/shard_map/ppermute | solution.py:61
  89.9 9.2 %collective-permute-start.31 = (bf16[400,256]{1,0:T(8,128)(2,1)S(1)}, bf16[400,256]{1,0:T(8,128)(2,1)S(1)}, u32[]{:S(2)}, u32[]{:S(2)}) collective-permute-start(bf16[400,256]{1,0:T(8,128)(2,1)S(1)} %get-tuple-element.68), channel_id=1, source_target_pairs={{0,16},{16,0},{32,48},{48,32},{64,80},{80,64},{96,112},{112,96},{1... | collective-permute-start | bytes 614408 | tf_op jit(solution)/shard_map/ppermute | solution.py:65
  90.3 10.3 %collective-permute-start.32 = (bf16[400,256]{1,0:T(8,128)(2,1)S(1)}, bf16[400,256]{1,0:T(8,128)(2,1)S(1)}, u32[]{:S(2)}, u32[]{:S(2)}) collective-permute-start(bf16[400,256]{1,0:T(8,128)(2,1)S(1)} %get-tuple-element.69), channel_id=1, source_target_pairs={{0,48},{16,32},{32,16},{48,0},{64,112},{80,96},{96,80},{112,64},{1... | collective-permute-start | bytes 614408 | tf_op jit(solution)/shard_map/ppermute | solution.py:65
  92.8 7.9 %collective-permute-start.37 = (bf16[400,256]{1,0:T(8,128)(2,1)S(1)}, bf16[400,256]{1,0:T(8,128)(2,1)S(1)}, u32[]{:S(2)}, u32[]{:S(2)}) collective-permute-start(bf16[400,256]{1,0:T(8,128)(2,1)S(1)} %add_z.7), channel_id=1, source_target_pairs={{0,64},{16,80},{32,96},{48,112},{64,0},{80,16},{96,32},{112,48},{1... | collective-permute-start | bytes 614408 | tf_op jit(solution)/shard_map/ppermute | solution.py:61
  94.6 7.6 %collective-permute-start.34 = (bf16[400,256]{1,0:T(8,128)(2,1)S(1)}, bf16[400,256]{1,0:T(8,128)(2,1)S(1)}, u32[]{:S(2)}, u32[]{:S(2)}) collective-permute-start(bf16[400,256]{1,0:T(8,128)(2,1)S(1)} %add_z.6), channel_id=1, source_target_pairs={{0,32},{16,48},{32,0},{48,16},{64,96},{80,112},{96,64},{112,80},{1... | collective-permute-start | bytes 614408 | tf_op jit(solution)/shard_map/ppermute | solution.py:65
  102.3 7.6 %collective-permute-start.41 = (bf16[400,256]{1,0:T(8,128)(2,1)S(1)}, bf16[400,256]{1,0:T(8,128)(2,1)S(1)}, u32[]{:S(2)}, u32[]{:S(2)}) collective-permute-start(bf16[400,256]{1,0:T(8,128)(2,1)S(1)} %latent_grad.1.refs_0_), channel_id=1, source_target_pairs={{0,64},{16,80},{32,96},{48,112},{64,0},{80,16},{96,32},{112,48},{1... | collective-permute-start | bytes 614408 | tf_op jit(solution)/shard_map/ppermute | solution.py:61
  104.3 9.2 %collective-permute-start.39 = (bf16[400,256]{1,0:T(8,128)(2,1)S(1)}, bf16[400,256]{1,0:T(8,128)(2,1)S(1)}, u32[]{:S(2)}, u32[]{:S(2)}) collective-permute-start(bf16[400,256]{1,0:T(8,128)(2,1)S(1)} %latent_grad.1.refs_0_), channel_id=1, source_target_pairs={{0,32},{16,48},{32,0},{48,16},{64,96},{80,112},{96,64},{112,80},{1... | collective-permute-start | bytes 614408 | tf_op jit(solution)/shard_map/ppermute | solution.py:65
  106.0 10.4 %collective-permute-start.40 = (bf16[400,256]{1,0:T(8,128)(2,1)S(1)}, bf16[400,256]{1,0:T(8,128)(2,1)S(1)}, u32[]{:S(2)}, u32[]{:S(2)}) collective-permute-start(bf16[400,256]{1,0:T(8,128)(2,1)S(1)} %latent_grad.1.refs_0_), channel_id=1, source_target_pairs={{0,48},{16,32},{32,16},{48,0},{64,112},{80,96},{96,80},{112,64},{1... | collective-permute-start | bytes 614408 | tf_op jit(solution)/shard_map/ppermute | solution.py:65
  107.3 9.1 %collective-permute-start.38 = (bf16[400,256]{1,0:T(8,128)(2,1)S(1)}, bf16[400,256]{1,0:T(8,128)(2,1)S(1)}, u32[]{:S(2)}, u32[]{:S(2)}) collective-permute-start(bf16[400,256]{1,0:T(8,128)(2,1)S(1)} %latent_grad.1.refs_0_), channel_id=1, source_target_pairs={{0,16},{16,0},{32,48},{48,32},{64,80},{80,64},{96,112},{112,96},{1... | collective-permute-start | bytes 614408 | tf_op jit(solution)/shard_map/ppermute | solution.py:65
  110.0 11.1 %collective-permute-start.44 = (bf16[400,256]{1,0:T(8,128)(2,1)S(1)}, bf16[400,256]{1,0:T(8,128)(2,1)S(1)}, u32[]{:S(2)}, u32[]{:S(2)}) collective-permute-start(bf16[400,256]{1,0:T(8,128)(2,1)S(1)} %collective-permute-done.41.refs_0_.refs_4_), channel_id=1, source_target_pairs={{0,48},{16,32},{32,16},{48,0},{64,112},{80,96},{96,80},{112,64},{1... | collective-permute-start | bytes 614408 | tf_op jit(solution)/shard_map/ppermute | solution.py:65
  111.8 9.2 %collective-permute-start.42 = (bf16[400,256]{1,0:T(8,128)(2,1)S(1)}, bf16[400,256]{1,0:T(8,128)(2,1)S(1)}, u32[]{:S(2)}, u32[]{:S(2)}) collective-permute-start(bf16[400,256]{1,0:T(8,128)(2,1)S(1)} %collective-permute-done.41.refs_0_.refs_4_), channel_id=1, source_target_pairs={{0,16},{16,0},{32,48},{48,32},{64,80},{80,64},{96,112},{112,96},{1... | collective-permute-start | bytes 614408 | tf_op jit(solution)/shard_map/ppermute | solution.py:65
  113.4 7.6 %collective-permute-start.43 = (bf16[400,256]{1,0:T(8,128)(2,1)S(1)}, bf16[400,256]{1,0:T(8,128)(2,1)S(1)}, u32[]{:S(2)}, u32[]{:S(2)}) collective-permute-start(bf16[400,256]{1,0:T(8,128)(2,1)S(1)} %collective-permute-done.39.refs_1_.refs_2_), channel_id=1, source_target_pairs={{0,64},{16,80},{32,96},{48,112},{64,0},{80,16},{96,32},{112,48},{1... | collective-permute-start | bytes 614408 | tf_op jit(solution)/shard_map/ppermute | solution.py:61
  (2 other events, 5.2 us)

commit v5 on v4

--- a/solution.py
+++ b/solution.py
@@ -15,15 +15,16 @@
 LAYERS = 8
 BLOCK = F // LAYERS
 CHIPS = 8
+QUARTER = HALF // 2
 PIECE = HALF // CHIPS
 EXTRA = 16
 GROUPS = ((0,), (4, 2, 1, 3), (5, 7, 6))
-READY = (4, 5, 6, 7)
+READY = (1, 2, 3, 4, 5, 6, 7)
+SENT = ((5, 7, 6), (1, 3), (4, 0, 2))
+BACK = ((0, 1, 2, 3), (4, 5, 7), (6,))
 SCALE = penalty_weight / ROWS
 MATMUL = 2 * ROWS * F * D
 
-NEAR = (0, 1, 2, 3)
-FAR = (4, 5, 6, 7)
 SIDES = (1, 3)
 
 f32 = jnp.float32
@@ -103,32 +104,38 @@
     return lax.dot_general(rows, weights, NT, preferred_element_type=f32).astype(bf16)
 
 
-def encode_far(acts, weights):
+def encode_first(acts, weights, blocks):
     def kernel(a, w, *refs):
-        rows = refs[4]
-        c = lax.axis_index("latent") & 1
-        for k, source in enumerate((c, 1 - c)):
-            rows[k * HALF : (k + 1) * HALF] = a[pl.ds(pl.multiple_of(source * HALF, HALF), HALF)]
-        for k, r in enumerate(FAR):
+        rows = refs[-1]
+        latent = lax.axis_index("latent")
+        for k in range(4):
+            at = ((latent & 1) ^ (k // 2)) * HALF + ((latent >> 3) ^ (k % 2)) * QUARTER
+            rows[k * QUARTER : (k + 1) * QUARTER] = a[pl.ds(pl.multiple_of(at, QUARTER), QUARTER)]
+        for k, r in enumerate(blocks):
             refs[k][...] = product(rows[...], w[block_rows(r)])
 
     return call(
         kernel,
         (acts, weights),
-        [half(ROWS, BLOCK)] * 4 + [half(ROWS, D)],
-        "encode_far",
-        MATMUL // 2,
+        [half(ROWS, BLOCK)] * len(blocks) + [half(ROWS, D)],
+        "encode_first",
+        MATMUL * len(blocks) // LAYERS,
         mib=8,
     )
 
 
-def encode_near(rows, weights):
+def encode(rows, weights, blocks):
     def kernel(a, w, *outs):
-        for k, r in enumerate(NEAR):
-            outs[k][...] = product(a[...], w[block_rows(r)])
-
-    return call(
-        kernel, (rows, weights), [half(ROWS, BLOCK)] * 4, "encode_near", MATMUL // 2, mib=8
+        for out, r in zip(outs, blocks):
+            out[...] = product(a[...], w[block_rows(r)])
+
+    return call(
+        kernel,
+        (rows, weights),
+        [half(ROWS, BLOCK)] * len(blocks),
+        "encode",
+        MATMUL * len(blocks) // LAYERS,
+        mib=8,
     )
 
 
@@ -148,10 +155,10 @@
                 preferred_element_type=f32,
             )
             norms[r] = jnp.sqrt(total + norm_eps)
-        value = a[:HALF].astype(f32)
-        for k in range(CHIPS):
+        value = a[:QUARTER].astype(f32)
+        for k in range(4):
             held[k] = value[k * PIECE : (k + 1) * PIECE]
-        piece[...] = held[chip_of(0)].astype(bf16)
+        piece[...] = held[chip_of(0) & 3].astype(bf16)
 
     return call(
         kernel,
@@ -159,7 +166,7 @@
         [full(LAYERS, 8, BLOCK), half(PIECE, D)],
         "prepare",
         1 << 30,
-        [pltpu.VMEM((CHIPS, PIECE, D), f32)],
+        [pltpu.VMEM((4, PIECE, D), f32)],
         8,
     )
 
@@ -195,56 +202,60 @@
     return call(kernel, (*terms, bias), half(ROWS, BLOCK), "activate", 1 << 20)
 
 
-def decode(active, weights, blocks, before=None, after=()):
+def decode(active, weights, blocks, before, last):
     width = 768
-
-    def kernel(*refs):
-        g, w, refs = refs[:4], refs[4], refs[5:]
-        if before is not None:
-            acc, lat, mine, other = refs
-        else:
-            lat, out = refs[len(after) :]
-        for k in range(4):
+    count = len(blocks)
+
+    def kernel(*refs):
+        g, w = refs[:count], refs[count]
+        lat, *outs = refs[count + 1 + len(before) :]
+        for k in range(count):
             x = g[k][...].astype(f32)
             lat[k] = (x * x).astype(bf16)
         for i in range(D // width):
             cols = slice(i * width, (i + 1) * width)
-            value = None if before is None else acc[:, cols]
+            value = refs[count + 1][:, cols] if before else None
             for k, r in enumerate(blocks):
                 term = jnp.dot(lat[k], w[block_rows(r), cols], preferred_element_type=f32)
                 value = term if value is None else value + term
-            if before is None:
-                out[:, cols] = value
+            if last:
+                for k in range(4):
+                    outs[k][:, cols] = value[k * QUARTER : (k + 1) * QUARTER].astype(bf16)
             else:
-                value = value.astype(bf16)
-                mine[:, cols] = value[:HALF]
-                other[:, cols] = value[HALF:]
-
-    shapes = [half(4, ROWS, BLOCK)]
-    if before is None:
-        shapes += [full(ROWS, D)]
-    else:
-        shapes += [half(HALF, D)] * 2
-    operands = (*active, weights, *after) + (() if before is None else (before,))
-    return call(kernel, operands, shapes, "decode", MATMUL // 2, mib=20)
+                outs[0][:, cols] = value
+
+    return call(
+        kernel,
+        (*active, weights, *before),
+        [half(count, ROWS, BLOCK)] + ([half(QUARTER, D)] * 4 if last else [full(ROWS, D)]),
+        "decode",
+        MATMUL * count // LAYERS,
+        mib=12,
+    )
+
+
+def latents_of(lats, r):
+    for lat, blocks in zip(lats, BACK):
+        if r in blocks:
+            return lat[blocks.index(r)]
 
 
 def add_core(own, other):
     def kernel(a, b, *refs):
-        outs, held = refs[:CHIPS], refs[CHIPS]
-        for k in range(CHIPS):
-            rows = slice(k * PIECE, (k + 1) * PIECE)
-            held[k] = a[rows].astype(f32) + b[rows].astype(f32)
-        for k in range(CHIPS):
-            outs[k][...] = held[chip_of(k)].astype(bf16)
+        outs, held = refs[:4], refs[4]
+        total = a[...].astype(f32) + b[...].astype(f32)
+        for k in range(4):
+            held[k] = total[k * PIECE : (k + 1) * PIECE]
+        for k in range(4):
+            outs[k][...] = held[chip_of(k) & 3].astype(bf16)
 
     return call(
         kernel,
         (own, other),
-        [half(PIECE, D)] * CHIPS,
+        [half(PIECE, D)] * 4,
         "add_core",
         1 << 20,
-        [pltpu.VMEM((CHIPS, PIECE, D), f32)],
+        [pltpu.VMEM((4, PIECE, D), f32)],
     )
 
 
@@ -287,40 +298,40 @@
     )
 
 
-def backward_far(parts, rows, norms, weights):
-    def kernel(*refs):
-        p, (x, n, w), outs, both = refs[:4], refs[4:7], refs[7:11], refs[11]
-        low = lax.axis_index("latent") >> 3
+def backward_first(parts, rows, norms, weights, blocks):
+    count = len(blocks)
+
+    def kernel(*refs):
+        p, (x, n, w), outs, both = refs[:4], refs[4:7], refs[7 : 7 + count], refs[7 + count]
         for k in range(4):
-            at = (k // 2) * HALF + (low ^ (k % 2)) * (HALF // 2)
-            both[pl.ds(pl.multiple_of(at, HALF // 2), HALF // 2)] = p[k][...]
-        for k, r in enumerate(FAR):
-            outs[k][:ROWS] = product(both[:ROWS], w[block_rows(r)])
-            outs[k][ROWS:] = split(n[r])
+            both[k * QUARTER : (k + 1) * QUARTER] = p[k][...]
+        for out, r in zip(outs, blocks):
+            out[:ROWS] = product(both[:ROWS], w[block_rows(r)])
+            out[ROWS:] = split(n[r])
         both[ROWS:] = x[...]
 
     return call(
         kernel,
         (*parts, rows, norms, weights),
-        [half(ROWS + EXTRA, BLOCK)] * 4 + [half(2 * ROWS, D)],
-        "backward_far",
-        MATMUL // 2,
+        [half(ROWS + EXTRA, BLOCK)] * count + [half(2 * ROWS, D)],
+        "backward_first",
+        MATMUL * count // LAYERS,
         mib=8,
     )
 
 
-def backward_near(both, norms, weights):
+def backward(both, norms, weights, blocks):
     def kernel(e, n, w, *outs):
-        for k, r in enumerate(NEAR):
-            outs[k][:ROWS] = product(e[:ROWS], w[block_rows(r)])
-            outs[k][ROWS:] = split(n[r])
+        for out, r in zip(outs, blocks):
+            out[:ROWS] = product(e[:ROWS], w[block_rows(r)])
+            out[ROWS:] = split(n[r])
 
     return call(
         kernel,
         (both, norms, weights),
-        [half(ROWS + EXTRA, BLOCK)] * 4,
-        "backward_near",
-        MATMUL // 2,
+        [half(ROWS + EXTRA, BLOCK)] * len(blocks),
+        "backward",
+        MATMUL * len(blocks) // LAYERS,
         mib=8,
     )
 
@@ -346,9 +357,10 @@
 def prepare_gradient(lats, both, norms, weights):
     width = 768
 
-    def kernel(early, late, e, n, w, out):
+    def kernel(*refs):
+        ls, (e, n, w, out) = refs[: len(BACK)], refs[len(BACK) :]
         for k, r in enumerate(READY):
-            l = early[r] if r < 4 else late[r - 4]
+            l = latents_of(ls, r)
             column = penalty(l, n[r])
             for i in range(D // width):
                 cols = slice(i * width, (i + 1) * width)
@@ -377,7 +389,8 @@
     used = tuple(range(LAYERS)) if last else blocks
     first = before is None
 
-    def kernel(early, late, *refs):
+    def kernel(*refs):
+        ls, refs = refs[: len(BACK)], refs[len(BACK) :]
         d = dict(zip(used, refs))
         e, n, w, p = refs[len(used) : len(used) + 4]
         refs = refs[len(used) + 4 + (not first) :]
@@ -399,7 +412,7 @@
             copy.start()
         for k, r in enumerate(blocks):
             if r not in READY:
-                l = early[r] if r < 4 else late[r - 4]
+                l = latents_of(ls, r)
                 lhs[:ROWS] = l
                 lhs[ROWS:] = d[r][:ROWS]
                 column = penalty(l, n[r])
@@ -469,29 +482,36 @@
     inputs, weights = acts[0], decoder[0]
     bias = enc_bias.reshape(LAYERS, 1, BLOCK)
 
-    *far, rows = encode_far(inputs, weights)
-    terms = list(encode_near(rows, weights)) + far
+    *out, rows = encode_first(inputs, weights, SENT[0])
+    for blocks in SENT[1:]:
+        out += encode(rows, weights, blocks)
+    terms = dict(zip(sum(SENT, ()), out))
     norms, piece = prepare(rows, weights)
     mine = activate(scatter(terms, move_z, move_y, add_z), bias)
     active = gather(mine, move_z, move_y)
-    lat_near, before = decode([active[r] for r in NEAR], weights, NEAR)
-    lat_far, here, there = decode([active[r] for r in FAR], weights, FAR, before)
-
-    pieces = add_core(here, move_core(there))
-    own = error(scatter(pieces, move_x, move_lo, add_x), dec_bias, piece)
+    lats, before = [], ()
+    for blocks in BACK:
+        last = blocks is BACK[-1]
+        lat, *before = decode([active[r] for r in blocks], weights, blocks, before, last)
+        lats.append(lat)
+
+    far, near = [add_core(before[k], move_core(before[2 + k])) for k in (1, 0)]
+    own = error(scatter([*near, *far], move_x, move_lo, add_x), dec_bias, piece)
     got = gather(own, move_x, move_lo)
-    here = [join([got[r] for r in blocks]) for blocks in (NEAR, FAR)]
-    errors = here + [move_core(x) for x in here]
-
-    *far, both = backward_far(errors, rows, norms, weights)
-    terms = list(backward_near(both, norms, weights)) + far
-    ready = prepare_gradient((lat_near, lat_far), both, norms, weights)
+    errors = [join([got[r + k] for k in range(4)]) for r in (0, 4)]
+    errors += [move_core(x) for x in errors]
+
+    *out, both = backward_first(errors, rows, norms, weights, SENT[0])
+    for blocks in SENT[1:]:
+        out += backward(both, norms, weights, blocks)
+    terms = dict(zip(sum(SENT, ()), out))
+    ready = prepare_gradient(lats, both, norms, weights)
     dpre = latent_grad(scatter(terms, move_z, move_y, add_z), mine, ready)
     dpres = gather(dpre, move_z, move_y)
     grad = None
     for i, blocks in enumerate(GROUPS):
         last = i == len(GROUPS) - 1
-        out = gradient((lat_near, lat_far), dpres, both, norms, weights, ready, blocks, grad, last)
+        out = gradient(lats, dpres, both, norms, weights, ready, blocks, grad, last)
         grad = out[0]
         if i == 0:
             dec_grad = out[1]

time: 125 us -> 122 us (0.976)
  waiting for transfers between devices: 27.4 us -> 22.8 us
  Pallas kernels: 28.6 us -> 30 us
    ppermute x20, waiting for transfers between devices: 12.5 us -> 9.51 us  [move_z(): return lax.ppermute(x, 'layer', [(i, i ^ r) for i in range(8)])]
    ppermute x8, starting transfers between devices: 14.9 us -> 16.8 us  [move_y(): return lax.ppermute(x, 'layer', [(i, i ^ 4) for i in range(8)])]
    pallas_call x23 -> x27, Pallas kernels: 28.6 us -> 30 us  [call(): pl.pallas_call(kernel, in_specs=places or [VMEM] * len(operands), out_spe...]
    ppermute x3 -> x4, waiting for transfers between devices: 4.18 us -> 3.06 us  [move_core(): return lax.ppermute(x, 'latent', [(i, i ^ 1) for i in range(16)])]
  transfers between devices with their start and end apart: 45 -> 46, of which waited for: 15 -> 22; matrix products, arithmetic and copies ran while one was open for 0% -> 0% of each run, Pallas kernels for 15% -> 19%
where the time goes in v5:
time: 122 us; the launch traced here: 121 us
  starting transfers between devices  62.3 us (51%)
  Pallas kernels  30 us (25%)
  waiting for transfers between devices  22.8 us (19%)
  local copies, waits for them, and re-layouts  5.17 us (4%)
    pallas_call x27, Pallas kernels, call(): pl.pallas_call(kernel, in_specs=places or [VMEM] * len(operands), out_spe...  30 us
    ppermute x20, starting transfers between devices, move_z(): return lax.ppermute(x, 'layer', [(i, i ^ r) for i in range(8)])  26.4 us
    ppermute x8, starting transfers between devices, move_y(): return lax.ppermute(x, 'layer', [(i, i ^ 4) for i in range(8)])  16.8 us
    ppermute x10, starting transfers between devices, move_x(): return lax.ppermute(x, 'latent', [(i, i ^ 2 * r) for i in range(16)])  14.3 us
    ppermute x20, waiting for transfers between devices, move_z(): return lax.ppermute(x, 'layer', [(i, i ^ r) for i in range(8)])  9.51 us
    unnamed x10, local copies, waits for them, and re-layouts  5.17 us
    ppermute x10, waiting for transfers between devices, move_x(): return lax.ppermute(x, 'latent', [(i, i ^ 2 * r) for i in range(16)])  4.38 us
    ppermute x8, waiting for transfers between devices, move_y(): return lax.ppermute(x, 'layer', [(i, i ^ 4) for i in range(8)])  4.38 us
  transfers between devices with their start and end apart: 46, of which 22 were waited for; matrix products, arithmetic and copies ran while one was open for 0% of the time, Pallas kernels for 19%

profile of v5, /device:TPU:0, one launch (start us, length us, event | category | flops | bytes accessed | tf_op | source)
XLA Modules:
  0.0 121.5 jit_solution(12738835619231947789)
XLA Ops:
  0.6 3.7 %copy-done = bf16[1,2048,2304]{2,1,0:T(8,128)(2,1)S(1)} copy-done((bf16[1,2048,2304]{2,1,0:T(8,128)(2,1)S(1)}, bf16[1,2048,2304]{2,1,0:T(8,128)(2,1)}, u32[]{:S(2)}) %copy-start) | copy-done | bytes 9437208
  4.3 1.5 %copy-done.2 = bf16[1,384,2304]{2,1,0:T(8,128)(2,1)S(1)} copy-done((bf16[1,384,2304]{2,1,0:T(8,128)(2,1)S(1)}, bf16[1,384,2304]{2,1,0:T(8,128)(2,1)}, u32[]{:S(2)}) %copy-start.2) | copy-done | bytes 1769496
  5.8 1.6 %encode_first.1 = (bf16[384,256]{1,0:T(8,128)(2,1)S(1)}, bf16[384,256]{1,0:T(8,128)(2,1)S(1)}, bf16[384,256]{1,0:T(8,128)(2,1)S(1)}, bf16[384,2304]{1,0:T(8,128)(2,1)S(1)}) custom-call(bf16[384,2304]{1,0:T(8,128)(2,1)S(1)} %bitcast.20, bf16[2048,2304]{1,0:T(8,128)(2,1)S(1)} %bitcast.6), custom_call_target="tpu_custom_call" | custom-call | flops 1358954496 | bytes 3397386 | tf_op jit(solution)/shard_map/encode_first/pallas_call | solution.py:48
  7.4 3.4 %collective-permute-start.2 = (bf16[384,256]{1,0:T(8,128)(2,1)S(1)}, bf16[384,256]{1,0:T(8,128)(2,1)S(1)}, u32[]{:S(2)}, u32[]{:S(2)}) collective-permute-start(bf16[384,256]{1,0:T(8,128)(2,1)S(1)} %get-tuple-element.51), channel_id=1, source_target_pairs={{0,64},{16,80},{32,96},{48,112},{64,0},{80,16},{96,32},{112,48},{1... | collective-permute-start | bytes 589832 | tf_op jit(solution)/shard_map/ppermute | solution.py:62
  10.7 1.9 %collective-permute-start.4 = (bf16[384,256]{1,0:T(8,128)(2,1)S(1)}, bf16[384,256]{1,0:T(8,128)(2,1)S(1)}, u32[]{:S(2)}, u32[]{:S(2)}) collective-permute-start(bf16[384,256]{1,0:T(8,128)(2,1)S(1)} %get-tuple-element.53), channel_id=1, source_target_pairs={{0,16},{16,0},{32,48},{48,32},{64,80},{80,64},{96,112},{112,96},{1... | collective-permute-start | bytes 589832 | tf_op jit(solution)/shard_map/ppermute | solution.py:66
  12.6 2.5 %collective-permute-start.5 = (bf16[384,256]{1,0:T(8,128)(2,1)S(1)}, bf16[384,256]{1,0:T(8,128)(2,1)S(1)}, u32[]{:S(2)}, u32[]{:S(2)}) collective-permute-start(bf16[384,256]{1,0:T(8,128)(2,1)S(1)} %get-tuple-element.54), channel_id=1, source_target_pairs={{0,48},{16,32},{32,16},{48,0},{64,112},{80,96},{96,80},{112,64},{1... | collective-permute-start | bytes 589832 | tf_op jit(solution)/shard_map/ppermute | solution.py:66
  18.0 1.6 %encode.2 = (bf16[384,256]{1,0:T(8,128)(2,1)S(1)}, bf16[384,256]{1,0:T(8,128)(2,1)S(1)}, bf16[384,256]{1,0:T(8,128)(2,1)S(1)}) custom-call(bf16[384,2304]{1,0:T(8,128)(2,1)S(1)} %get-tuple-element.46.a.refs_4_, bf16[2048,2304]{1,0:T(8,128)(2,1)S(1)} %bitcast.8), custom_call_target="tpu_custom_call" | custom-call | flops 1358954496 | bytes 3397386 | tf_op jit(solution)/shard_map/encode/pallas_call | solution.py:48
  19.6 2.5 %collective-permute-start.3 = (bf16[384,256]{1,0:T(8,128)(2,1)S(1)}, bf16[384,256]{1,0:T(8,128)(2,1)S(1)}, u32[]{:S(2)}, u32[]{:S(2)}) collective-permute-start(bf16[384,256]{1,0:T(8,128)(2,1)S(1)} %add_z.4), channel_id=1, source_target_pairs={{0,32},{16,48},{32,0},{48,16},{64,96},{80,112},{96,64},{112,80},{1... | collective-permute-start | bytes 589832 | tf_op jit(solution)/shard_map/ppermute | solution.py:66
  23.0 4.1 %collective-permute-done.1.refs_2_ = bf16[384,256]{1,0:T(8,128)(2,1)S(1)} collective-permute-done((bf16[384,256]{1,0:T(8,128)(2,1)S(1)}, bf16[384,256]{1,0:T(8,128)(2,1)S(1)}, u32[]{:S(2)}, u32[]{:S(2)}) %collective-permute-start.1) | collective-permute-done | bytes 196640 | tf_op jit(solution)/shard_map/ppermute | solution.py:66
  27.2 1.8 %collective-permute-done.3.refs_3_ = bf16[384,256]{1,0:T(8,128)(2,1)S(1)} collective-permute-done((bf16[384,256]{1,0:T(8,128)(2,1)S(1)}, bf16[384,256]{1,0:T(8,128)(2,1)S(1)}, u32[]{:S(2)}, u32[]{:S(2)}) %collective-permute-start.3) | collective-permute-done | bytes 196640 | tf_op jit(solution)/shard_map/ppermute | solution.py:66
  30.5 1.3 %collective-permute-start.8 = (bf16[384,256]{1,0:T(8,128)(2,1)S(1)}, bf16[384,256]{1,0:T(8,128)(2,1)S(1)}, u32[]{:S(2)}, u32[]{:S(2)}) collective-permute-start(bf16[384,256]{1,0:T(8,128)(2,1)S(1)} %activate.1.refs_0_.refs_5_), channel_id=1, source_target_pairs={{0,32},{16,48},{32,0},{48,16},{64,96},{80,112},{96,64},{112,80},{1... | collective-permute-start | bytes 589832 | tf_op jit(solution)/shard_map/ppermute | solution.py:66
  31.7 2.4 %collective-permute-start.9 = (bf16[384,256]{1,0:T(8,128)(2,1)S(1)}, bf16[384,256]{1,0:T(8,128)(2,1)S(1)}, u32[]{:S(2)}, u32[]{:S(2)}) collective-permute-start(bf16[384,256]{1,0:T(8,128)(2,1)S(1)} %activate.1.refs_0_.refs_5_), channel_id=1, source_target_pairs={{0,48},{16,32},{32,16},{48,0},{64,112},{80,96},{96,80},{112,64},{1... | collective-permute-start | bytes 589832 | tf_op jit(solution)/shard_map/ppermute | solution.py:66
  34.1 2.8 %collective-permute-done.10.refs_0_ = bf16[384,256]{1,0:T(8,128)(2,1)S(1)} collective-permute-done((bf16[384,256]{1,0:T(8,128)(2,1)S(1)}, bf16[384,256]{1,0:T(8,128)(2,1)S(1)}, u32[]{:S(2)}, u32[]{:S(2)}) %collective-permute-start.10) | collective-permute-done | bytes 196640 | tf_op jit(solution)/shard_map/ppermute | solution.py:62
  36.9 1.9 %collective-permute-start.12 = (bf16[384,256]{1,0:T(8,128)(2,1)S(1)}, bf16[384,256]{1,0:T(8,128)(2,1)S(1)}, u32[]{:S(2)}, u32[]{:S(2)}) collective-permute-start(bf16[384,256]{1,0:T(8,128)(2,1)S(1)} %collective-permute-done.10.refs_0_), channel_id=1, source_target_pairs={{0,48},{16,32},{32,16},{48,0},{64,112},{80,96},{96,80},{112,64},{1... | collective-permute-start | bytes 589832 | tf_op jit(solution)/shard_map/ppermute | solution.py:66
  38.9 3.7 %collective-permute-start.13 = (bf16[384,256]{1,0:T(8,128)(2,1)S(1)}, bf16[384,256]{1,0:T(8,128)(2,1)S(1)}, u32[]{:S(2)}, u32[]{:S(2)}) collective-permute-start(bf16[384,256]{1,0:T(8,128)(2,1)S(1)} %collective-permute-done.8.refs_2_), channel_id=1, source_target_pairs={{0,64},{16,80},{32,96},{48,112},{64,0},{80,16},{96,32},{112,48},{1... | collective-permute-start | bytes 589832 | tf_op jit(solution)/shard_map/ppermute | solution.py:62
  42.6 2.0 %decode.3 = (bf16[4,384,256]{2,1,0:T(8,128)(2,1)S(1)}, f32[384,2304]{1,0:T(8,128)S(1)}) custom-call(bf16[384,256]{1,0:T(8,128)(2,1)S(1)} %activate.1.refs_0_.refs_5_, bf16[384,256]{1,0:T(8,128)(2,1)S(1)} %collective-permute-done.7.refs_1_, bf16[384,256]{1,0:T(8,128)(2,1)S(1)} %collective-permute-done.8.refs_2_, ...), custom_call_target="tpu_custom_call" | custom-call | flops 1811939328 | bytes 4529848 | tf_op jit(solution)/shard_map/decode/pallas_call | solution.py:48
  45.2 1.6 %decode.4 = (bf16[3,384,256]{2,1,0:T(8,128)(2,1)S(1)}, f32[384,2304]{1,0:T(8,128)S(1)}) custom-call(bf16[384,256]{1,0:T(8,128)(2,1)S(1)} %collective-permute-done.10.refs_0_, bf16[384,256]{1,0:T(8,128)(2,1)S(1)} %collective-permute-done.11.refs_1_, bf16[384,256]{1,0:T(8,128)(2,1)S(1)} %collective-permute-done.12.refs_2_, bf16[2048,2304]{1,0:T(8,128)(2,1)S(1)} %bitcast.10, ...), custom_call_target="tpu_custom_call" | custom-call | flops 1358954496 | bytes 3397386 | tf_op jit(solution)/shard_map/decode/pallas_call | solution.py:48
  48.0 1.3 %collective-permute-done.17.b = bf16[96,2304]{1,0:T(8,128)(2,1)S(1)} collective-permute-done((bf16[96,2304]{1,0:T(8,128)(2,1)S(1)}, bf16[96,2304]{1,0:T(8,128)(2,1)S(1)}, u32[]{:S(2)}, u32[]{:S(2)}) %collective-permute-start.17) | collective-permute-done | bytes 442400 | tf_op jit(solution)/shard_map/ppermute | solution.py:70
  50.4 1.5 %collective-permute-start.20 = (bf16[24,2304]{1,0:T(8,128)(2,1)S(1)}, bf16[24,2304]{1,0:T(8,128)(2,1)S(1)}, u32[]{:S(2)}, u32[]{:S(2)}) collective-permute-start(bf16[24,2304]{1,0:T(8,128)(2,1)S(1)} %get-tuple-element.70), channel_id=1, source_target_pairs={{0,2},{1,3},{2,0},{3,1},{4,6},{5,7},{6,4},{7,5},{8,10},{9,11},{10,... | collective-permute-start | bytes 331784 | tf_op jit(solution)/shard_map/ppermute | solution.py:78
  51.9 2.1 %collective-permute-start.21 = (bf16[24,2304]{1,0:T(8,128)(2,1)S(1)}, bf16[24,2304]{1,0:T(8,128)(2,1)S(1)}, u32[]{:S(2)}, u32[]{:S(2)}) collective-permute-start(bf16[24,2304]{1,0:T(8,128)(2,1)S(1)} %get-tuple-element.71), channel_id=1, source_target_pairs={{0,6},{1,7},{2,4},{3,5},{4,2},{5,3},{6,0},{7,1},{8,14},{9,15},{10,... | collective-permute-start | bytes 331784 | tf_op jit(solution)/shard_map/ppermute | solution.py:78
  55.5 2.9 %collective-permute-start.19 = (bf16[24,2304]{1,0:T(8,128)(2,1)S(1)}, bf16[24,2304]{1,0:T(8,128)(2,1)S(1)}, u32[]{:S(2)}, u32[]{:S(2)}) collective-permute-start(bf16[24,2304]{1,0:T(8,128)(2,1)S(1)} %add_x.2), channel_id=1, source_target_pairs={{0,4},{1,5},{2,6},{3,7},{4,0},{5,1},{6,2},{7,3},{8,12},{9,13},{10,... | collective-permute-start | bytes 331784 | tf_op jit(solution)/shard_map/ppermute | solution.py:78
  58.5 1.3 %collective-permute-start.22 = (bf16[24,2304]{1,0:T(8,128)(2,1)S(1)}, bf16[24,2304]{1,0:T(8,128)(2,1)S(1)}, u32[]{:S(2)}, u32[]{:S(2)}) collective-permute-start(bf16[24,2304]{1,0:T(8,128)(2,1)S(1)} %add_x.3), channel_id=1, source_target_pairs={{0,8},{1,9},{2,10},{3,11},{4,12},{5,13},{6,14},{7,15},{8,0},{9,1},... | collective-permute-start | bytes 331784 | tf_op jit(solution)/shard_map/ppermute | solution.py:74
  59.8 2.5 %prepare.1 = (f32[8,8,256]{2,1,0:T(8,128)S(1)}, bf16[24,2304]{1,0:T(8,128)(2,1)S(1)}) custom-call(bf16[384,2304]{1,0:T(8,128)(2,1)S(1)} %get-tuple-element.46.a.refs_4_, bf16[2048,2304]{1,0:T(8,128)(2,1)S(1)} %bitcast.12), custom_call_target="tpu_custom_call" | custom-call | flops 1073741824 | bytes 2684354 | tf_op jit(solution)/shard_map/prepare/pallas_call | solution.py:48
  63.5 1.3 %collective-permute-start.26 = (bf16[24,2304]{1,0:T(8,128)(2,1)S(1)}, bf16[24,2304]{1,0:T(8,128)(2,1)S(1)}, u32[]{:S(2)}, u32[]{:S(2)}) collective-permute-start(bf16[24,2304]{1,0:T(8,128)(2,1)S(1)} %error.1.refs_0_), channel_id=1, source_target_pairs={{0,8},{1,9},{2,10},{3,11},{4,12},{5,13},{6,14},{7,15},{8,0},{9,1},... | collective-permute-start | bytes 331784 | tf_op jit(solution)/shard_map/ppermute | solution.py:74
  64.7 1.8 %collective-permute-start.24 = (bf16[24,2304]{1,0:T(8,128)(2,1)S(1)}, bf16[24,2304]{1,0:T(8,128)(2,1)S(1)}, u32[]{:S(2)}, u32[]{:S(2)}) collective-permute-start(bf16[24,2304]{1,0:T(8,128)(2,1)S(1)} %error.1.refs_0_), channel_id=1, source_target_pairs={{0,4},{1,5},{2,6},{3,7},{4,0},{5,1},{6,2},{7,3},{8,12},{9,13},{10,... | collective-permute-start | bytes 331784 | tf_op jit(solution)/shard_map/ppermute | solution.py:78
  66.5 1.5 %collective-permute-start.25 = (bf16[24,2304]{1,0:T(8,128)(2,1)S(1)}, bf16[24,2304]{1,0:T(8,128)(2,1)S(1)}, u32[]{:S(2)}, u32[]{:S(2)}) collective-permute-start(bf16[24,2304]{1,0:T(8,128)(2,1)S(1)} %error.1.refs_0_), channel_id=1, source_target_pairs={{0,6},{1,7},{2,4},{3,5},{4,2},{5,3},{6,0},{7,1},{8,14},{9,15},{10,... | collective-permute-start | bytes 331784 | tf_op jit(solution)/shard_map/ppermute | solution.py:78
  68.4 2.7 %collective-permute-start.29 = (bf16[24,2304]{1,0:T(8,128)(2,1)S(1)}, bf16[24,2304]{1,0:T(8,128)(2,1)S(1)}, u32[]{:S(2)}, u32[]{:S(2)}) collective-permute-start(bf16[24,2304]{1,0:T(8,128)(2,1)S(1)} %collective-permute-done.26.refs_0_), channel_id=1, source_target_pairs={{0,6},{1,7},{2,4},{3,5},{4,2},{5,3},{6,0},{7,1},{8,14},{9,15},{10,... | collective-permute-start | bytes 331784 | tf_op jit(solution)/shard_map/ppermute | solution.py:78
  73.0 1.4 %collective-permute-done.29.refs_3_ = bf16[24,2304]{1,0:T(8,128)(2,1)S(1)} collective-permute-done((bf16[24,2304]{1,0:T(8,128)(2,1)S(1)}, bf16[24,2304]{1,0:T(8,128)(2,1)S(1)}, u32[]{:S(2)}, u32[]{:S(2)}) %collective-permute-start.29) | collective-permute-done | bytes 110624 | tf_op jit(solution)/shard_map/ppermute | solution.py:78
  74.4 1.5 %collective-permute-done.27.refs_1_ = bf16[24,2304]{1,0:T(8,128)(2,1)S(1)} collective-permute-done((bf16[24,2304]{1,0:T(8,128)(2,1)S(1)}, bf16[24,2304]{1,0:T(8,128)(2,1)S(1)}, u32[]{:S(2)}, u32[]{:S(2)}) %collective-permute-start.27) | collective-permute-done | bytes 110624 | tf_op jit(solution)/shard_map/ppermute | solution.py:78
  76.9 1.8 %collective-permute-done.31.refs_3_ = bf16[96,2304]{1,0:T(8,128)(2,1)S(1)} collective-permute-done((bf16[96,2304]{1,0:T(8,128)(2,1)S(1)}, bf16[96,2304]{1,0:T(8,128)(2,1)S(1)}, u32[]{:S(2)}, u32[]{:S(2)}) %collective-permute-start.31) | collective-permute-done | bytes 442400 | tf_op jit(solution)/shard_map/ppermute | solution.py:70
  78.7 1.6 %backward_first.1 = (bf16[400,256]{1,0:T(8,128)(2,1)S(1)}, bf16[400,256]{1,0:T(8,128)(2,1)S(1)}, bf16[400,256]{1,0:T(8,128)(2,1)S(1)}, bf16[768,2304]{1,0:T(8,128)(2,1)S(1)}) custom-call(bf16[96,2304]{1,0:T(8,128)(2,1)S(1)} %join.2.refs_0_, bf16[96,2304]{1,0:T(8,128)(2,1)S(1)} %join.3.refs_1_, bf16[96,2304]{1,0:T(8,128)(2,1)S(1)} %collective-permute-done.30.refs_2_, ...), custom_call_target="tpu_custom_call" | custom-call | flops 1358954496 | bytes 3397386 | tf_op jit(solution)/shard_map/backward_first/pallas_call | solution.py:48
  80.3 2.7 %collective-permute-start.34 = (bf16[400,256]{1,0:T(8,128)(2,1)S(1)}, bf16[400,256]{1,0:T(8,128)(2,1)S(1)}, u32[]{:S(2)}, u32[]{:S(2)}) collective-permute-start(bf16[400,256]{1,0:T(8,128)(2,1)S(1)} %get-tuple-element.79), channel_id=1, source_target_pairs={{0,64},{16,80},{32,96},{48,112},{64,0},{80,16},{96,32},{112,48},{1... | collective-permute-start | bytes 614408 | tf_op jit(solution)/shard_map/ppermute | solution.py:62
  83.1 1.2 collective-permute-start.36
  84.2 1.3 %collective-permute-start.37 = (bf16[400,256]{1,0:T(8,128)(2,1)S(1)}, bf16[400,256]{1,0:T(8,128)(2,1)S(1)}, u32[]{:S(2)}, u32[]{:S(2)}) collective-permute-start(bf16[400,256]{1,0:T(8,128)(2,1)S(1)} %get-tuple-element.82), channel_id=1, source_target_pairs={{0,48},{16,32},{32,16},{48,0},{64,112},{80,96},{96,80},{112,64},{1... | collective-permute-start | bytes 614408 | tf_op jit(solution)/shard_map/ppermute | solution.py:66
  87.6 1.3 %collective-permute-start.33 = (bf16[400,256]{1,0:T(8,128)(2,1)S(1)}, bf16[400,256]{1,0:T(8,128)(2,1)S(1)}, u32[]{:S(2)}, u32[]{:S(2)}) collective-permute-start(bf16[400,256]{1,0:T(8,128)(2,1)S(1)} %get-tuple-element.77), channel_id=1, source_target_pairs={{0,48},{16,32},{32,16},{48,0},{64,112},{80,96},{96,80},{112,64},{1... | collective-permute-start | bytes 614408 | tf_op jit(solution)/shard_map/ppermute | solution.py:66
  88.9 1.6 %backward.2 = (bf16[400,256]{1,0:T(8,128)(2,1)S(1)}, bf16[400,256]{1,0:T(8,128)(2,1)S(1)}, bf16[400,256]{1,0:T(8,128)(2,1)S(1)}) custom-call(bf16[768,2304]{1,0:T(8,128)(2,1)S(1)} %get-tuple-element.74.e.refs_3_.refs_4_.refs_7_.refs_11_, f32[8,8,256]{2,1,0:T(8,128)S(1)} %get-tuple-element.73.refs_5_.n.refs_4_.refs_8_.refs_12_, bf16[2048,2304]{1,0:T(8,128)(2,1)S(1)} %bitcast.15), custom_call_target="tpu_custom_call" | custom-call | flops 1358954496 | bytes 3397386 | tf_op jit(solution)/shard_map/backward/pallas_call | solution.py:48
  90.6 2.0 %collective-permute-start.35 = (bf16[400,256]{1,0:T(8,128)(2,1)S(1)}, bf16[400,256]{1,0:T(8,128)(2,1)S(1)}, u32[]{:S(2)}, u32[]{:S(2)}) collective-permute-start(bf16[400,256]{1,0:T(8,128)(2,1)S(1)} %add_z.6), channel_id=1, source_target_pairs={{0,32},{16,48},{32,0},{48,16},{64,96},{80,112},{96,64},{112,80},{1... | collective-permute-start | bytes 614408 | tf_op jit(solution)/shard_map/ppermute | solution.py:66
  93.5 1.4 %collective-permute-start.38 = (bf16[400,256]{1,0:T(8,128)(2,1)S(1)}, bf16[400,256]{1,0:T(8,128)(2,1)S(1)}, u32[]{:S(2)}, u32[]{:S(2)}) collective-permute-start(bf16[400,256]{1,0:T(8,128)(2,1)S(1)} %add_z.7), channel_id=1, source_target_pairs={{0,64},{16,80},{32,96},{48,112},{64,0},{80,16},{96,32},{112,48},{1... | collective-permute-start | bytes 614408 | tf_op jit(solution)/shard_map/ppermute | solution.py:62
  94.9 4.7 %prepare_gradient.1.refs_6_.refs_7_.refs_10_.refs_14_ = bf16[7,256,2304]{2,1,0:T(8,128)(2,1)S(1)} custom-call(bf16[4,384,256]{2,1,0:T(8,128)(2,1)S(1)} %get-tuple-element.55.refs_0_, bf16[3,384,256]{2,1,0:T(8,128)(2,1)S(1)} %get-tuple-element.57.refs_1_, bf16[1,384,256]{2,1,0:T(8,128)(2,1)S(1)} %get-tuple-element.59.refs_2_, ...), custom_call_target="tpu_custom_call" | custom-call | flops 3170893824 | bytes 7927234 | tf_op jit(solution)/shard_map/prepare_gradient/pallas_call | solution.py:48
  99.6 1.2 collective-permute-done.33.refs_2_
  101.3 1.1 collective-permute-start.42
  102.4 1.1 collective-permute-start.40
  103.5 1.9 %collective-permute-start.41 = (bf16[400,256]{1,0:T(8,128)(2,1)S(1)}, bf16[400,256]{1,0:T(8,128)(2,1)S(1)}, u32[]{:S(2)}, u32[]{:S(2)}) collective-permute-start(bf16[400,256]{1,0:T(8,128)(2,1)S(1)} %latent_grad.1.refs_3_), channel_id=1, source_target_pairs={{0,48},{16,32},{32,16},{48,0},{64,112},{80,96},{96,80},{112,64},{1... | collective-permute-start | bytes 614408 | tf_op jit(solution)/shard_map/ppermute | solution.py:66
  105.9 2.2 %gradient.3 = (bf16[2048,2304]{1,0:T(8,128)(2,1)}, f32[1,2304]{1,0:T(1,128)}) custom-call(bf16[4,384,256]{2,1,0:T(8,128)(2,1)S(1)} %get-tuple-element.55.refs_0_, bf16[3,384,256]{2,1,0:T(8,128)(2,1)S(1)} %get-tuple-element.57.refs_1_, bf16[1,384,256]{2,1,0:T(8,128)(2,1)S(1)} %get-tuple-element.59.refs_2_, bf16[400,256]{1,0:T(8,128)(2,1)S(1)} %latent_grad.1.refs_3_, ...), custom_call_target="tpu_custom_call" | custom-call | flops 905969664 | bytes 2264924 | tf_op jit(solution)/shard_map/gradient/pallas_call | solution.py:48
  108.6 1.3 %collective-permute-start.45 = (bf16[400,256]{1,0:T(8,128)(2,1)S(1)}, bf16[400,256]{1,0:T(8,128)(2,1)S(1)}, u32[]{:S(2)}, u32[]{:S(2)}) collective-permute-start(bf16[400,256]{1,0:T(8,128)(2,1)S(1)} %collective-permute-done.42.refs_3_.refs_7_), channel_id=1, source_target_pairs={{0,48},{16,32},{32,16},{48,0},{64,112},{80,96},{96,80},{112,64},{1... | collective-permute-start | bytes 614408 | tf_op jit(solution)/shard_map/ppermute | solution.py:66
  111.0 3.0 %collective-permute-start.44 = (bf16[400,256]{1,0:T(8,128)(2,1)S(1)}, bf16[400,256]{1,0:T(8,128)(2,1)S(1)}, u32[]{:S(2)}, u32[]{:S(2)}) collective-permute-start(bf16[400,256]{1,0:T(8,128)(2,1)S(1)} %collective-permute-done.40.refs_4_.refs_5_), channel_id=1, source_target_pairs={{0,64},{16,80},{32,96},{48,112},{64,0},{80,16},{96,32},{112,48},{1... | collective-permute-start | bytes 614408 | tf_op jit(solution)/shard_map/ppermute | solution.py:62
  114.5 3.5 %gradient.4.refs_15_ = bf16[2048,2304]{1,0:T(8,128)(2,1)} custom-call(bf16[4,384,256]{2,1,0:T(8,128)(2,1)S(1)} %get-tuple-element.55.refs_0_, bf16[3,384,256]{2,1,0:T(8,128)(2,1)S(1)} %get-tuple-element.57.refs_1_, bf16[1,384,256]{2,1,0:T(8,128)(2,1)S(1)} %get-tuple-element.59.refs_2_, ...), custom_call_target="tpu_custom_call", output_to_operand_aliasing={{}: (11, {})} | custom-call | flops 3623878656 | bytes 9059696 | tf_op jit(solution)/shard_map/gradient/pallas_call | solution.py:48
  118.2 3.0 %gradient.5 = (bf16[2048,2304]{1,0:T(8,128)(2,1)}, f32[8,1,256]{2,1,0:T(1,128)}, f32[8,1,256]{2,1,0:T(1,128)}) custom-call(bf16[4,384,256]{2,1,0:T(8,128)(2,1)S(1)} %get-tuple-element.55.refs_0_, bf16[3,384,256]{2,1,0:T(8,128)(2,1)S(1)} %get-tuple-element.57.refs_1_, ...), custom_call_target="tpu_custom_call", output_to_operand_aliasing={{0}: (15, {})} | custom-call | flops 2717908992 | bytes 6794772 | tf_op jit(solution)/shard_map/gradient/pallas_call | solution.py:48
  (81 shorter events, 20.5 us)
Async XLA Ops:
  7.4 12.2 %collective-permute-start.2 = (bf16[384,256]{1,0:T(8,128)(2,1)S(1)}, bf16[384,256]{1,0:T(8,128)(2,1)S(1)}, u32[]{:S(2)}, u32[]{:S(2)}) collective-permute-start(bf16[384,256]{1,0:T(8,128)(2,1)S(1)} %get-tuple-element.51), channel_id=1, source_target_pairs={{0,64},{16,80},{32,96},{48,112},{64,0},{80,16},{96,32},{112,48},{1... | collective-permute-start | bytes 589832 | tf_op jit(solution)/shard_map/ppermute | solution.py:62
  10.7 11.5 %collective-permute-start.4 = (bf16[384,256]{1,0:T(8,128)(2,1)S(1)}, bf16[384,256]{1,0:T(8,128)(2,1)S(1)}, u32[]{:S(2)}, u32[]{:S(2)}) collective-permute-start(bf16[384,256]{1,0:T(8,128)(2,1)S(1)} %get-tuple-element.53), channel_id=1, source_target_pairs={{0,16},{16,0},{32,48},{48,32},{64,80},{80,64},{96,112},{112,96},{1... | collective-permute-start | bytes 589832 | tf_op jit(solution)/shard_map/ppermute | solution.py:66
  12.6 9.5 %collective-permute-start.5 = (bf16[384,256]{1,0:T(8,128)(2,1)S(1)}, bf16[384,256]{1,0:T(8,128)(2,1)S(1)}, u32[]{:S(2)}, u32[]{:S(2)}) collective-permute-start(bf16[384,256]{1,0:T(8,128)(2,1)S(1)} %get-tuple-element.54), channel_id=1, source_target_pairs={{0,48},{16,32},{32,16},{48,0},{64,112},{80,96},{96,80},{112,64},{1... | collective-permute-start | bytes 589832 | tf_op jit(solution)/shard_map/ppermute | solution.py:66
  16.3 13.2 %copy-start.4 = (f32[2048]{0:T(1024)S(1)}, f32[2048]{0:T(1024)}, u32[]{:S(2)}) copy-start(f32[2048]{0:T(1024)} %param.6) | copy-start | bytes 24580
  16.3 6.8 %collective-permute-start = (bf16[384,256]{1,0:T(8,128)(2,1)S(1)}, bf16[384,256]{1,0:T(8,128)(2,1)S(1)}, u32[]{:S(2)}, u32[]{:S(2)}) collective-permute-start(bf16[384,256]{1,0:T(8,128)(2,1)S(1)} %get-tuple-element.48), channel_id=1, source_target_pairs={{0,16},{16,0},{32,48},{48,32},{64,80},{80,64},{96,112},{112,96},{1... | collective-permute-start | bytes 589832 | tf_op jit(solution)/shard_map/ppermute | solution.py:66
  17.4 9.8 %collective-permute-start.1 = (bf16[384,256]{1,0:T(8,128)(2,1)S(1)}, bf16[384,256]{1,0:T(8,128)(2,1)S(1)}, u32[]{:S(2)}, u32[]{:S(2)}) collective-permute-start(bf16[384,256]{1,0:T(8,128)(2,1)S(1)} %get-tuple-element.49), channel_id=1, source_target_pairs={{0,48},{16,32},{32,16},{48,0},{64,112},{80,96},{96,80},{112,64},{1... | collective-permute-start | bytes 589832 | tf_op jit(solution)/shard_map/ppermute | solution.py:66
  19.6 9.3 %collective-permute-start.3 = (bf16[384,256]{1,0:T(8,128)(2,1)S(1)}, bf16[384,256]{1,0:T(8,128)(2,1)S(1)}, u32[]{:S(2)}, u32[]{:S(2)}) collective-permute-start(bf16[384,256]{1,0:T(8,128)(2,1)S(1)} %add_z.4), channel_id=1, source_target_pairs={{0,32},{16,48},{32,0},{48,16},{64,96},{80,112},{96,64},{112,80},{1... | collective-permute-start | bytes 589832 | tf_op jit(solution)/shard_map/ppermute | solution.py:66
  22.3 7.3 %collective-permute-start.6 = (bf16[384,256]{1,0:T(8,128)(2,1)S(1)}, bf16[384,256]{1,0:T(8,128)(2,1)S(1)}, u32[]{:S(2)}, u32[]{:S(2)}) collective-permute-start(bf16[384,256]{1,0:T(8,128)(2,1)S(1)} %add_z.5), channel_id=1, source_target_pairs={{0,64},{16,80},{32,96},{48,112},{64,0},{80,16},{96,32},{112,48},{1... | collective-permute-start | bytes 589832 | tf_op jit(solution)/shard_map/ppermute | solution.py:62
  29.7 7.3 %collective-permute-start.10 = (bf16[384,256]{1,0:T(8,128)(2,1)S(1)}, bf16[384,256]{1,0:T(8,128)(2,1)S(1)}, u32[]{:S(2)}, u32[]{:S(2)}) collective-permute-start(bf16[384,256]{1,0:T(8,128)(2,1)S(1)} %activate.1.refs_0_.refs_5_), channel_id=1, source_target_pairs={{0,64},{16,80},{32,96},{48,112},{64,0},{80,16},{96,32},{112,48},{1... | collective-permute-start | bytes 589832 | tf_op jit(solution)/shard_map/ppermute | solution.py:62
  30.5 8.5 %collective-permute-start.8 = (bf16[384,256]{1,0:T(8,128)(2,1)S(1)}, bf16[384,256]{1,0:T(8,128)(2,1)S(1)}, u32[]{:S(2)}, u32[]{:S(2)}) collective-permute-start(bf16[384,256]{1,0:T(8,128)(2,1)S(1)} %activate.1.refs_0_.refs_5_), channel_id=1, source_target_pairs={{0,32},{16,48},{32,0},{48,16},{64,96},{80,112},{96,64},{112,80},{1... | collective-permute-start | bytes 589832 | tf_op jit(solution)/shard_map/ppermute | solution.py:66
  31.7 10.9 %collective-permute-start.9 = (bf16[384,256]{1,0:T(8,128)(2,1)S(1)}, bf16[384,256]{1,0:T(8,128)(2,1)S(1)}, u32[]{:S(2)}, u32[]{:S(2)}) collective-permute-start(bf16[384,256]{1,0:T(8,128)(2,1)S(1)} %activate.1.refs_0_.refs_5_), channel_id=1, source_target_pairs={{0,48},{16,32},{32,16},{48,0},{64,112},{80,96},{96,80},{112,64},{1... | collective-permute-start | bytes 589832 | tf_op jit(solution)/shard_map/ppermute | solution.py:66
  34.1 8.5 %collective-permute-start.7 = (bf16[384,256]{1,0:T(8,128)(2,1)S(1)}, bf16[384,256]{1,0:T(8,128)(2,1)S(1)}, u32[]{:S(2)}, u32[]{:S(2)}) collective-permute-start(bf16[384,256]{1,0:T(8,128)(2,1)S(1)} %activate.1.refs_0_.refs_5_), channel_id=1, source_target_pairs={{0,16},{16,0},{32,48},{48,32},{64,80},{80,64},{96,112},{112,96},{1... | collective-permute-start | bytes 589832 | tf_op jit(solution)/shard_map/ppermute | solution.py:66
  36.9 8.2 %collective-permute-start.12 = (bf16[384,256]{1,0:T(8,128)(2,1)S(1)}, bf16[384,256]{1,0:T(8,128)(2,1)S(1)}, u32[]{:S(2)}, u32[]{:S(2)}) collective-permute-start(bf16[384,256]{1,0:T(8,128)(2,1)S(1)} %collective-permute-done.10.refs_0_), channel_id=1, source_target_pairs={{0,48},{16,32},{32,16},{48,0},{64,112},{80,96},{96,80},{112,64},{1... | collective-permute-start | bytes 589832 | tf_op jit(solution)/shard_map/ppermute | solution.py:66
  38.9 6.3 %collective-permute-start.11 = (bf16[384,256]{1,0:T(8,128)(2,1)S(1)}, bf16[384,256]{1,0:T(8,128)(2,1)S(1)}, u32[]{:S(2)}, u32[]{:S(2)}) collective-permute-start(bf16[384,256]{1,0:T(8,128)(2,1)S(1)} %collective-permute-done.10.refs_0_), channel_id=1, source_target_pairs={{0,16},{16,0},{32,48},{48,32},{64,80},{80,64},{96,112},{112,96},{1... | collective-permute-start | bytes 589832 | tf_op jit(solution)/shard_map/ppermute | solution.py:66
  38.9 7.8 %collective-permute-start.13 = (bf16[384,256]{1,0:T(8,128)(2,1)S(1)}, bf16[384,256]{1,0:T(8,128)(2,1)S(1)}, u32[]{:S(2)}, u32[]{:S(2)}) collective-permute-start(bf16[384,256]{1,0:T(8,128)(2,1)S(1)} %collective-permute-done.8.refs_2_), channel_id=1, source_target_pairs={{0,64},{16,80},{32,96},{48,112},{64,0},{80,16},{96,32},{112,48},{1... | collective-permute-start | bytes 589832 | tf_op jit(solution)/shard_map/ppermute | solution.py:62
  47.4 16.0 %copy-start.3 = (f32[1,2304]{1,0:T(1,128)S(1)}, f32[1,2304]{1,0:T(1,128)}, u32[]{:S(2)}) copy-start(f32[1,2304]{1,0:T(1,128)} %refs_5_.1) | copy-start | bytes 27652
  47.4 1.9 %collective-permute-start.17 = (bf16[96,2304]{1,0:T(8,128)(2,1)S(1)}, bf16[96,2304]{1,0:T(8,128)(2,1)S(1)}, u32[]{:S(2)}, u32[]{:S(2)}) collective-permute-start(bf16[96,2304]{1,0:T(8,128)(2,1)S(1)} %get-tuple-element.67), channel_id=1, source_target_pairs={{0,1},{1,0},{2,3},{3,2},{4,5},{5,4},{6,7},{7,6},{8,9},{9,8},{10,11... | collective-permute-start | bytes 1327112 | tf_op jit(solution)/shard_map/ppermute | solution.py:70
  47.5 6.5 %collective-permute-start.14 = (bf16[96,2304]{1,0:T(8,128)(2,1)S(1)}, bf16[96,2304]{1,0:T(8,128)(2,1)S(1)}, u32[]{:S(2)}, u32[]{:S(2)}) collective-permute-start(bf16[96,2304]{1,0:T(8,128)(2,1)S(1)} %get-tuple-element.61), channel_id=1, source_target_pairs={{0,1},{1,0},{2,3},{3,2},{4,5},{5,4},{6,7},{7,6},{8,9},{9,8},{10,11... | collective-permute-start | bytes 1327112 | tf_op jit(solution)/shard_map/ppermute | solution.py:70
  49.5 6.0 %collective-permute-start.18 = (bf16[24,2304]{1,0:T(8,128)(2,1)S(1)}, bf16[24,2304]{1,0:T(8,128)(2,1)S(1)}, u32[]{:S(2)}, u32[]{:S(2)}) collective-permute-start(bf16[24,2304]{1,0:T(8,128)(2,1)S(1)} %get-tuple-element.68), channel_id=1, source_target_pairs={{0,8},{1,9},{2,10},{3,11},{4,12},{5,13},{6,14},{7,15},{8,0},{9,1},... | collective-permute-start | bytes 331784 | tf_op jit(solution)/shard_map/ppermute | solution.py:74
  50.4 8.1 %collective-permute-start.20 = (bf16[24,2304]{1,0:T(8,128)(2,1)S(1)}, bf16[24,2304]{1,0:T(8,128)(2,1)S(1)}, u32[]{:S(2)}, u32[]{:S(2)}) collective-permute-start(bf16[24,2304]{1,0:T(8,128)(2,1)S(1)} %get-tuple-element.70), channel_id=1, source_target_pairs={{0,2},{1,3},{2,0},{3,1},{4,6},{5,7},{6,4},{7,5},{8,10},{9,11},{10,... | collective-permute-start | bytes 331784 | tf_op jit(solution)/shard_map/ppermute | solution.py:78
  51.9 6.6 %collective-permute-start.21 = (bf16[24,2304]{1,0:T(8,128)(2,1)S(1)}, bf16[24,2304]{1,0:T(8,128)(2,1)S(1)}, u32[]{:S(2)}, u32[]{:S(2)}) collective-permute-start(bf16[24,2304]{1,0:T(8,128)(2,1)S(1)} %get-tuple-element.71), channel_id=1, source_target_pairs={{0,6},{1,7},{2,4},{3,5},{4,2},{5,3},{6,0},{7,1},{8,14},{9,15},{10,... | collective-permute-start | bytes 331784 | tf_op jit(solution)/shard_map/ppermute | solution.py:78
  54.2 8.1 %collective-permute-start.15 = (bf16[24,2304]{1,0:T(8,128)(2,1)S(1)}, bf16[24,2304]{1,0:T(8,128)(2,1)S(1)}, u32[]{:S(2)}, u32[]{:S(2)}) collective-permute-start(bf16[24,2304]{1,0:T(8,128)(2,1)S(1)} %get-tuple-element.63), channel_id=1, source_target_pairs={{0,2},{1,3},{2,0},{3,1},{4,6},{5,7},{6,4},{7,5},{8,10},{9,11},{10,... | collective-permute-start | bytes 331784 | tf_op jit(solution)/shard_map/ppermute | solution.py:78
  54.8 7.9 %collective-permute-start.16 = (bf16[24,2304]{1,0:T(8,128)(2,1)S(1)}, bf16[24,2304]{1,0:T(8,128)(2,1)S(1)}, u32[]{:S(2)}, u32[]{:S(2)}) collective-permute-start(bf16[24,2304]{1,0:T(8,128)(2,1)S(1)} %get-tuple-element.64), channel_id=1, source_target_pairs={{0,6},{1,7},{2,4},{3,5},{4,2},{5,3},{6,0},{7,1},{8,14},{9,15},{10,... | collective-permute-start | bytes 331784 | tf_op jit(solution)/shard_map/ppermute | solution.py:78
  55.5 7.2 %collective-permute-start.19 = (bf16[24,2304]{1,0:T(8,128)(2,1)S(1)}, bf16[24,2304]{1,0:T(8,128)(2,1)S(1)}, u32[]{:S(2)}, u32[]{:S(2)}) collective-permute-start(bf16[24,2304]{1,0:T(8,128)(2,1)S(1)} %add_x.2), channel_id=1, source_target_pairs={{0,4},{1,5},{2,6},{3,7},{4,0},{5,1},{6,2},{7,3},{8,12},{9,13},{10,... | collective-permute-start | bytes 331784 | tf_op jit(solution)/shard_map/ppermute | solution.py:78
  58.5 4.8 %collective-permute-start.22 = (bf16[24,2304]{1,0:T(8,128)(2,1)S(1)}, bf16[24,2304]{1,0:T(8,128)(2,1)S(1)}, u32[]{:S(2)}, u32[]{:S(2)}) collective-permute-start(bf16[24,2304]{1,0:T(8,128)(2,1)S(1)} %add_x.3), channel_id=1, source_target_pairs={{0,8},{1,9},{2,10},{3,11},{4,12},{5,13},{6,14},{7,15},{8,0},{9,1},... | collective-permute-start | bytes 331784 | tf_op jit(solution)/shard_map/ppermute | solution.py:74
  63.5 5.0 %collective-permute-start.26 = (bf16[24,2304]{1,0:T(8,128)(2,1)S(1)}, bf16[24,2304]{1,0:T(8,128)(2,1)S(1)}, u32[]{:S(2)}, u32[]{:S(2)}) collective-permute-start(bf16[24,2304]{1,0:T(8,128)(2,1)S(1)} %error.1.refs_0_), channel_id=1, source_target_pairs={{0,8},{1,9},{2,10},{3,11},{4,12},{5,13},{6,14},{7,15},{8,0},{9,1},... | collective-permute-start | bytes 331784 | tf_op jit(solution)/shard_map/ppermute | solution.py:74
  64.7 7.2 %collective-permute-start.24 = (bf16[24,2304]{1,0:T(8,128)(2,1)S(1)}, bf16[24,2304]{1,0:T(8,128)(2,1)S(1)}, u32[]{:S(2)}, u32[]{:S(2)}) collective-permute-start(bf16[24,2304]{1,0:T(8,128)(2,1)S(1)} %error.1.refs_0_), channel_id=1, source_target_pairs={{0,4},{1,5},{2,6},{3,7},{4,0},{5,1},{6,2},{7,3},{8,12},{9,13},{10,... | collective-permute-start | bytes 331784 | tf_op jit(solution)/shard_map/ppermute | solution.py:78
  66.5 6.3 %collective-permute-start.25 = (bf16[24,2304]{1,0:T(8,128)(2,1)S(1)}, bf16[24,2304]{1,0:T(8,128)(2,1)S(1)}, u32[]{:S(2)}, u32[]{:S(2)}) collective-permute-start(bf16[24,2304]{1,0:T(8,128)(2,1)S(1)} %error.1.refs_0_), channel_id=1, source_target_pairs={{0,6},{1,7},{2,4},{3,5},{4,2},{5,3},{6,0},{7,1},{8,14},{9,15},{10,... | collective-permute-start | bytes 331784 | tf_op jit(solution)/shard_map/ppermute | solution.py:78
  68.0 4.8 %collective-permute-start.23 = (bf16[24,2304]{1,0:T(8,128)(2,1)S(1)}, bf16[24,2304]{1,0:T(8,128)(2,1)S(1)}, u32[]{:S(2)}, u32[]{:S(2)}) collective-permute-start(bf16[24,2304]{1,0:T(8,128)(2,1)S(1)} %error.1.refs_0_), channel_id=1, source_target_pairs={{0,2},{1,3},{2,0},{3,1},{4,6},{5,7},{6,4},{7,5},{8,10},{9,11},{10,... | collective-permute-start | bytes 331784 | tf_op jit(solution)/shard_map/ppermute | solution.py:78
  68.4 6.0 %collective-permute-start.29 = (bf16[24,2304]{1,0:T(8,128)(2,1)S(1)}, bf16[24,2304]{1,0:T(8,128)(2,1)S(1)}, u32[]{:S(2)}, u32[]{:S(2)}) collective-permute-start(bf16[24,2304]{1,0:T(8,128)(2,1)S(1)} %collective-permute-done.26.refs_0_), channel_id=1, source_target_pairs={{0,6},{1,7},{2,4},{3,5},{4,2},{5,3},{6,0},{7,1},{8,14},{9,15},{10,... | collective-permute-start | bytes 331784 | tf_op jit(solution)/shard_map/ppermute | solution.py:78
  71.1 4.7 %collective-permute-start.27 = (bf16[24,2304]{1,0:T(8,128)(2,1)S(1)}, bf16[24,2304]{1,0:T(8,128)(2,1)S(1)}, u32[]{:S(2)}, u32[]{:S(2)}) collective-permute-start(bf16[24,2304]{1,0:T(8,128)(2,1)S(1)} %collective-permute-done.26.refs_0_), channel_id=1, source_target_pairs={{0,2},{1,3},{2,0},{3,1},{4,6},{5,7},{6,4},{7,5},{8,10},{9,11},{10,... | collective-permute-start | bytes 331784 | tf_op jit(solution)/shard_map/ppermute | solution.py:78
  72.0 4.7 %collective-permute-start.28 = (bf16[24,2304]{1,0:T(8,128)(2,1)S(1)}, bf16[24,2304]{1,0:T(8,128)(2,1)S(1)}, u32[]{:S(2)}, u32[]{:S(2)}) collective-permute-start(bf16[24,2304]{1,0:T(8,128)(2,1)S(1)} %collective-permute-done.24.refs_2_), channel_id=1, source_target_pairs={{0,8},{1,9},{2,10},{3,11},{4,12},{5,13},{6,14},{7,15},{8,0},{9,1},... | collective-permute-start | bytes 331784 | tf_op jit(solution)/shard_map/ppermute | solution.py:74
  72.9 4.0 %collective-permute-start.30 = (bf16[96,2304]{1,0:T(8,128)(2,1)S(1)}, bf16[96,2304]{1,0:T(8,128)(2,1)S(1)}, u32[]{:S(2)}, u32[]{:S(2)}) collective-permute-start(bf16[96,2304]{1,0:T(8,128)(2,1)S(1)} %join.2.refs_0_), channel_id=1, source_target_pairs={{0,1},{1,0},{2,3},{3,2},{4,5},{5,4},{6,7},{7,6},{8,9},{9,8},{10,11... | collective-permute-start | bytes 1327112 | tf_op jit(solution)/shard_map/ppermute | solution.py:70
  76.8 1.9 %collective-permute-start.31 = (bf16[96,2304]{1,0:T(8,128)(2,1)S(1)}, bf16[96,2304]{1,0:T(8,128)(2,1)S(1)}, u32[]{:S(2)}, u32[]{:S(2)}) collective-permute-start(bf16[96,2304]{1,0:T(8,128)(2,1)S(1)} %join.3.refs_1_), channel_id=1, source_target_pairs={{0,1},{1,0},{2,3},{3,2},{4,5},{5,4},{6,7},{7,6},{8,9},{9,8},{10,11... | collective-permute-start | bytes 1327112 | tf_op jit(solution)/shard_map/ppermute | solution.py:70
  80.3 10.2 %collective-permute-start.34 = (bf16[400,256]{1,0:T(8,128)(2,1)S(1)}, bf16[400,256]{1,0:T(8,128)(2,1)S(1)}, u32[]{:S(2)}, u32[]{:S(2)}) collective-permute-start(bf16[400,256]{1,0:T(8,128)(2,1)S(1)} %get-tuple-element.79), channel_id=1, source_target_pairs={{0,64},{16,80},{32,96},{48,112},{64,0},{80,16},{96,32},{112,48},{1... | collective-permute-start | bytes 614408 | tf_op jit(solution)/shard_map/ppermute | solution.py:62
  83.1 9.5 %collective-permute-start.36 = (bf16[400,256]{1,0:T(8,128)(2,1)S(1)}, bf16[400,256]{1,0:T(8,128)(2,1)S(1)}, u32[]{:S(2)}, u32[]{:S(2)}) collective-permute-start(bf16[400,256]{1,0:T(8,128)(2,1)S(1)} %get-tuple-element.81), channel_id=1, source_target_pairs={{0,16},{16,0},{32,48},{48,32},{64,80},{80,64},{96,112},{112,96},{1... | collective-permute-start | bytes 614408 | tf_op jit(solution)/shard_map/ppermute | solution.py:66
  84.2 9.2 %collective-permute-start.37 = (bf16[400,256]{1,0:T(8,128)(2,1)S(1)}, bf16[400,256]{1,0:T(8,128)(2,1)S(1)}, u32[]{:S(2)}, u32[]{:S(2)}) collective-permute-start(bf16[400,256]{1,0:T(8,128)(2,1)S(1)} %get-tuple-element.82), channel_id=1, source_target_pairs={{0,48},{16,32},{32,16},{48,0},{64,112},{80,96},{96,80},{112,64},{1... | collective-permute-start | bytes 614408 | tf_op jit(solution)/shard_map/ppermute | solution.py:66
  86.7 12.9 %collective-permute-start.32 = (bf16[400,256]{1,0:T(8,128)(2,1)S(1)}, bf16[400,256]{1,0:T(8,128)(2,1)S(1)}, u32[]{:S(2)}, u32[]{:S(2)}) collective-permute-start(bf16[400,256]{1,0:T(8,128)(2,1)S(1)} %get-tuple-element.76), channel_id=1, source_target_pairs={{0,16},{16,0},{32,48},{48,32},{64,80},{80,64},{96,112},{112,96},{1... | collective-permute-start | bytes 614408 | tf_op jit(solution)/shard_map/ppermute | solution.py:66
  87.6 13.2 %collective-permute-start.33 = (bf16[400,256]{1,0:T(8,128)(2,1)S(1)}, bf16[400,256]{1,0:T(8,128)(2,1)S(1)}, u32[]{:S(2)}, u32[]{:S(2)}) collective-permute-start(bf16[400,256]{1,0:T(8,128)(2,1)S(1)} %get-tuple-element.77), channel_id=1, source_target_pairs={{0,48},{16,32},{32,16},{48,0},{64,112},{80,96},{96,80},{112,64},{1... | collective-permute-start | bytes 614408 | tf_op jit(solution)/shard_map/ppermute | solution.py:66
  90.6 10.2 %collective-permute-start.35 = (bf16[400,256]{1,0:T(8,128)(2,1)S(1)}, bf16[400,256]{1,0:T(8,128)(2,1)S(1)}, u32[]{:S(2)}, u32[]{:S(2)}) collective-permute-start(bf16[400,256]{1,0:T(8,128)(2,1)S(1)} %add_z.6), channel_id=1, source_target_pairs={{0,32},{16,48},{32,0},{48,16},{64,96},{80,112},{96,64},{112,80},{1... | collective-permute-start | bytes 614408 | tf_op jit(solution)/shard_map/ppermute | solution.py:66
  93.5 7.6 %collective-permute-start.38 = (bf16[400,256]{1,0:T(8,128)(2,1)S(1)}, bf16[400,256]{1,0:T(8,128)(2,1)S(1)}, u32[]{:S(2)}, u32[]{:S(2)}) collective-permute-start(bf16[400,256]{1,0:T(8,128)(2,1)S(1)} %add_z.7), channel_id=1, source_target_pairs={{0,64},{16,80},{32,96},{48,112},{64,0},{80,16},{96,32},{112,48},{1... | collective-permute-start | bytes 614408 | tf_op jit(solution)/shard_map/ppermute | solution.py:62
  101.3 7.3 %collective-permute-start.42 = (bf16[400,256]{1,0:T(8,128)(2,1)S(1)}, bf16[400,256]{1,0:T(8,128)(2,1)S(1)}, u32[]{:S(2)}, u32[]{:S(2)}) collective-permute-start(bf16[400,256]{1,0:T(8,128)(2,1)S(1)} %latent_grad.1.refs_3_), channel_id=1, source_target_pairs={{0,64},{16,80},{32,96},{48,112},{64,0},{80,16},{96,32},{112,48},{1... | collective-permute-start | bytes 614408 | tf_op jit(solution)/shard_map/ppermute | solution.py:62
  102.4 8.5 %collective-permute-start.40 = (bf16[400,256]{1,0:T(8,128)(2,1)S(1)}, bf16[400,256]{1,0:T(8,128)(2,1)S(1)}, u32[]{:S(2)}, u32[]{:S(2)}) collective-permute-start(bf16[400,256]{1,0:T(8,128)(2,1)S(1)} %latent_grad.1.refs_3_), channel_id=1, source_target_pairs={{0,32},{16,48},{32,0},{48,16},{64,96},{80,112},{96,64},{112,80},{1... | collective-permute-start | bytes 614408 | tf_op jit(solution)/shard_map/ppermute | solution.py:66
  103.5 10.9 %collective-permute-start.41 = (bf16[400,256]{1,0:T(8,128)(2,1)S(1)}, bf16[400,256]{1,0:T(8,128)(2,1)S(1)}, u32[]{:S(2)}, u32[]{:S(2)}) collective-permute-start(bf16[400,256]{1,0:T(8,128)(2,1)S(1)} %latent_grad.1.refs_3_), channel_id=1, source_target_pairs={{0,48},{16,32},{32,16},{48,0},{64,112},{80,96},{96,80},{112,64},{1... | collective-permute-start | bytes 614408 | tf_op jit(solution)/shard_map/ppermute | solution.py:66
  105.5 9.0 %collective-permute-start.39 = (bf16[400,256]{1,0:T(8,128)(2,1)S(1)}, bf16[400,256]{1,0:T(8,128)(2,1)S(1)}, u32[]{:S(2)}, u32[]{:S(2)}) collective-permute-start(bf16[400,256]{1,0:T(8,128)(2,1)S(1)} %latent_grad.1.refs_3_), channel_id=1, source_target_pairs={{0,16},{16,0},{32,48},{48,32},{64,80},{80,64},{96,112},{112,96},{1... | collective-permute-start | bytes 614408 | tf_op jit(solution)/shard_map/ppermute | solution.py:66
  108.6 9.4 %collective-permute-start.45 = (bf16[400,256]{1,0:T(8,128)(2,1)S(1)}, bf16[400,256]{1,0:T(8,128)(2,1)S(1)}, u32[]{:S(2)}, u32[]{:S(2)}) collective-permute-start(bf16[400,256]{1,0:T(8,128)(2,1)S(1)} %collective-permute-done.42.refs_3_.refs_7_), channel_id=1, source_target_pairs={{0,48},{16,32},{32,16},{48,0},{64,112},{80,96},{96,80},{112,64},{1... | collective-permute-start | bytes 614408 | tf_op jit(solution)/shard_map/ppermute | solution.py:66
  110.0 8.0 %collective-permute-start.43 = (bf16[400,256]{1,0:T(8,128)(2,1)S(1)}, bf16[400,256]{1,0:T(8,128)(2,1)S(1)}, u32[]{:S(2)}, u32[]{:S(2)}) collective-permute-start(bf16[400,256]{1,0:T(8,128)(2,1)S(1)} %collective-permute-done.42.refs_3_.refs_7_), channel_id=1, source_target_pairs={{0,16},{16,0},{32,48},{48,32},{64,80},{80,64},{96,112},{112,96},{1... | collective-permute-start | bytes 614408 | tf_op jit(solution)/shard_map/ppermute | solution.py:66
  111.0 7.3 %collective-permute-start.44 = (bf16[400,256]{1,0:T(8,128)(2,1)S(1)}, bf16[400,256]{1,0:T(8,128)(2,1)S(1)}, u32[]{:S(2)}, u32[]{:S(2)}) collective-permute-start(bf16[400,256]{1,0:T(8,128)(2,1)S(1)} %collective-permute-done.40.refs_4_.refs_5_), channel_id=1, source_target_pairs={{0,64},{16,80},{32,96},{48,112},{64,0},{80,16},{96,32},{112,48},{1... | collective-permute-start | bytes 614408 | tf_op jit(solution)/shard_map/ppermute | solution.py:62
  (3 other events, 14.5 us)
